TPU v7x, 256 devices: a whole 4x4x8 slice. The times are simulated.
256 devices in a mesh: rep: 8 (over x, core), dom: 32 (over y, z).
Axes of the slice: x: 4, y: 4, z: 8, core: 2. Of those that a mesh axis runs over, the one named last changes fastest.
Arguments:
- coords: float32 [8, 3, 131072], P('rep', None, 'dom'), may hold values from -6 to 6
- atom_var: float32 [131072], P('dom'), may hold values from 0.2 to 1
- atom_weight: float32 [131072], P('dom'), may hold values from 0.5 to 2
- atoms_live: int32 [1024], P('dom'), may hold values from 1 to 128, 98304 in all
- block_list: int32 [1024, 16], P('dom'), may hold values from 0 to 2047, as said below
- owner_map: int32 [2048], replicated, may hold values from 0 to 2047, as said below
- comp_means: float32 [3, 262144], replicated, may hold values from -6 to 6
- comp_var: float32 [262144], replicated, may hold values from 0.3 to 1.5
- comp_weight: float32 [262144], replicated, may hold values from 0.1 to 1
- target: float32 [262144], P('dom'), may hold values from 0 to 2
- noise_sigma: float32 [262144], P('dom'), may hold values from 0.05 to 0.5
Outputs:
- intersection_avg: float32 [262144], P('dom')
- forces: float32 [8, 3, 131072], P('rep', None, 'dom')
Inputs may be any that keep to these rules, and one draw needn't show every extreme that they name: `atoms_live`: entry a is the number of live atoms of atom block a, held in the first slots of the block. `owner_map`: A permutation of the component blocks. Storage position p lies on dom index p // 64. `block_list`: of the 32 x 16 entries of one dom index's atom blocks, at most 64 name blocks whose storage position lies on any one dom index, and in every draw some dom index receives exactly 64 entries from every dom index. An atom block may list a component block more than once; each entry counts.
All inputs are finite; a program needn't handle non-finite values.
Results may differ from a plain program's by a relative error of at most 0.0003.
Values sent between devices are 32-bit elements; how exact they have to be, the bound alone decides.
No kernel may reach another device: no remote copies, remote signals or barrier semaphores. Data moves between devices by JAX's collectives and lax.ppermute only.
A program may use at most 128 MiB of HBM per device.

v0:
```python
import math

import jax
import jax.numpy as jnp
from jax import lax
from jax.sharding import PartitionSpec as P

ATOM_BLK = 128
COMP_BLK = 128
LISTED = 16
BLK_DEV = 32
COMP_BLOCKS = 2048
CAPACITY = 64


full_turn = 2.0 * math.pi
energy_unit = 2.494


def intersection_tile(positions, variances, weights, listed_tile):
    centers = listed_tile[:, 0:3].transpose(1, 0, 2)
    center_var = listed_tile[:, 3]
    center_weight = listed_tile[:, 4]
    offsets = positions[:, None, :, None] - centers[:, :, None, :]
    squared = jnp.sum(offsets * offsets, axis=0)
    widths = variances[None, :, None] + center_var[:, None, :]
    prefactor = weights[None, :, None] * center_weight[:, None, :]
    intersection = prefactor * (full_turn * widths) ** (-1.5) * jnp.exp(-0.5 * squared / widths)
    return (offsets, widths, intersection)


def accumulate(rows, slots, owned):
    picks = (jnp.arange(owned, dtype=jnp.int32)[:, None] == slots.reshape(-1)[None, :]).astype(
        jnp.float32
    )
    return jnp.dot(picks, rows.reshape(-1, COMP_BLK), precision=lax.Precision.HIGHEST)


def shards(
    coords,
    atom_var,
    atom_weight,
    atoms_live,
    block_list,
    owner_map,
    comp_means,
    comp_var,
    comp_weight,
    target,
    noise_sigma,
):
    replicas = lax.axis_size("rep")
    domains = lax.axis_size("dom")
    owned = target.shape[0] // COMP_BLK
    slot_index = jnp.arange(ATOM_BLK, dtype=jnp.int32)
    live_mask = (slot_index[None, :] < atoms_live[:, None]).astype(atom_weight.dtype)
    positions = coords[0].reshape(3, BLK_DEV, ATOM_BLK).transpose(1, 0, 2)
    variances = atom_var.reshape(BLK_DEV, ATOM_BLK)
    weights = atom_weight.reshape(BLK_DEV, ATOM_BLK) * live_mask
    stacked = jnp.concatenate(
        [
            comp_means.reshape(3, COMP_BLOCKS, COMP_BLK).transpose(1, 0, 2),
            comp_var.reshape(COMP_BLOCKS, 1, COMP_BLK),
            comp_weight.reshape(COMP_BLOCKS, 1, COMP_BLK),
        ],
        axis=1,
    )
    listed = stacked[block_list]
    tile_inputs = (positions, variances, weights, listed)

    def tile_of(inputs):
        coord_tile, var_tile, weight_tile, listed_tile = inputs
        return intersection_tile(coord_tile, var_tile, weight_tile, listed_tile)

    def partial_kept(inputs):
        offsets, widths, intersection = tile_of(inputs)
        return (jnp.sum(intersection, axis=1), intersection / widths)

    partials, ratios = lax.map(partial_kept, tile_inputs)
    entries = BLK_DEV * LISTED
    places = owner_map[block_list].reshape(-1)
    target_dev = places // owned
    target_slot = places % owned
    hits = (target_dev[:, None] == jnp.arange(domains, dtype=jnp.int32)[None, :]).astype(
        jnp.float32
    )
    entry_index = jnp.arange(entries, dtype=jnp.int32)
    lower = (entry_index[:, None] > entry_index[None, :]).astype(jnp.float32)
    before = jnp.dot(lower, hits, precision=lax.Precision.HIGHEST)
    ranks = jnp.sum(before * hits, axis=1).astype(jnp.int32)
    destination = target_dev * CAPACITY + ranks
    placing = (
        jnp.arange(domains * CAPACITY, dtype=jnp.int32)[:, None] == destination[None, :]
    ).astype(jnp.float32)
    send_rows = jnp.dot(
        placing, partials.reshape(entries, COMP_BLK), precision=lax.Precision.HIGHEST
    ).reshape(domains, CAPACITY, COMP_BLK)
    shifted = (target_slot - owned).astype(jnp.float32)[:, None]
    slot_values = jnp.dot(placing, shifted, precision=lax.Precision.HIGHEST)[:, 0] + owned
    send_slots = slot_values.astype(jnp.int32).reshape(domains, CAPACITY)
    got_rows, got_slots = (
        lax.all_to_all(send_rows, "dom", split_axis=0, concat_axis=0, tiled=True),
        lax.all_to_all(send_slots, "dom", split_axis=0, concat_axis=0, tiled=True),
    )
    local_sum = accumulate(got_rows, got_slots, owned)
    summed = lax.psum(local_sum, "rep")
    mean_rows = summed / replicas
    wanted = target.reshape(owned, COMP_BLK)
    sigmas = noise_sigma.reshape(owned, COMP_BLK)
    misfit = mean_rows - wanted
    adjoint = misfit / (sigmas * sigmas + 0.5 * misfit * misfit) / replicas
    padded = jnp.concatenate([adjoint, jnp.zeros((1, COMP_BLK), jnp.float32)], axis=0)
    slot_picks = (
        got_slots.reshape(-1)[:, None] == jnp.arange(owned + 1, dtype=jnp.int32)[None, :]
    ).astype(jnp.float32)
    back_rows = jnp.dot(slot_picks, padded, precision=lax.Precision.HIGHEST).reshape(
        got_slots.shape[0], got_slots.shape[1], COMP_BLK
    )
    returned = lax.all_to_all(back_rows, "dom", split_axis=0, concat_axis=0, tiled=True)
    flat_returned = returned.reshape(domains * CAPACITY, COMP_BLK)
    entry_adjoint = lax.dot_general(
        placing, flat_returned, (((0,), (0,)), ((), ())), precision=lax.Precision.HIGHEST
    ).reshape(BLK_DEV, LISTED, COMP_BLK)

    def force_kept(inputs):
        coord_tile, listed_tile, ratio_tile, adjoint_tile = inputs
        centers = listed_tile[:, 0:3].transpose(1, 0, 2)
        offsets = coord_tile[:, None, :, None] - centers[:, :, None, :]
        weight = adjoint_tile[:, None, :] * ratio_tile
        return energy_unit * jnp.sum(weight[None] * offsets, axis=(1, 3))

    forces = lax.map(force_kept, (positions, listed, ratios, entry_adjoint))
    forces = forces.transpose(1, 0, 2).reshape(3, BLK_DEV * ATOM_BLK)[None]
    return (mean_rows.reshape(-1), forces)


def solution(mesh):
    return jax.shard_map(
        shards,
        mesh=mesh,
        in_specs=(
            P("rep", None, "dom"),
            P("dom"),
            P("dom"),
            P("dom"),
            P("dom", None),
            P(),
            P(),
            P(),
            P(),
            P("dom"),
            P("dom"),
        ),
        out_specs=(P("dom"), P("rep", None, "dom")),
        check_vma=False,
    )
```

profile of v0, /device:TPU:32, one launch (start us, length us, event | category | flops | bytes accessed | tf_op | source)
XLA Modules:
  0.0 355.6 jit_solution(11357589740480110078)
XLA Ops:
  1.6 3.1 gather_fusion
  5.0 2.6 fusion.14
  8.3 11.4 %all-to-all-start = ((s32[32,1,64]{2,1,0:T(1,128)}), s32[32,1,64]{2,1,0:T(1,128)S(1)}, u32[]{:S(2)}, u32[]{:S(2)}) async-start(s32[32,1,64]{2,1,0:T(1,128)} %bitcast.18), calls=%async_computation | async-start | bytes 32768 | tf_op jit(solution)/shard_map/all_to_all | solution.py:103
  19.7 6.3 %pad_maximum_fusion = f32[2048,5,128]{2,1,0:T(8,128)} fusion(f32[2048,1,128]{2,1,0:T(1,128)S(1)} %bitcast.99, f32[2048,1,128]{2,1,0:T(1,128)S(1)} %bitcast.100, f32[2048,3,128]{2,1,0:T(4,128)} %bitcast.97), kind=kLoop, calls=%fused_computation.35 | loop fusion | flops 2621440 | bytes 10485760 | tf_op jit(solution)/shard_map/concatenate | solution.py:60
  25.9 4.4 %gather_fusion.1 = f32[512,5,128]{2,1,0:T(8,128)S(1)} fusion(f32[2048,5,128]{2,1,0:T(8,128)} %pad_maximum_fusion, s32[1024]{0:T(1024)S(1)} %pad_clamp_fusion), kind=kCustom, calls=%fused_computation.1 | custom fusion | bytes 2623488 | tf_op jit(solution)/shard_map/gather | solution.py:68
  31.4 138.7 %while.22 = (s32[]{:T(128)}, f32[32,16,128]{2,1,0:T(8,128)}, f32[32,16,128,128]{3,2,1,0:T(8,128)}, f32[32,128]{1,0:T(8,128)S(1)}, f32[32,16,5,128]{3,1,2,0:T(8,1...) while((s32[]{:T(128)}, f32[32,16,128]{2,1,0:T(8,128)}, ...), condition=%wide.region_4.5_spmd, body=%wide.region_1.0_spmd.sunk | while | flops 6289410 | bytes 4449889 | solution.py:79
  36.9 1.8 fusion.45
  41.2 1.8 fusion.45
  54.2 1.8 fusion.45
  58.5 1.8 fusion.45
  62.9 1.8 fusion.45
  67.2 1.8 fusion.45
  84.5 1.8 fusion.45
  93.2 1.8 fusion.45
  106.2 1.8 fusion.45
  110.6 1.8 fusion.45
  114.9 1.8 fusion.45
  123.5 1.8 fusion.45
  127.9 1.8 fusion.45
  132.2 1.8 fusion.45
  136.5 1.8 fusion.45
  153.9 1.8 fusion.45
  162.6 1.8 fusion.45
  166.9 1.8 fusion.45
  170.1 3.9 %fusion.12 = f32[32,64,128]{2,1,0:T(8,128)} fusion(f32[512,128,1]{1,0,2:T(8,128)} %bitcast.109, s32[512]{0:T(512)S(1)} %convert_add_fusion, s32[32,64]{1,0:T(8,128)S(1)} %copy-done.7), kind=kOutput, calls=%fused_computation.36 | convolution fusion | flops 1611661312 | bytes 1320960 | tf_op jit(solution)/shard_map/dot_general | solution.py:95
  174.0 9.8 %all-to-all-start.1 = ((f32[32,64,128]{2,1,0:T(8,128)}), f32[32,64,128]{2,1,0:T(8,128)S(1)}, u32[]{:S(2)}, u32[]{:S(2)}) async-start(f32[32,64,128]{2,1,0:T(8,128)} %fusion.12), calls=%async_computation.1 | async-start | bytes 2097152 | tf_op jit(solution)/shard_map/all_to_all | solution.py:102
  185.1 26.7 %all-to-all-done.1 = f32[32,64,128]{2,1,0:T(8,128)S(1)} async-done(((f32[32,64,128]{2,1,0:T(8,128)}), f32[32,64,128]{2,1,0:T(8,128)S(1)}, u32[]{:S(2)}, u32[]{:S(2)}) %all-to-all-start.1) | async-done | bytes 1048608 | tf_op jit(solution)/shard_map/all_to_all | solution.py:102
  212.3 23.6 %psum.7 = f32[64,128]{1,0:T(8,128)S(1)} all-reduce(f32[64,128]{1,0:T(8,128)S(1)} %fusion.23), channel_id=1, replica_groups=mesh['rep'=8,'dom'=32] {'rep'}, use_global_device_ids=true, to_apply=%region_5.6 | all-reduce | flops 8192 | bytes 65536 | tf_op jit(solution)/shard_map/psum | solution.py:106
  238.2 6.7 %all-to-all-start.2 = ((f32[32,64,128]{2,1,0:T(8,128)}), f32[32,64,128]{2,1,0:T(8,128)S(1)}, u32[]{:S(2)}, u32[]{:S(2)}) async-start(f32[32,64,128]{2,1,0:T(8,128)} %bitcast.35), calls=%async_computation.2 | async-start | bytes 2097152 | tf_op jit(solution)/shard_map/all_to_all | solution.py:119
  245.6 25.0 %all-to-all-done.2 = f32[32,64,128]{2,1,0:T(8,128)S(1)} async-done(((f32[32,64,128]{2,1,0:T(8,128)}), f32[32,64,128]{2,1,0:T(8,128)S(1)}, u32[]{:S(2)}, u32[]{:S(2)}) %all-to-all-start.2) | async-done | bytes 1048608 | tf_op jit(solution)/shard_map/all_to_all | solution.py:119
  270.6 2.5 fusion.34
  273.2 81.8 %while.23 = (s32[]{:T(128)}, f32[32,3,128]{2,1,0:T(4,128)S(1)}, f32[32,16,128]{2,1,0:T(8,128)}, f32[32,16,128,128]{3,2,1,0:T(8,128)}, f32[32,3,128]{2,1,0:T(4,12...) while((s32[]{:T(128)}, f32[32,3,128]{2,1,0:T(4,128)S(1)}, f32[32,16,128]{2,1,0:T(8,128)}, ...), condition=%wide.region_8.9_spmd, body=%wide.region_6.8_spmd.sunk | while | flops 2621442 | bytes 3336289 | solution.py:132
  (536 shorter events, 194.0 us)
Async XLA Ops:
  0.6 0.9 copy-start
  0.7 4.4 %copy-start.6 = (s32[32,64]{1,0:T(8,128)}, s32[32,64]{1,0:T(8,128)S(1)}, u32[]{:S(2)}) copy-start(s32[32,64]{1,0:T(8,128)S(1)} %multiply_add_fusion) | copy-start | bytes 24580
  1.6 18.1 %copy-start.1 = (f32[262144]{0:T(1024)S(1)}, f32[262144]{0:T(1024)}, u32[]{:S(2)}) copy-start(f32[262144]{0:T(1024)} %param.23) | copy-start | bytes 3145732
  1.6 18.1 %copy-start.2 = (f32[262144]{0:T(1024)S(1)}, f32[262144]{0:T(1024)}, u32[]{:S(2)}) copy-start(f32[262144]{0:T(1024)} %param.22) | copy-start | bytes 3145732
  8.3 165.7 %all-to-all-start = ((s32[32,1,64]{2,1,0:T(1,128)}), s32[32,1,64]{2,1,0:T(1,128)S(1)}, u32[]{:S(2)}, u32[]{:S(2)}) async-start(s32[32,1,64]{2,1,0:T(1,128)} %bitcast.18), calls=%async_computation | async-start | bytes 32768 | tf_op jit(solution)/shard_map/all_to_all | solution.py:103
  25.9 4.6 %copy-start.3 = (f32[1,3,4096]{2,0,1:T(1,128)S(1)}, f32[1,3,4096]{2,0,1:T(1,128)}, u32[]{:S(2)}) copy-start(f32[1,3,4096]{2,0,1:T(1,128)} %param.15) | copy-start | bytes 147460
  25.9 4.7 %copy-start.8 = (s32[32]{0:T(128)S(1)}, s32[32]{0:T(128)}, u32[]{:S(2)}) copy-start(s32[32]{0:T(128)} %param.18) | copy-start | bytes 388
  31.4 138.7 %copy-start.7 = (s32[32,64]{1,0:T(8,128)S(1)}, s32[32,64]{1,0:T(8,128)}, u32[]{:S(2)}) copy-start(s32[32,64]{1,0:T(8,128)} %copy-done.6) | copy-start | bytes 24580
  170.1 65.8 %copy-start.4 = (f32[8192]{0:T(1024)S(1)}, f32[8192]{0:T(1024)}, u32[]{:S(2)}) copy-start(f32[8192]{0:T(1024)} %param.24) | copy-start | bytes 98308
  170.1 65.8 %copy-start.5 = (f32[8192]{0:T(1024)S(1)}, f32[8192]{0:T(1024)}, u32[]{:S(2)}) copy-start(f32[8192]{0:T(1024)} %param.25) | copy-start | bytes 98308
  174.0 37.8 %all-to-all-start.1 = ((f32[32,64,128]{2,1,0:T(8,128)}), f32[32,64,128]{2,1,0:T(8,128)S(1)}, u32[]{:S(2)}, u32[]{:S(2)}) async-start(f32[32,64,128]{2,1,0:T(8,128)} %fusion.12), calls=%async_computation.1 | async-start | bytes 2097152 | tf_op jit(solution)/shard_map/all_to_all | solution.py:102
  238.2 32.4 %all-to-all-start.2 = ((f32[32,64,128]{2,1,0:T(8,128)}), f32[32,64,128]{2,1,0:T(8,128)S(1)}, u32[]{:S(2)}, u32[]{:S(2)}) async-start(f32[32,64,128]{2,1,0:T(8,128)} %bitcast.35), calls=%async_computation.2 | async-start | bytes 2097152 | tf_op jit(solution)/shard_map/all_to_all | solution.py:119
where the time goes:
time: 360 us; the launch traced here: 356 us
  other arithmetic  163 us (45%)
  local copies, waits for them, and re-layouts  74.6 us (21%)
  waiting for transfers between devices  51.7 us (14%)
  starting transfers between devices  27.9 us (8%)
  blocking collectives  23.6 us (7%)
  matrix products  11.6 us (3%)
    dynamic_update_slice x32, other arithmetic, shards(): partials, ratios = lax.map(partial_kept, tile_inputs)  57.2 us
    mul x32, other arithmetic, force_kept(): return energy_unit * jnp.sum(weight[None] * offsets, axis=(1, 3))  41.9 us
    all_to_all x1, waiting for transfers between devices, shards(): lax.all_to_all(send_rows, 'dom', split_axis=0, concat_axis=0, tiled=True)  26.7 us
    reduce_sum x32, other arithmetic, partial_kept(): return (jnp.sum(intersection, axis=1), intersection / widths)  25.9 us
    all_to_all x1, waiting for transfers between devices, shards(): lax.all_to_all(back_rows, 'dom', split_axis=0, concat_axis=0, tiled=True)  25 us
    psum x1, blocking collectives, shards(): summed = lax.psum(local_sum, 'rep')  23.6 us
    mul x64, local copies, waits for them, and re-layouts, intersection_tile(): prefactor = weights[None, :, None] * center_weight[:, None, :]  22.5 us
    mul x32, local copies, waits for them, and re-layouts, force_kept(): weight = adjoint_tile[:, None, :] * ratio_tile  22.5 us
  transfers between devices with their start and end apart: 3, of which 2 were waited for; matrix products, arithmetic and copies ran while one was open for 44% of the time, Pallas kernels for 0%

commit v1 on v0

v1 whole, which is shorter than its diff:
```python
import functools
import math

import jax
import jax.numpy as jnp
from jax import lax
from jax.experimental import pallas as pl
from jax.experimental.pallas import tpu as pltpu
from jax.sharding import PartitionSpec as P

ATOM_BLK = 128
COMP_BLK = 128
LISTED = 16
BLK_DEV = 32
COMP_BLOCKS = 2048
CHUNK = 32
FEATS = 48

ENERGY_UNIT = 2.494
EXP_SCALE = -0.5 / math.log(2.0)
NORM = (2.0 * math.pi) ** -1.5


def split3(v):
    hi = v.astype(jnp.bfloat16).astype(jnp.float32)
    rest = v - hi
    mid = rest.astype(jnp.bfloat16).astype(jnp.float32)
    low = (rest - mid).astype(jnp.bfloat16).astype(jnp.float32)
    return hi, mid, low


def choose(row, parts, shape):
    out = jnp.zeros(shape, jnp.float32)
    for k, part in enumerate(parts):
        out = jnp.where(row == k, part, out)
    return out


def overlap_kernel(
    live_ref, list_ref, owner_ref, coords_ref, var_ref, weight_ref, means_ref, cvar_ref, cweight_ref,
    model_ref, ratio_ref,
    left_ref, right_ref, var_lane, weight_lane, comp_rows,
):
    shape = (8, 128)
    row = lax.broadcasted_iota(jnp.int32, shape, 0)
    lane = lax.broadcasted_iota(jnp.int32, (1, 128), 1)
    model_ref[...] = jnp.zeros_like(model_ref)

    def block(a, _):
        at = pl.ds(pl.multiple_of(a * 128, 128), 128)
        live = live_ref[a]
        x, y, z = (coords_ref[0, d : d + 1, at] for d in range(3))
        norm2 = EXP_SCALE * (x * x + y * y + z * z)
        feats = choose(row, (x, y, z, jnp.float32(1.0), norm2), shape)
        hi, mid, low = split3(feats)
        weight = jnp.where(lane < live, weight_ref[pl.ds(a, 1), :], 0.0)
        extra = choose(row, (var_ref[pl.ds(a, 1), :], weight), shape)
        turned = jnp.concatenate([hi, mid, low, hi, mid, hi, extra], axis=0).T
        left_ref[...] = turned[:, :FEATS].astype(jnp.bfloat16)
        var_lane[...] = jnp.broadcast_to(turned[:, FEATS : FEATS + 1], (128, 128))
        weight_lane[...] = jnp.broadcast_to(turned[:, FEATS + 1 : FEATS + 2], (128, 128))

        for k in range(LISTED):
            b = list_ref[a, k]
            cols = pl.ds(pl.multiple_of(b * 128, 128), 128)
            cx, cy, cz = (means_ref[d : d + 1, cols] for d in range(3))
            cnorm = EXP_SCALE * (cx * cx + cy * cy + cz * cz)
            t = -2.0 * EXP_SCALE
            comp = choose(row, (t * cx, t * cy, t * cz, cnorm, jnp.float32(1.0)), shape)
            hi, mid, low = split3(comp)
            right_ref[:, k * 128 : (k + 1) * 128] = jnp.concatenate([hi, hi, hi, mid, mid, low], axis=0).astype(jnp.bfloat16)
            comp_rows[k] = jnp.broadcast_to(cvar_ref[pl.ds(b, 1), :], shape)

        def chunk(c, sums):
            rows = pl.ds(pl.multiple_of(c * CHUNK, CHUNK), CHUNK)
            left = left_ref[rows, :]
            va = var_lane[rows, :]
            wa = weight_lane[rows, :]
            out = []
            for k in range(LISTED):
                scaled = jnp.dot(left, right_ref[:, k * 128 : (k + 1) * 128], preferred_element_type=jnp.float32)
                vc = comp_rows[k]
                v = va.reshape(CHUNK // 8, 8, 128) + vc[None]
                r = lax.rsqrt(v)
                q = r * r
                p = jnp.exp2(scaled.reshape(CHUNK // 8, 8, 128) * q)
                t = (q * r) * p
                ratio_ref[a, rows, k * 128 : (k + 1) * 128] = (t * q).reshape(CHUNK, 128)
                out.append(sums[k] + jnp.sum(t * wa.reshape(CHUNK // 8, 8, 128), axis=0))
            return tuple(out)

        zero = jnp.zeros(shape, jnp.float32)
        sums = lax.fori_loop(0, (live + CHUNK - 1) // CHUNK, chunk, (zero,) * LISTED)
        for k in range(LISTED):
            b = list_ref[a, k]
            place = owner_ref[b]
            target = ((place & 56) << 5) + ((place >> 6) << 3) + (place & 7)
            total = NORM * jnp.sum(sums[k], axis=0, keepdims=True) * cweight_ref[pl.ds(b, 1), :]
            model_ref[pl.ds(target, 1), :] += total
        return 0

    lax.fori_loop(0, BLK_DEV, block, 0)


def force_kernel(
    live_ref, list_ref, owner_ref, coords_ref, weight_ref, means_ref, cweight_ref, adjoint_ref, ratio_ref,
    force_ref,
    right_ref, sums_ref,
):
    shape = (8, 128)
    row = lax.broadcasted_iota(jnp.int32, shape, 0)
    lane = lax.broadcasted_iota(jnp.int32, (1, 128), 1)
    sums_ref[...] = jnp.zeros_like(sums_ref)

    def block(a, _):
        at = pl.ds(pl.multiple_of(a * 128, 128), 128)
        live = live_ref[a]
        for k in range(LISTED):
            b = list_ref[a, k]
            place = owner_ref[b]
            target = (place & 56) * 33 + ((place >> 6) << 3) + (place & 7)
            cols = pl.ds(pl.multiple_of(b * 128, 128), 128)
            cx, cy, cz = (means_ref[d : d + 1, cols] for d in range(3))
            pull = (ENERGY_UNIT * NORM) * adjoint_ref[pl.ds(target, 1), :] * cweight_ref[pl.ds(b, 1), :]
            comp = choose(row, (pull * cx, pull * cy, pull * cz, pull), shape)
            hi, mid, low = split3(comp)
            right_ref[:, k * 128 : (k + 1) * 128] = jnp.concatenate([hi, mid, low, jnp.zeros_like(hi)], axis=0).astype(jnp.bfloat16)

        def chunk(c, _):
            rows = pl.ds(pl.multiple_of(c * CHUNK, CHUNK), CHUNK)
            ratio = ratio_ref[a, rows, :]
            hi = ratio.astype(jnp.bfloat16)
            low = (ratio - hi.astype(jnp.float32)).astype(jnp.bfloat16)
            right = right_ref[...]
            dims = (((1,), (1,)), ((), ()))
            sums_ref[rows, 0:32] = lax.dot_general(
                hi, right, dims, preferred_element_type=jnp.float32
            ) + lax.dot_general(low, right, dims, preferred_element_type=jnp.float32)
            return 0

        lax.fori_loop(0, (live + CHUNK - 1) // CHUNK, chunk, 0)
        turned = sums_ref[...].T
        got = turned[0:8] + turned[8:16] + turned[16:24]
        weight = jnp.where(lane < live, weight_ref[pl.ds(a, 1), :], 0.0)
        for d in range(3):
            force_ref[0, d : d + 1, at] = weight * (coords_ref[0, d : d + 1, at] * got[3:4] - got[d : d + 1])
        return 0

    lax.fori_loop(0, BLK_DEV, block, 0)


def shards(
    coords, atom_var, atom_weight, atoms_live, block_list, owner_map, comp_means, comp_var, comp_weight, target, noise_sigma,
):
    replicas = lax.axis_size("rep")
    domains = lax.axis_size("dom")
    share = COMP_BLOCKS // domains // replicas
    smem = pl.BlockSpec(memory_space=pltpu.SMEM)
    vmem = pl.BlockSpec(memory_space=pltpu.VMEM)
    variances = atom_var.reshape(BLK_DEV, ATOM_BLK)
    weights = atom_weight.reshape(BLK_DEV, ATOM_BLK)
    cvar = comp_var.reshape(COMP_BLOCKS, COMP_BLK)
    cweight = comp_weight.reshape(COMP_BLOCKS, COMP_BLK)
    model, ratio = pl.pallas_call(
        overlap_kernel,
        out_shape=(
            jax.ShapeDtypeStruct((COMP_BLOCKS, COMP_BLK), jnp.float32),
            pltpu.VMEM((BLK_DEV, ATOM_BLK, LISTED * COMP_BLK), jnp.float32),
        ),
        in_specs=[smem] * 3 + [vmem] * 6,
        out_specs=(vmem, vmem),
        scratch_shapes=[
            pltpu.VMEM((ATOM_BLK, FEATS), jnp.bfloat16),
            pltpu.VMEM((FEATS, LISTED * COMP_BLK), jnp.bfloat16),
            pltpu.VMEM((128, 128), jnp.float32),
            pltpu.VMEM((128, 128), jnp.float32),
            pltpu.VMEM((LISTED, 8, 128), jnp.float32),
        ],
        compiler_params=pltpu.CompilerParams(vmem_limit_bytes=16 << 20),
        name="overlap",
    )(atoms_live, block_list, owner_map, coords, variances, weights, comp_means, cvar, cweight)

    parts = lax.all_to_all(model.reshape(replicas, domains * share, COMP_BLK), "rep", 0, 0, tiled=True)
    over_rep = jnp.sum(parts, axis=0)
    parts = lax.all_to_all(over_rep.reshape(domains, share, COMP_BLK), "dom", 0, 0, tiled=True)
    mean = jnp.sum(parts, axis=0) / replicas
    first = lax.axis_index("rep") * share
    wanted = lax.dynamic_slice(target.reshape(-1, COMP_BLK), (first, 0), (share, COMP_BLK))
    sigmas = lax.dynamic_slice(noise_sigma.reshape(-1, COMP_BLK), (first, 0), (share, COMP_BLK))
    misfit = mean - wanted
    adjoint = misfit / (sigmas * sigmas + 0.5 * misfit * misfit) / replicas
    spread = jnp.broadcast_to(adjoint[None], (domains, share, COMP_BLK))
    over_dom = lax.all_to_all(spread, "dom", 0, 0, tiled=True).reshape(domains * share, COMP_BLK)
    back = jnp.concatenate([over_dom, mean], axis=0)
    spread = jnp.broadcast_to(back[None], (replicas,) + back.shape)
    returned = lax.all_to_all(spread, "rep", 0, 0, tiled=True)
    average = returned[:, domains * share :].reshape(-1)
    returned = returned.reshape(-1, COMP_BLK)

    forces = pl.pallas_call(
        force_kernel,
        out_shape=jax.ShapeDtypeStruct(coords.shape, jnp.float32),
        in_specs=[smem] * 3 + [vmem] * 6,
        out_specs=vmem,
        scratch_shapes=[
            pltpu.VMEM((32, LISTED * COMP_BLK), jnp.bfloat16),
            pltpu.VMEM((128, 128), jnp.float32),
        ],
        compiler_params=pltpu.CompilerParams(vmem_limit_bytes=16 << 20),
        name="force",
    )(
        atoms_live, block_list, owner_map, coords, weights, comp_means, cweight, returned,
        pltpu.with_memory_space_constraint(ratio, pltpu.VMEM),
    )
    return average, forces


def solution(mesh):
    return jax.shard_map(
        shards,
        mesh=mesh,
        in_specs=(
            P("rep", None, "dom"), P("dom"), P("dom"), P("dom"), P("dom", None), P(), P(), P(), P(), P("dom"), P("dom"),
        ),
        out_specs=(P("dom"), P("rep", None, "dom")),
        check_vma=False,
    )
```

time: 360 us -> 176 us (0.49)
  the two profiles are of different devices: /device:TPU:32 before, /device:TPU:1 now
where the time goes in v1:
time: 176 us
  Pallas kernels  67.1 us (38%)
  blocking collectives  55.5 us (32%)
  local copies, waits for them, and re-layouts  29.9 us (17%)
  starting transfers between devices  12.4 us (7%)
  waiting for transfers between devices  9.16 us (5%)
    pallas_call x1, Pallas kernels, shards(): pl.pallas_call(overlap_kernel, out_shape=(jax.ShapeDtypeStruct((COMP_BLOC...  35.8 us
    pallas_call x1, Pallas kernels, shards(): pl.pallas_call(force_kernel, out_shape=jax.ShapeDtypeStruct(coords.shape,...  31.3 us
    unnamed x27, local copies, waits for them, and re-layouts  29.2 us
    all_to_all x1, blocking collectives, shards(): returned = lax.all_to_all(spread, 'rep', 0, 0, tiled=True)  22.1 us
    all_to_all x1, blocking collectives, shards(): lax.all_to_all(model.reshape(replicas, domains * share, COMP_BLK), 'rep',...  20.7 us
    all_to_all x1, blocking collectives, shards(): lax.all_to_all(spread, 'dom', 0, 0, tiled=True)  12.7 us
    all_to_all x1, starting transfers between devices, shards(): lax.all_to_all(over_rep.reshape(domains, share, COMP_BLK), 'dom', 0, 0, t...  12.4 us
    all_to_all x1, waiting for transfers between devices, shards(): lax.all_to_all(over_rep.reshape(domains, share, COMP_BLK), 'dom', 0, 0, t...  9.16 us
  transfers between devices with their start and end apart: 1, of which 1 were waited for; matrix products, arithmetic and copies ran while one was open for 0% of the time, Pallas kernels for 0%

profile of v1, /device:TPU:1, one launch (start us, length us, event | category | flops | bytes accessed | tf_op | source)
XLA Modules:
  0.0 176.2 jit_solution(10710084416367506427)
XLA Ops:
  0.6 0.8 copy.18.list_ref
  1.4 0.8 copy.19.coords_ref
  2.2 0.0 copy-start.2
  2.3 1.2 copy-done.2
  3.5 1.2 copy-done.4
  4.7 0.7 copy-done.5
  5.4 0.7 copy-done.7
  6.1 0.7 copy-done.9
  6.8 0.7 copy-done.10
  7.5 35.8 %overlap.1 = (f32[2048,128]{1,0:T(8,128)S(1)}, f32[32,128,2048]{2,1,0:T(8,128)S(1)}) custom-call(s32[32]{0:T(128)S(1)} %copy-done.10, s32[32,16]{1,0:T(8,128)S(1)} %copy.18.list_ref, s32[2048]{0:T(1024)S(1)} %copy-done.7, f32[1,3,4096]{2,1,0:T(4,128)S(1)} %copy.19.coords_ref, f32[32,128]{1,0:T(8,128)S(1)} %bitcast.19, f32[32,128]{1,0:T(8,128)S(1)} %bitcast.17, ...), custom_call_target="tpu_custom_call" | custom-call | tf_op jit(solution)/shard_map/overlap/pallas_call | solution.py:164
  43.3 0.0 copy-start
  43.3 11.1 %copy-done = f32[32,128,2048]{2,1,0:T(8,128)} copy-done((f32[32,128,2048]{2,1,0:T(8,128)}, f32[32,128,2048]{2,1,0:T(8,128)S(1)}, u32[]{:S(2)}) %copy-start) | copy-done | bytes 33554456
  54.3 20.7 %all_to_all.20 = f32[8,256,128]{2,1,0:T(8,128)S(1)} all-to-all(f32[8,256,128]{2,1,0:T(8,128)S(1)} %bitcast.16), channel_id=1, replica_groups=mesh['rep'=8,'dom'=32] {'rep'}, dimensions={0} | all-to-all | bytes 2097152 | tf_op jit(solution)/shard_map/all_to_all | solution.py:183
  75.0 0.7 reduce_sum.18
  75.7 12.4 %all-to-all-start.1 = ((f32[32,8,128]{2,1,0:T(8,128)}), f32[32,8,128]{2,1,0:T(8,128)S(1)}, u32[]{:S(2)}, u32[]{:S(2)}) async-start(f32[32,8,128]{2,1,0:T(8,128)} %bitcast.5), calls=%async_computation.1 | async-start | bytes 262144 | tf_op jit(solution)/shard_map/all_to_all | solution.py:185
  88.1 9.2 %all-to-all-done.1 = f32[32,8,128]{2,1,0:T(8,128)S(1)} async-done(((f32[32,8,128]{2,1,0:T(8,128)}), f32[32,8,128]{2,1,0:T(8,128)S(1)}, u32[]{:S(2)}, u32[]{:S(2)}) %all-to-all-start.1) | async-done | bytes 131104 | tf_op jit(solution)/shard_map/all_to_all | solution.py:185
  97.3 0.7 fusion.2
  98.1 12.7 %all_to_all.21 = f32[32,8,128]{2,1,0:T(8,128)S(1)} all-to-all(f32[32,8,128]{2,1,0:T(8,128)S(1)} %broadcast_in_dim.4), channel_id=1, replica_groups=mesh['rep'=8,'dom'=32] {'dom'}, dimensions={0} | all-to-all | bytes 262144 | tf_op jit(solution)/shard_map/all_to_all | solution.py:193
  110.8 0.1 broadcast_in_dim.5
  110.9 0.0 copy-start.3
  110.9 0.0 copy-start.6
  110.9 0.0 copy-start.8
  110.9 0.0 copy-start.11
  110.9 22.1 %all_to_all.22 = f32[8,264,128]{2,1,0:T(8,128)S(1)} all-to-all(f32[8,264,128]{2,1,0:T(8,128)S(1)} %broadcast_in_dim.5), channel_id=1, replica_groups=mesh['rep'=8,'dom'=32] {'rep'}, dimensions={0} | all-to-all | bytes 2162688 | tf_op jit(solution)/shard_map/all_to_all | solution.py:196
  133.0 0.0 copy-done.3
  133.0 0.0 copy-done.6
  133.0 0.0 copy-done.8
  133.0 0.0 copy-done.11
  133.1 10.5 %copy-done.1 = f32[32,128,2048]{2,1,0:T(8,128)S(1)} copy-done((f32[32,128,2048]{2,1,0:T(8,128)S(1)}, f32[32,128,2048]{2,1,0:T(8,128)}, u32[]{:S(2)}) %copy-start.1) | copy-done | bytes 33554456
  143.6 31.3 %force.1 = f32[1,3,4096]{2,1,0:T(4,128)S(1)} custom-call(s32[32]{0:T(128)S(1)} %copy-done.11, s32[32,16]{1,0:T(8,128)S(1)} %copy.18.list_ref, s32[2048]{0:T(1024)S(1)} %copy-done.8, f32[1,3,4096]{2,1,0:T(4,128)S(1)} %copy.19.coords_ref, f32[32,128]{1,0:T(8,128)S(1)} %bitcast.18, f32[3,262144]{1,0:T(4,128)} %means_ref.3, f32[2048,128]{1,0:T(8,128)S(1)} %bitcast.14, ...), custom_call_target="tpu_custom_call" | custom-call | tf_op jit(solution)/shard_map/force/pallas_call | solution.py:200
  174.9 0.7 copy.22
  175.6 0.6 slice_bitcast_fusion
  (9 shorter events, 0.1 us)
Async XLA Ops:
  2.2 1.2 copy-start.2
  3.5 1.2 copy-start.4
  4.7 0.7 copy-start.5
  5.4 0.7 copy-start.7
  6.1 0.7 copy-start.9
  6.8 0.7 copy-start.10
  43.3 11.1 %copy-start = (f32[32,128,2048]{2,1,0:T(8,128)}, f32[32,128,2048]{2,1,0:T(8,128)S(1)}, u32[]{:S(2)}) copy-start(f32[32,128,2048]{2,1,0:T(8,128)S(1)} %get-tuple-element.5.ratio_ref) | copy-start | bytes 100663296
  75.7 21.6 %all-to-all-start.1 = ((f32[32,8,128]{2,1,0:T(8,128)}), f32[32,8,128]{2,1,0:T(8,128)S(1)}, u32[]{:S(2)}, u32[]{:S(2)}) async-start(f32[32,8,128]{2,1,0:T(8,128)} %bitcast.5), calls=%async_computation.1 | async-start | bytes 262144 | tf_op jit(solution)/shard_map/all_to_all | solution.py:185
  110.9 22.1 %copy-start.3 = (f32[262144]{0:T(1024)S(1)}, f32[262144]{0:T(1024)}, u32[]{:S(2)}) copy-start(f32[262144]{0:T(1024)} %param.19) | copy-start | bytes 3145732
  110.9 22.1 %copy-start.6 = (f32[4096]{0:T(1024)S(1)}, f32[4096]{0:T(1024)}, u32[]{:S(2)}) copy-start(f32[4096]{0:T(1024)} %param.13) | copy-start | bytes 49156
  110.9 22.1 %copy-start.8 = (s32[2048]{0:T(1024)S(1)}, s32[2048]{0:T(1024)}, u32[]{:S(2)}) copy-start(s32[2048]{0:T(1024)} %owner_ref.3) | copy-start | bytes 24580
  110.9 22.1 %copy-start.11 = (s32[32]{0:T(128)S(1)}, s32[32]{0:T(128)}, u32[]{:S(2)}) copy-start(s32[32]{0:T(128)} %live_ref.3) | copy-start | bytes 388
  133.1 10.5 %copy-start.1 = (f32[32,128,2048]{2,1,0:T(8,128)S(1)}, f32[32,128,2048]{2,1,0:T(8,128)}, u32[]{:S(2)}) copy-start(f32[32,128,2048]{2,1,0:T(8,128)} %copy-done) | copy-start | bytes 100663296

commit v2 on v1

v2 whole, which is shorter than its diff:
```python
import functools
import math

import jax
import jax.numpy as jnp
from jax import lax
from jax.experimental import pallas as pl
from jax.experimental.pallas import tpu as pltpu
from jax.sharding import PartitionSpec as P

ATOM_BLK = 128
COMP_BLK = 128
LISTED = 16
BLK_DEV = 32
COMP_BLOCKS = 2048
REPLICAS = 8
DEAD = 1e30

ENERGY_UNIT = 2.494
EXP_SCALE = -0.5 / math.log(2.0)
NORM = (2.0 * math.pi) ** -1.5


def split3(v):
    hi = v.astype(jnp.bfloat16).astype(jnp.float32)
    rest = v - hi
    mid = rest.astype(jnp.bfloat16).astype(jnp.float32)
    return hi, mid, rest - mid


def atom_scale(weight, live, dead):
    return jnp.where(live, jnp.exp2(jnp.log(weight) * (-2.0 / (3.0 * math.log(2.0)))), dead)


def choose(row, parts, shape, other=0.0):
    out = jnp.full(shape, other, jnp.float32)
    for k, part in enumerate(parts):
        out = jnp.where(row == k, part, out)
    return out


def overlap_kernel(
    live_any, list_any, owner_any, coords_any, var_any, weight_any, means_any, cvar_any, cweight_any,
    model_ref, ratio_ref,
    live_ref, list_ref, owner_ref, coords_ref, var_ref, weight_ref, means_ref, cvar_ref, cweight_ref, sems,
    ratio_buf, ratio_sems,
):
    pairs = (
        (live_any, live_ref), (list_any, list_ref), (owner_any, owner_ref), (coords_any, coords_ref),
        (var_any, var_ref), (weight_any, weight_ref), (means_any, means_ref), (cvar_any, cvar_ref),
        (cweight_any, cweight_ref),
    )
    copies = [pltpu.make_async_copy(src, dst, sems.at[n]) for n, (src, dst) in enumerate(pairs)]
    for copy in copies:
        copy.start()
    shape = (8, 128)
    row = lax.broadcasted_iota(jnp.int32, shape, 0)
    lane = lax.broadcasted_iota(jnp.int32, (1, 128), 1)
    for_distance = ((row < 4) | (row == 5)).astype(jnp.float32)
    for_variance = ((row == 4) | (row == 6)).astype(jnp.float32)
    model_ref[...] = jnp.zeros_like(model_ref)
    for copy in copies:
        copy.wait()

    def store(a):
        slot = a & 1
        return pltpu.make_async_copy(ratio_buf.at[slot], ratio_ref.at[a], ratio_sems.at[slot])

    def block(a, _):
        live = live_ref[a]
        slot = a & 1

        @pl.when(a >= 2)
        def _():
            store(a - 2).wait()

        x, y, z = (coords_ref[pl.ds(d * BLK_DEV + a, 1), :] for d in range(3))
        scale = atom_scale(weight_ref[pl.ds(a, 1), :], lane < live, DEAD)
        norm2 = EXP_SCALE * (x * x + y * y + z * z)
        t = -2.0 * EXP_SCALE
        feats = scale * choose(row, (t * x, t * y, t * z, EXP_SCALE, 1.0, norm2, var_ref[pl.ds(a, 1), :]), shape)
        hi, mid, low = split3(feats)
        left = jnp.concatenate([hi, mid, low, hi, mid, hi], axis=0).T.astype(jnp.bfloat16)

        for k in range(LISTED):
            b = list_ref[k, a]
            cols = pl.ds(pl.multiple_of(b * 128, 128), 128)
            cx, cy, cz = (means_ref[d : d + 1, cols] for d in range(3))
            cnorm = cx * cx + cy * cy + cz * cz
            comp = choose(row, (cx, cy, cz, cnorm, cvar_ref[pl.ds(b, 1), :]), shape, 1.0)
            sides = []
            hi, mid, low = split3(comp)
            for mask in (for_distance, for_variance):
                h, m, w = hi * mask, mid * mask, low * mask
                sides.append(jnp.concatenate([h, h, h, m, m, w], axis=0).astype(jnp.bfloat16))
            right = jnp.concatenate(sides, axis=1)
            both = jnp.dot(left, right, preferred_element_type=jnp.float32).reshape(16, 8, 256)
            r = lax.rsqrt(both[:, :, 128:])
            q = r * r
            t = (q * r) * jnp.exp2(both[:, :, :128] * q)
            ratio_buf[slot, :, k * 128 : (k + 1) * 128] = (t * q).reshape(128, 128)
            total = jnp.sum(jnp.sum(t, axis=0), axis=0, keepdims=True)
            place = owner_ref[b]
            target = ((place & 56) << 5) + ((place >> 6) << 3) + (place & 7)
            model_ref[pl.ds(target, 1), :] += NORM * total * cweight_ref[pl.ds(b, 1), :]
        store(a).start()
        return 0

    lax.fori_loop(0, BLK_DEV, block, 0)
    store(BLK_DEV - 2).wait()
    store(BLK_DEV - 1).wait()


def in_hbm(array):
    return pltpu.with_memory_space_constraint(array, pltpu.HBM)


def rep_sum_kernel(parts_ref, out_ref):
    out_ref[...] = jnp.sum(parts_ref[...], axis=0)


def adjoint_kernel(parts_ref, target_ref, sigma_ref, spread_ref, mean_ref):
    share = mean_ref.shape[0]
    mean = jnp.sum(parts_ref[...], axis=0) / REPLICAS
    first = pl.ds(pl.multiple_of(lax.axis_index("rep") * share, share), share)
    sigma = sigma_ref[first, :]
    misfit = mean - target_ref[first, :]
    adjoint = misfit / (sigma * sigma + 0.5 * misfit * misfit) / REPLICAS
    mean_ref[...] = mean
    spread_ref[...] = jnp.broadcast_to(adjoint[None], spread_ref.shape)


def spread_kernel(adjoint_ref, mean_ref, out_ref):
    rows = adjoint_ref.shape[0]
    for r in range(REPLICAS):
        out_ref[r, :rows] = adjoint_ref[...]
        out_ref[r, rows:] = mean_ref[...]


def force_kernel(
    live_ref, list_ref, owner_ref, coords_ref, weight_ref, means_ref, cweight_ref, adjoint_ref, ratio_any,
    force_ref,
    ratio_ref, ratio_sems,
):
    depth = ratio_ref.shape[0]

    def load(a):
        slot = lax.rem(a, depth)
        return pltpu.make_async_copy(ratio_any.at[a], ratio_ref.at[slot], ratio_sems.at[slot])

    for first in range(depth - 1):
        load(jnp.int32(first)).start()

    shape = (8, 128)
    row = lax.broadcasted_iota(jnp.int32, shape, 0)
    upper = row < 4
    lane = lax.broadcasted_iota(jnp.int32, (1, 128), 1)

    def block(a, _):
        @pl.when(a + depth - 1 < BLK_DEV)
        def _():
            load(a + depth - 1).start()

        live = live_ref[a]
        rights = []
        for k in range(LISTED):
            b = list_ref[k, a]
            place = owner_ref[b]
            target = (place & 56) * 33 + ((place >> 6) << 3) + (place & 7)
            cols = pl.ds(pl.multiple_of(b * 128, 128), 128)
            cx, cy, cz = (means_ref[d : d + 1, cols] for d in range(3))
            pull = (ENERGY_UNIT * NORM) * adjoint_ref[pl.ds(target, 1), :] * cweight_ref[pl.ds(b, 1), :]
            hi, mid, low = split3(pull * choose(row & 3, (cx, cy, cz, 1.0), shape))
            rights.append(
                jnp.concatenate([jnp.where(upper, hi, mid), jnp.where(upper, low, 0.0)], axis=0).astype(jnp.bfloat16)
            )
        load(a).wait()
        slot = lax.rem(a, depth)
        total = jnp.zeros((128, 16), jnp.float32)
        dims = (((1,), (1,)), ((), ()))
        for k in range(0, LISTED, 2):
            right = jnp.concatenate(rights[k : k + 2], axis=1)
            ratio = ratio_ref[slot, :, k * 128 : (k + 2) * 128]
            hi = ratio.astype(jnp.bfloat16)
            low = (ratio - hi.astype(jnp.float32)).astype(jnp.bfloat16)
            total += lax.dot_general(hi, right, dims, preferred_element_type=jnp.float32)
            total += lax.dot_general(low, right, dims, preferred_element_type=jnp.float32)
        turned = total.T
        got = turned[0:8] + turned[8:16]
        got = got[0:4] + got[4:8]
        scale = atom_scale(weight_ref[pl.ds(a, 1), :], lane < live, 0.0)
        for d in range(3):
            at = pl.ds(d * BLK_DEV + a, 1)
            force_ref[at, :] = scale * (coords_ref[at, :] * got[3:4] - got[d : d + 1])
        return 0

    lax.fori_loop(0, BLK_DEV, block, 0)


def shards(
    coords, atom_var, atom_weight, atoms_live, block_list, owner_map, comp_means, comp_var, comp_weight, target, noise_sigma,
):
    replicas = lax.axis_size("rep")
    domains = lax.axis_size("dom")
    share = COMP_BLOCKS // domains // replicas
    smem = pl.BlockSpec(memory_space=pltpu.SMEM)
    vmem = pl.BlockSpec(memory_space=pltpu.VMEM)
    hbm = pl.BlockSpec(memory_space=pltpu.HBM)
    small = pltpu.CompilerParams(vmem_limit_bytes=6 << 20)
    f32 = jnp.float32
    positions = coords.reshape(3 * BLK_DEV, ATOM_BLK)
    listed = block_list.T
    variances = atom_var.reshape(BLK_DEV, ATOM_BLK)
    weights = atom_weight.reshape(BLK_DEV, ATOM_BLK)
    cvar = comp_var.reshape(COMP_BLOCKS, COMP_BLK)
    cweight = comp_weight.reshape(COMP_BLOCKS, COMP_BLK)
    model, ratio = pl.pallas_call(
        overlap_kernel,
        out_shape=(
            jax.ShapeDtypeStruct((COMP_BLOCKS, COMP_BLK), f32),
            pltpu.HBM((BLK_DEV, ATOM_BLK, LISTED * COMP_BLK), f32),
        ),
        in_specs=[hbm] * 9,
        out_specs=(vmem, hbm),
        scratch_shapes=[
            pltpu.SMEM((BLK_DEV,), jnp.int32),
            pltpu.SMEM((LISTED, BLK_DEV), jnp.int32),
            pltpu.SMEM((COMP_BLOCKS,), jnp.int32),
            pltpu.VMEM((3 * BLK_DEV, ATOM_BLK), f32),
            pltpu.VMEM((BLK_DEV, ATOM_BLK), f32),
            pltpu.VMEM((BLK_DEV, ATOM_BLK), f32),
            pltpu.VMEM((3, COMP_BLOCKS * COMP_BLK), f32),
            pltpu.VMEM((COMP_BLOCKS, COMP_BLK), f32),
            pltpu.VMEM((COMP_BLOCKS, COMP_BLK), f32),
            pltpu.SemaphoreType.DMA((9,)),
            pltpu.VMEM((2, ATOM_BLK, LISTED * COMP_BLK), f32),
            pltpu.SemaphoreType.DMA((2,)),
        ],
        compiler_params=pltpu.CompilerParams(vmem_limit_bytes=16 << 20),
        name="overlap",
    )(*(in_hbm(v) for v in (atoms_live, listed, owner_map, positions, variances, weights, comp_means, cvar, cweight)))

    parts = lax.all_to_all(model.reshape(replicas, domains * share, COMP_BLK), "rep", 0, 0, tiled=True)
    over_rep = pl.pallas_call(
        rep_sum_kernel,
        out_shape=jax.ShapeDtypeStruct((domains * share, COMP_BLK), f32),
        in_specs=[vmem], out_specs=vmem, compiler_params=small, name="rep_sum",
    )(parts)
    parts = lax.all_to_all(over_rep.reshape(domains, share, COMP_BLK), "dom", 0, 0, tiled=True)
    spread, mean = pl.pallas_call(
        adjoint_kernel,
        out_shape=(
            jax.ShapeDtypeStruct((domains, share, COMP_BLK), f32), jax.ShapeDtypeStruct((share, COMP_BLK), f32),
        ),
        in_specs=[vmem] * 3, out_specs=(vmem, vmem), compiler_params=small, name="adjoint",
    )(parts, target.reshape(-1, COMP_BLK), noise_sigma.reshape(-1, COMP_BLK))
    over_dom = lax.all_to_all(spread, "dom", 0, 0, tiled=True).reshape(domains * share, COMP_BLK)
    spread = pl.pallas_call(
        spread_kernel,
        out_shape=jax.ShapeDtypeStruct((replicas, (domains + 1) * share, COMP_BLK), f32),
        in_specs=[vmem] * 2, out_specs=vmem, compiler_params=small, name="spread",
    )(over_dom, mean)
    returned = lax.all_to_all(spread, "rep", 0, 0, tiled=True)
    average = returned[:, domains * share :].reshape(-1)
    returned = returned.reshape(-1, COMP_BLK)

    forces = pl.pallas_call(
        force_kernel,
        out_shape=jax.ShapeDtypeStruct(positions.shape, f32),
        in_specs=[smem] * 3 + [vmem] * 5 + [hbm],
        out_specs=vmem,
        scratch_shapes=[
            pltpu.VMEM((4, ATOM_BLK, LISTED * COMP_BLK), f32),
            pltpu.SemaphoreType.DMA((4,)),
        ],
        compiler_params=pltpu.CompilerParams(vmem_limit_bytes=16 << 20),
        name="force",
    )(
        atoms_live, listed, owner_map, positions, weights, comp_means, cweight, returned,
        in_hbm(ratio),
    )
    return average, forces.reshape(coords.shape)


def solution(mesh):
    return jax.shard_map(
        shards,
        mesh=mesh,
        in_specs=(
            P("rep", None, "dom"), P("dom"), P("dom"), P("dom"), P("dom", None), P(), P(), P(), P(), P("dom"), P("dom"),
        ),
        out_specs=(P("dom"), P("rep", None, "dom")),
        check_vma=False,
    )
```

time: 176 us -> 127 us (0.72)
  local copies, waits for them, and re-layouts: 29.9 us -> 0.67 us
  blocking collectives: 55.5 us -> 76 us
  Pallas kernels: 67.1 us -> 49.1 us
  starting transfers between devices: 12.4 us -> 0 us
  waiting for transfers between devices: 9.16 us -> 0 us
    unnamed x27 -> x18, local copies, waits for them, and re-layouts: 29.2 us -> 0.05 us
    all_to_all x0 -> x1, blocking collectives: none -> 20.4 us  [shards(): lax.all_to_all(over_rep.reshape(domains, share, COMP_BLK), 'dom', 0, 0, t...]
    all_to_all x1 -> x0, starting transfers between devices: 12.4 us -> none  [shards(): lax.all_to_all(over_rep.reshape(domains, share, COMP_BLK), 'dom', 0, 0, t...]
    pallas_call x1 -> x4, Pallas kernels: 31.3 us -> 20.4 us  [the longest x1 20.2 us: shards(): pl.pallas_call(force_kernel, out_shape=jax.ShapeDtypeStruct(positions.sha...]
    all_to_all x1 -> x0, waiting for transfers between devices: 9.16 us -> none  [shards(): lax.all_to_all(over_rep.reshape(domains, share, COMP_BLK), 'dom', 0, 0, t...]
    pallas_call x1, Pallas kernels: 35.8 us -> 28.7 us  [shards(): pl.pallas_call(overlap_kernel, out_shape=(jax.ShapeDtypeStruct((COMP_BLOC...]
  transfers between devices with their start and end apart: 1 -> 0, of which waited for: 1 -> 0; matrix products, arithmetic and copies ran while one was open for 0% -> 0% of each run, Pallas kernels for 0% -> 0%
where the time goes in v2:
time: 127 us
  blocking collectives  76 us (60%)
  Pallas kernels  49.1 us (39%)
    pallas_call x1, Pallas kernels, shards(): pl.pallas_call(overlap_kernel, out_shape=(jax.ShapeDtypeStruct((COMP_BLOC...  28.7 us
    all_to_all x1, blocking collectives, shards(): returned = lax.all_to_all(spread, 'rep', 0, 0, tiled=True)  22.1 us
    all_to_all x1, blocking collectives, shards(): lax.all_to_all(model.reshape(replicas, domains * share, COMP_BLK), 'rep',...  20.9 us
    all_to_all x1, blocking collectives, shards(): lax.all_to_all(over_rep.reshape(domains, share, COMP_BLK), 'dom', 0, 0, t...  20.4 us
    pallas_call x1, Pallas kernels, shards(): pl.pallas_call(force_kernel, out_shape=jax.ShapeDtypeStruct(positions.sha...  20.2 us
    all_to_all x1, blocking collectives, shards(): lax.all_to_all(spread, 'dom', 0, 0, tiled=True)  12.7 us

profile of v2, /device:TPU:1, one launch (start us, length us, event | category | flops | bytes accessed | tf_op | source)
XLA Modules:
  0.0 126.5 jit_solution(2722684564138971704)
XLA Ops:
  0.6 28.7 %overlap.1 = (f32[2048,128]{1,0:T(8,128)S(1)}, f32[32,128,2048]{2,1,0:T(8,128)}) custom-call(s32[32]{0:T(128)} %live_ref.1, s32[16,32]{1,0:T(8,128)} %bitcast.25, s32[2048]{0:T(1024)} %owner_ref.1, f32[96,128]{1,0:T(8,128)} %bitcast.21, f32[32,128]{1,0:T(8,128)} %bitcast.31, f32[32,128]{1,0:T(8,128)} %bitcast.23, f32[3,262144]{1,0:T(4,128)} %means_ref.1, ...), custom_call_target="tpu_custom_call" | custom-call | tf_op jit(solution)/shard_map/overlap/pallas_call | solution.py:217
  29.4 0.0 copy-start.6
  29.4 0.0 copy-start.7
  29.4 0.0 copy-start.3
  29.4 0.0 copy-start.4
  29.4 0.0 copy-start.5
  29.4 20.9 %all_to_all.20.parts_ref = f32[8,256,128]{2,1,0:T(8,128)S(1)} all-to-all(f32[8,256,128]{2,1,0:T(8,128)S(1)} %bitcast.18), channel_id=1, replica_groups=mesh['rep'=8,'dom'=32] {'rep'}, dimensions={0} | all-to-all | bytes 2097152 | tf_op jit(solution)/shard_map/all_to_all | solution.py:243
  50.3 0.0 copy-start
  50.3 0.1 rep_sum.1
  50.3 20.4 %all_to_all.21.parts_ref = f32[32,8,128]{2,1,0:T(8,128)S(1)} all-to-all(f32[32,8,128]{2,1,0:T(8,128)S(1)} %bitcast.20), channel_id=1, replica_groups=mesh['rep'=8,'dom'=32] {'dom'}, dimensions={0} | all-to-all | bytes 262144 | tf_op jit(solution)/shard_map/all_to_all | solution.py:249
  70.7 0.0 copy-done.6
  70.7 0.0 copy-done.7
  70.7 0.1 adjoint.1
  70.8 12.7 %all_to_all.22 = f32[32,8,128]{2,1,0:T(8,128)S(1)} all-to-all(f32[32,8,128]{2,1,0:T(8,128)S(1)} %get-tuple-element.7), channel_id=1, replica_groups=mesh['rep'=8,'dom'=32] {'dom'}, dimensions={0} | all-to-all | bytes 262144 | tf_op jit(solution)/shard_map/all_to_all | solution.py:257
  83.5 0.1 spread.1
  83.6 0.0 copy-start.1
  83.6 0.0 copy-start.2
  83.6 0.0 copy-start.8
  83.6 22.1 %all_to_all.23 = f32[8,264,128]{2,1,0:T(8,128)S(1)} all-to-all(f32[8,264,128]{2,1,0:T(8,128)S(1)} %spread.1), channel_id=1, replica_groups=mesh['rep'=8,'dom'=32] {'rep'}, dimensions={0} | all-to-all | bytes 2162688 | tf_op jit(solution)/shard_map/all_to_all | solution.py:263
  105.7 0.0 copy-done.3
  105.7 0.0 copy-done.4
  105.7 0.0 copy-done.5
  105.7 0.0 copy-done
  105.7 0.0 copy-done.1
  105.7 0.0 copy-done.2
  105.7 0.0 copy-done.8
  105.7 20.2 %force.1 = f32[96,128]{1,0:T(8,128)} custom-call(s32[32]{0:T(128)S(1)} %copy-done.8, s32[16,32]{1,0:T(8,128)S(1)} %bitcast.26, s32[2048]{0:T(1024)S(1)} %copy-done.5, f32[96,128]{1,0:T(8,128)S(1)} %bitcast.22, f32[32,128]{1,0:T(8,128)S(1)} %bitcast.24, f32[3,262144]{1,0:T(4,128)S(1)} %copy-done, f32[2048,128]{1,0:T(8,128)S(1)} %bitcast.17, ...), custom_call_target="tpu_custom_call" | custom-call | tf_op jit(solution)/shard_map/force/pallas_call | solution.py:267
  125.9 0.6 slice_bitcast_fusion
Async XLA Ops:
  29.4 41.3 %copy-start.6 = (f32[8192]{0:T(1024)S(1)}, f32[8192]{0:T(1024)}, u32[]{:S(2)}) copy-start(f32[8192]{0:T(1024)} %param.20) | copy-start | bytes 98308
  29.4 41.3 %copy-start.7 = (f32[8192]{0:T(1024)S(1)}, f32[8192]{0:T(1024)}, u32[]{:S(2)}) copy-start(f32[8192]{0:T(1024)} %param.21) | copy-start | bytes 98308
  29.4 76.3 %copy-start.3 = (f32[4096]{0:T(1024)S(1)}, f32[4096]{0:T(1024)}, u32[]{:S(2)}) copy-start(f32[4096]{0:T(1024)} %param.13) | copy-start | bytes 49156
  29.4 76.3 %copy-start.4 = (s32[32,16]{0,1:T(8,128)S(1)}, s32[32,16]{0,1:T(8,128)}, u32[]{:S(2)}) copy-start(s32[32,16]{0,1:T(8,128)} %param.15) | copy-start | bytes 6148
  29.4 76.3 %copy-start.5 = (s32[2048]{0:T(1024)S(1)}, s32[2048]{0:T(1024)}, u32[]{:S(2)}) copy-start(s32[2048]{0:T(1024)} %owner_ref.1) | copy-start | bytes 24580
  50.3 55.4 %copy-start = (f32[3,262144]{1,0:T(4,128)S(1)}, f32[3,262144]{1,0:T(4,128)}, u32[]{:S(2)}) copy-start(f32[3,262144]{1,0:T(4,128)} %means_ref.1) | copy-start | bytes 9437188
  83.6 22.1 %copy-start.1 = (f32[262144]{0:T(1024)S(1)}, f32[262144]{0:T(1024)}, u32[]{:S(2)}) copy-start(f32[262144]{0:T(1024)} %param.19) | copy-start | bytes 3145732
  83.6 22.1 %copy-start.2 = (f32[1,3,4096]{2,0,1:T(1,128)S(1)}, f32[1,3,4096]{2,0,1:T(1,128)}, u32[]{:S(2)}) copy-start(f32[1,3,4096]{2,0,1:T(1,128)} %param.11) | copy-start | bytes 147460
  83.6 22.1 %copy-start.8 = (s32[32]{0:T(128)S(1)}, s32[32]{0:T(128)}, u32[]{:S(2)}) copy-start(s32[32]{0:T(128)} %live_ref.1) | copy-start | bytes 388

commit v3 on v2

v3 whole, which is shorter than its diff:
```python
import functools
import math

import jax
import jax.numpy as jnp
from jax import lax
from jax.experimental import pallas as pl
from jax.experimental.pallas import tpu as pltpu
from jax.sharding import PartitionSpec as P

ATOM_BLK = 128
COMP_BLK = 128
LISTED = 16
BLK_DEV = 32
COMP_BLOCKS = 2048
REPLICAS = 8
FEATS = 48
PART = 8

ENERGY_UNIT = 2.494
EXP_SCALE = -0.5 / math.log(2.0)
NORM = (2.0 * math.pi) ** -1.5


def split3(v):
    hi = v.astype(jnp.bfloat16).astype(jnp.float32)
    rest = v - hi
    mid = rest.astype(jnp.bfloat16).astype(jnp.float32)
    return hi, mid, rest - mid


def choose(row, parts, shape, other=0.0):
    out = jnp.full(shape, other, jnp.float32)
    for k, part in enumerate(parts):
        out = jnp.where(row == k, part, out)
    return out


def right_side(comp):
    hi, mid, low = split3(comp)
    return jnp.concatenate([hi, hi, hi, mid, mid, low], axis=0).astype(jnp.bfloat16)


def spread_lanes(atoms, column):
    return jnp.broadcast_to(atoms[:, column : column + 1], (128, 128)).reshape(16, 8, 128)


def pair_terms(left, spread_var, comp_of):
    for k in range(0, LISTED, 2):
        comps = [comp_of(k), comp_of(k + 1)]
        right = jnp.concatenate([right_side(comp) for comp in comps], axis=1)
        scaled = jnp.dot(left, right, preferred_element_type=jnp.float32).reshape(16, 8, 256)
        for n in range(2):
            r = lax.rsqrt(spread_var + comps[n][5:6].reshape(1, 1, 128))
            q = r * r
            yield k + n, q, (q * r) * jnp.exp2(scaled[:, :, n * 128 : (n + 1) * 128] * q)


def overlap_kernel(
    live_any, list_any, owner_any, coords_any, var_any, weight_any, means_any, cvar_any, cweight_any,
    model_ref, comps_ref, atoms_ref,
    live_ref, list_ref, owner_ref, coords_ref, var_ref, weight_ref, means_ref, cvar_ref, cweight_ref, sems,
):
    pairs = (
        (live_any, live_ref), (list_any, list_ref), (owner_any, owner_ref), (coords_any, coords_ref),
        (var_any, var_ref), (weight_any, weight_ref), (means_any, means_ref), (cvar_any, cvar_ref),
        (cweight_any, cweight_ref),
    )
    copies = [pltpu.make_async_copy(src, dst, sems.at[n]) for n, (src, dst) in enumerate(pairs)]
    for copy in copies:
        copy.start()
    shape = (8, 128)
    row = lax.broadcasted_iota(jnp.int32, shape, 0)
    lane = lax.broadcasted_iota(jnp.int32, (1, 128), 1)
    model_ref[...] = jnp.zeros_like(model_ref)
    for copy in copies:
        copy.wait()

    def block(a, _):
        x, y, z = (coords_ref[pl.ds(d * BLK_DEV + a, 1), :] for d in range(3))
        norm2 = EXP_SCALE * (x * x + y * y + z * z)
        t = -2.0 * EXP_SCALE
        hi, mid, low = split3(choose(row, (t * x, t * y, t * z, EXP_SCALE, norm2), shape))
        weight = jnp.where(lane < live_ref[a], weight_ref[pl.ds(a, 1), :], 0.0)
        extra = choose(row, (var_ref[pl.ds(a, 1), :], weight), shape)
        feats = jnp.concatenate([hi, mid, low, hi, mid, hi, extra], axis=0)
        atoms_ref[a] = feats
        atoms = feats.T
        left = atoms[:, :FEATS].astype(jnp.bfloat16)
        spread_var = spread_lanes(atoms, FEATS)
        spread_weight = spread_lanes(atoms, FEATS + 1)

        def comp_of(k):
            b = list_ref[k, a]
            cols = pl.ds(pl.multiple_of(b * 128, 128), 128)
            cx, cy, cz = (means_ref[d : d + 1, cols] for d in range(3))
            norm = cx * cx + cy * cy + cz * cz
            comp = choose(row, (cx, cy, cz, norm, 1.0, cvar_ref[pl.ds(b, 1), :], cweight_ref[pl.ds(b, 1), :]), shape)
            comps_ref[a, k] = comp
            return comp

        for k, _, t in pair_terms(left, spread_var, comp_of):
            total = jnp.sum(jnp.sum(t * spread_weight, axis=0), axis=0, keepdims=True)
            place = owner_ref[list_ref[k, a]]
            target = ((place & 56) << 5) + ((place >> 6) << 3) + (place & 7)
            model_ref[pl.ds(target, 1), :] += NORM * total * comps_ref[a, k, 6:7, :]
        return 0

    lax.fori_loop(0, BLK_DEV, block, 0)


def ratio_kernel(atoms_ref, comps_ref, ratio_any, ratio_buf, sems):
    blocks = ratio_any.shape[0]

    def store(a):
        return pltpu.make_async_copy(ratio_buf.at[a & 1], ratio_any.at[a], sems.at[a & 1])

    def block(a, _):
        @pl.when(a >= 2)
        def _():
            store(a - 2).wait()

        atoms = atoms_ref[a].T
        left = atoms[:, :FEATS].astype(jnp.bfloat16)
        spread_var = spread_lanes(atoms, FEATS)
        slot = a & 1
        for k, q, t in pair_terms(left, spread_var, lambda k: comps_ref[a, k]):
            ratio_buf[slot, :, k * 128 : (k + 1) * 128] = (t * q).reshape(128, 128)
        store(a).start()
        return 0

    lax.fori_loop(0, blocks, block, 0)
    store(blocks - 2).wait()
    store(blocks - 1).wait()


def in_hbm(array):
    return pltpu.with_memory_space_constraint(array, pltpu.HBM)


def rep_sum_kernel(parts_ref, out_ref):
    out_ref[...] = jnp.sum(parts_ref[...], axis=0)


def adjoint_kernel(parts_ref, target_ref, sigma_ref, spread_ref, mean_ref):
    share = mean_ref.shape[0]
    mean = jnp.sum(parts_ref[...], axis=0) / REPLICAS
    first = pl.ds(pl.multiple_of(lax.axis_index("rep") * share, share), share)
    sigma = sigma_ref[first, :]
    misfit = mean - target_ref[first, :]
    adjoint = misfit / (sigma * sigma + 0.5 * misfit * misfit) / REPLICAS
    mean_ref[...] = mean
    spread_ref[...] = jnp.broadcast_to(adjoint[None], spread_ref.shape)


def spread_kernel(adjoint_ref, mean_ref, out_ref):
    rows = adjoint_ref.shape[0]
    for r in range(REPLICAS):
        out_ref[r, :rows] = adjoint_ref[...]
        out_ref[r, rows:] = mean_ref[...]


def force_kernel(
    live_ref, list_ref, owner_ref, coords_ref, weight_ref, comps_ref, adjoint_ref, *refs,
):
    parts = BLK_DEV // PART
    ratio_any, (force_ref, ratio_ref, ratio_sems) = refs[:parts], refs[parts:]
    depth = ratio_ref.shape[0]
    shape = (8, 128)
    row = lax.broadcasted_iota(jnp.int32, shape, 0)
    upper = row < 4
    lane = lax.broadcasted_iota(jnp.int32, (1, 128), 1)

    def load(part, n):
        slot = (part * PART + n) % depth
        return pltpu.make_async_copy(ratio_any[part].at[n], ratio_ref.at[slot], ratio_sems.at[slot])

    def ahead(part, n):
        if n >= PART:
            part, n = part + 1, n - PART
        if part < parts:
            load(part, n).start()

    def block(part, n):
        a = part * PART + n
        load(part, n).wait()
        slot = a % depth
        rights = []
        for k in range(LISTED):
            place = owner_ref[list_ref[k, a]]
            target = (place & 56) * 33 + ((place >> 6) << 3) + (place & 7)
            cx, cy, cz, cw = (comps_ref[a, k, d : d + 1, :] for d in (0, 1, 2, 6))
            pull = (ENERGY_UNIT * NORM) * adjoint_ref[pl.ds(target, 1), :] * cw
            hi, mid, low = split3(pull * choose(row & 3, (cx, cy, cz, 1.0), shape))
            rights.append(
                jnp.concatenate([jnp.where(upper, hi, mid), jnp.where(upper, low, 0.0)], axis=0).astype(jnp.bfloat16)
            )
        total = jnp.zeros((128, 16), jnp.float32)
        dims = (((1,), (1,)), ((), ()))
        for k in range(0, LISTED, 2):
            right = jnp.concatenate(rights[k : k + 2], axis=1)
            ratio = ratio_ref[slot, :, k * 128 : (k + 2) * 128]
            hi = ratio.astype(jnp.bfloat16)
            low = (ratio - hi.astype(jnp.float32)).astype(jnp.bfloat16)
            total += lax.dot_general(hi, right, dims, preferred_element_type=jnp.float32)
            total += lax.dot_general(low, right, dims, preferred_element_type=jnp.float32)
        turned = total.T
        got = turned[0:8] + turned[8:16]
        got = got[0:4] + got[4:8]
        weight = jnp.where(lane < live_ref[a], weight_ref[pl.ds(a, 1), :], 0.0)
        for d in range(3):
            at = pl.ds(d * BLK_DEV + a, 1)
            force_ref[at, :] = weight * (coords_ref[at, :] * got[3:4] - got[d : d + 1])

    for n in range(depth - 1):
        ahead(0, n)
    for part in range(parts):
        def step(n, _, part=part):
            @pl.when(n + depth - 1 < PART)
            def _():
                load(part, n + depth - 1).start()

            if part + 1 < parts:
                @pl.when(n + depth - 1 >= PART)
                def _():
                    load(part + 1, n + depth - 1 - PART).start()

            block(part, n)
            return 0

        lax.fori_loop(0, PART, step, 0)


SMEM_SPEC = pl.BlockSpec(memory_space=pltpu.SMEM)
VMEM_SPEC = pl.BlockSpec(memory_space=pltpu.VMEM)
HBM_SPEC = pl.BlockSpec(memory_space=pltpu.HBM)


def call_overlap(*arrays):
    f32 = jnp.float32
    vmem, hbm = VMEM_SPEC, HBM_SPEC
    return pl.pallas_call(
        overlap_kernel,
        out_shape=(
            jax.ShapeDtypeStruct((COMP_BLOCKS, COMP_BLK), f32),
            jax.ShapeDtypeStruct((BLK_DEV, LISTED, 8, COMP_BLK), f32),
            jax.ShapeDtypeStruct((BLK_DEV, FEATS + 8, ATOM_BLK), f32),
        ),
        in_specs=[hbm] * 9,
        out_specs=(vmem,) * 3,
        scratch_shapes=[
            pltpu.SMEM((BLK_DEV,), jnp.int32),
            pltpu.SMEM((LISTED, BLK_DEV), jnp.int32),
            pltpu.SMEM((COMP_BLOCKS,), jnp.int32),
            pltpu.VMEM((3 * BLK_DEV, ATOM_BLK), f32),
            pltpu.VMEM((BLK_DEV, ATOM_BLK), f32),
            pltpu.VMEM((BLK_DEV, ATOM_BLK), f32),
            pltpu.VMEM((3, COMP_BLOCKS * COMP_BLK), f32),
            pltpu.VMEM((COMP_BLOCKS, COMP_BLK), f32),
            pltpu.VMEM((COMP_BLOCKS, COMP_BLK), f32),
            pltpu.SemaphoreType.DMA((9,)),
        ],
        compiler_params=pltpu.CompilerParams(vmem_limit_bytes=20 << 20),
        name="overlap",
    )(*(in_hbm(v) for v in arrays))


def call_ratio(atoms, comps, part):
    f32 = jnp.float32
    specs = [
        pl.BlockSpec((PART,) + a.shape[1:], lambda i, n=a.ndim: (part,) + (0,) * (n - 1)) for a in (atoms, comps)
    ]
    return pl.pallas_call(
        ratio_kernel,
        grid=(1,),
        out_shape=pltpu.HBM((PART, ATOM_BLK, LISTED * COMP_BLK), f32),
        in_specs=specs,
        out_specs=HBM_SPEC,
        scratch_shapes=[
            pltpu.VMEM((2, ATOM_BLK, LISTED * COMP_BLK), f32),
            pltpu.SemaphoreType.DMA((2,)),
        ],
        compiler_params=pltpu.CompilerParams(vmem_limit_bytes=12 << 20),
        cost_estimate=pl.CostEstimate(flops=PART << 24, bytes_accessed=PART << 20, transcendentals=PART << 19),
        name="ratio",
    )(atoms, comps)


def call_force(*arrays):
    f32 = jnp.float32
    smem, vmem, hbm = SMEM_SPEC, VMEM_SPEC, HBM_SPEC
    *arrays, ratios = arrays
    return pl.pallas_call(
        force_kernel,
        out_shape=jax.ShapeDtypeStruct((3 * BLK_DEV, ATOM_BLK), f32),
        in_specs=[smem] * 3 + [vmem] * 4 + [hbm] * len(ratios),
        out_specs=vmem,
        scratch_shapes=[
            pltpu.VMEM((4, ATOM_BLK, LISTED * COMP_BLK), f32),
            pltpu.SemaphoreType.DMA((4,)),
        ],
        compiler_params=pltpu.CompilerParams(vmem_limit_bytes=16 << 20),
        name="force",
    )(*arrays, *(in_hbm(ratio) for ratio in ratios))


def shards(
    coords, atom_var, atom_weight, atoms_live, block_list, owner_map, comp_means, comp_var, comp_weight, target, noise_sigma,
):
    replicas = lax.axis_size("rep")
    domains = lax.axis_size("dom")
    share = COMP_BLOCKS // domains // replicas
    vmem = VMEM_SPEC
    small = pltpu.CompilerParams(vmem_limit_bytes=6 << 20)
    f32 = jnp.float32
    positions = coords.reshape(3 * BLK_DEV, ATOM_BLK)
    listed = block_list.T
    variances = atom_var.reshape(BLK_DEV, ATOM_BLK)
    weights = atom_weight.reshape(BLK_DEV, ATOM_BLK)
    cvar = comp_var.reshape(COMP_BLOCKS, COMP_BLK)
    cweight = comp_weight.reshape(COMP_BLOCKS, COMP_BLK)
    model, comps, atoms = call_overlap(
        atoms_live, listed, owner_map, positions, variances, weights, comp_means, cvar, cweight
    )
    tie = lax.optimization_barrier
    ratios = [call_ratio(atoms, comps, 0)]
    parts = lax.all_to_all(model.reshape(replicas, domains * share, COMP_BLK), "rep", 0, 0, tiled=True)
    parts, ratios[0] = tie((parts, ratios[0]))
    over_rep = pl.pallas_call(
        rep_sum_kernel,
        out_shape=jax.ShapeDtypeStruct((domains * share, COMP_BLK), f32),
        in_specs=[vmem], out_specs=vmem, compiler_params=small, name="rep_sum",
    )(parts)
    over_rep, atoms = tie((over_rep, atoms))
    ratios.append(call_ratio(atoms, comps, 1))
    parts = lax.all_to_all(over_rep.reshape(domains, share, COMP_BLK), "dom", 0, 0, tiled=True)
    parts, ratios[1] = tie((parts, ratios[1]))
    spread, mean = pl.pallas_call(
        adjoint_kernel,
        out_shape=(
            jax.ShapeDtypeStruct((domains, share, COMP_BLK), f32), jax.ShapeDtypeStruct((share, COMP_BLK), f32),
        ),
        in_specs=[vmem] * 3, out_specs=(vmem, vmem), compiler_params=small, name="adjoint",
    )(parts, target.reshape(-1, COMP_BLK), noise_sigma.reshape(-1, COMP_BLK))
    spread, atoms = tie((spread, atoms))
    ratios.append(call_ratio(atoms, comps, 2))
    over_dom = lax.all_to_all(spread, "dom", 0, 0, tiled=True).reshape(domains * share, COMP_BLK)
    over_dom, ratios[2] = tie((over_dom, ratios[2]))
    spread = pl.pallas_call(
        spread_kernel,
        out_shape=jax.ShapeDtypeStruct((replicas, (domains + 1) * share, COMP_BLK), f32),
        in_specs=[vmem] * 2, out_specs=vmem, compiler_params=small, name="spread",
    )(over_dom, mean)
    spread, atoms = tie((spread, atoms))
    ratios.append(call_ratio(atoms, comps, 3))
    returned = lax.all_to_all(spread, "rep", 0, 0, tiled=True)
    average = returned[:, domains * share :].reshape(-1)
    returned = returned.reshape(-1, COMP_BLK)

    forces = call_force(atoms_live, listed, owner_map, positions, weights, comps, returned, ratios)
    return average, forces.reshape(coords.shape)


def solution(mesh):
    return jax.shard_map(
        shards,
        mesh=mesh,
        in_specs=(
            P("rep", None, "dom"), P("dom"), P("dom"), P("dom"), P("dom", None), P(), P(), P(), P(), P("dom"), P("dom"),
        ),
        out_specs=(P("dom"), P("rep", None, "dom")),
        check_vma=False,
    )
```

time: 127 us -> 125 us (0.984)
  blocking collectives: 76 us -> 0 us
  starting transfers between devices: 0 us -> 30.6 us
  waiting for transfers between devices: 0 us -> 23.7 us
  Pallas kernels: 49.1 us -> 66.2 us
  local copies, waits for them, and re-layouts: 0.67 us -> 3.36 us
    all_to_all x4 -> x0, blocking collectives: 76 us -> none  [the longest x1 22.1 us: shards(): returned = lax.all_to_all(spread, 'rep', 0, 0, tiled=True)]
    all_to_all x0 -> x4, starting transfers between devices: none -> 30.6 us  [the longest x1 9.62 us: shards(): lax.all_to_all(over_rep.reshape(domains, share, COMP_BLK), 'dom', 0, 0, t...]
    all_to_all x0 -> x4, waiting for transfers between devices: none -> 23.7 us  [the longest x1 9.18 us: shards(): returned = lax.all_to_all(spread, 'rep', 0, 0, tiled=True)]
    pallas_call x2 -> x6, Pallas kernels: 48.9 us -> 63.5 us  [the longest x4 25.3 us: call_ratio(): pl.pallas_call(ratio_kernel, grid=(1,), out_shape=pltpu.HBM((PART, ATOM_B...]
    unnamed x18, local copies, waits for them, and re-layouts: 0.05 us -> 1.99 us
    pallas_call x1, Pallas kernels: 0.05 us -> 1.94 us  [shards(): pl.pallas_call(rep_sum_kernel, out_shape=jax.ShapeDtypeStruct((domains *...]
  transfers between devices with their start and end apart: 0 -> 4, of which waited for: 0 -> 4; matrix products, arithmetic and copies ran while one was open for 0% -> 0% of each run, Pallas kernels for 0% -> 20%
where the time goes in v3:
time: 125 us
  Pallas kernels  66.2 us (53%)
  starting transfers between devices  30.6 us (24%)
  waiting for transfers between devices  23.7 us (19%)
  local copies, waits for them, and re-layouts  3.36 us (3%)
    pallas_call x4, Pallas kernels, call_ratio(): pl.pallas_call(ratio_kernel, grid=(1,), out_shape=pltpu.HBM((PART, ATOM_B...  25.3 us
    pallas_call x1, Pallas kernels, call_overlap(): pl.pallas_call(overlap_kernel, out_shape=(jax.ShapeDtypeStruct((COMP_BLOC...  19.6 us
    pallas_call x1, Pallas kernels, call_force(): pl.pallas_call(force_kernel, out_shape=jax.ShapeDtypeStruct((3 * BLK_DEV,...  18.6 us
    all_to_all x1, starting transfers between devices, shards(): lax.all_to_all(over_rep.reshape(domains, share, COMP_BLK), 'dom', 0, 0, t...  9.62 us
    all_to_all x1, waiting for transfers between devices, shards(): returned = lax.all_to_all(spread, 'rep', 0, 0, tiled=True)  9.18 us
    all_to_all x1, waiting for transfers between devices, shards(): lax.all_to_all(model.reshape(replicas, domains * share, COMP_BLK), 'rep',...  8.89 us
    all_to_all x1, starting transfers between devices, shards(): lax.all_to_all(model.reshape(replicas, domains * share, COMP_BLK), 'rep',...  7.36 us
    all_to_all x1, starting transfers between devices, shards(): returned = lax.all_to_all(spread, 'rep', 0, 0, tiled=True)  7.1 us
  transfers between devices with their start and end apart: 4, of which 4 were waited for; matrix products, arithmetic and copies ran while one was open for 0% of the time, Pallas kernels for 20%

profile of v3, /device:TPU:1, one launch (start us, length us, event | category | flops | bytes accessed | tf_op | source)
XLA Modules:
  0.0 124.6 jit_solution(3460277909428860179)
XLA Ops:
  0.6 19.6 %overlap.1 = (f32[2048,128]{1,0:T(8,128)S(1)}, f32[32,16,8,128]{3,2,1,0:T(8,128)S(1)}, f32[32,56,128]{2,1,0:T(8,128)S(1)}) custom-call(s32[32]{0:T(128)} %live_ref.1, s32[16,32]{1,0:T(8,128)} %bitcast.23, s32[2048]{0:T(1024)} %owner_ref.1, f32[96,128]{1,0:T(8,128)} %bitcast.17, f32[32,128]{1,0:T(8,128)} %bitcast.28, f32[32,128]{1,0:T(8,128)} %bitcast.19, ...), custom_call_target="tpu_custom_call" | custom-call | tf_op jit(solution)/shard_map/overlap/pallas_call | solution.py:242
  20.2 0.0 copy-start.1
  20.2 1.0 copy-done.1
  21.2 7.4 %all-to-all-start = ((f32[8,256,128]{2,1,0:T(8,128)}), f32[8,256,128]{2,1,0:T(8,128)}, u32[]{:S(2)}, u32[]{:S(2)}) async-start(f32[8,256,128]{2,1,0:T(8,128)} %bitcast.15), calls=%async_computation | async-start | bytes 2097152 | tf_op jit(solution)/shard_map/all_to_all | solution.py:327
  28.5 6.3 %ratio.4.refs_0_ = f32[8,128,2048]{2,1,0:T(8,128)} custom-call(f32[32,56,128]{2,1,0:T(8,128)S(1)} %get-tuple-element.35.atoms_ref, f32[32,16,8,128]{3,2,1,0:T(8,128)S(1)} %get-tuple-element.21.comps_ref), custom_call_target="tpu_custom_call" | custom-call | flops 134217728 | bytes 8388608 | tf_op jit(solution)/shard_map/ratio/pallas_call | solution.py:273
  34.9 8.9 %all-to-all-done.parts_ref = f32[8,256,128]{2,1,0:T(8,128)} async-done(((f32[8,256,128]{2,1,0:T(8,128)}), f32[8,256,128]{2,1,0:T(8,128)}, u32[]{:S(2)}, u32[]{:S(2)}) %all-to-all-start) | async-done | bytes 1048608 | tf_op jit(solution)/shard_map/all_to_all | solution.py:327
  43.8 1.9 %rep_sum.1 = f32[256,128]{1,0:T(8,128)} custom-call(f32[8,256,128]{2,1,0:T(8,128)} %all-to-all-done.parts_ref), custom_call_target="tpu_custom_call" | custom-call | tf_op jit(solution)/shard_map/rep_sum/pallas_call | solution.py:329
  45.7 9.6 %all-to-all-start.1 = ((f32[32,8,128]{2,1,0:T(8,128)}), f32[32,8,128]{2,1,0:T(8,128)S(1)}, u32[]{:S(2)}, u32[]{:S(2)}) async-start(f32[32,8,128]{2,1,0:T(8,128)} %bitcast.7), calls=%async_computation.1 | async-start | bytes 262144 | tf_op jit(solution)/shard_map/all_to_all | solution.py:336
  55.3 0.0 copy-start.4
  55.4 0.0 copy-start.5
  55.4 6.3 %ratio.5.refs_1_ = f32[8,128,2048]{2,1,0:T(8,128)} custom-call(f32[32,56,128]{2,1,0:T(8,128)S(1)} %get-tuple-element.35.atoms_ref, f32[32,16,8,128]{3,2,1,0:T(8,128)S(1)} %get-tuple-element.21.comps_ref), custom_call_target="tpu_custom_call" | custom-call | flops 134217728 | bytes 8388608 | tf_op jit(solution)/shard_map/ratio/pallas_call | solution.py:273
  61.7 2.8 %all-to-all-done.1.parts_ref = f32[32,8,128]{2,1,0:T(8,128)S(1)} async-done(((f32[32,8,128]{2,1,0:T(8,128)}), f32[32,8,128]{2,1,0:T(8,128)S(1)}, u32[]{:S(2)}, u32[]{:S(2)}) %all-to-all-start.1) | async-done | bytes 131104 | tf_op jit(solution)/shard_map/all_to_all | solution.py:336
  64.5 0.0 copy-done.4
  64.5 0.0 copy-done.5
  64.5 0.7 adjoint.1
  65.2 6.5 %all-to-all-start.2 = ((f32[32,8,128]{2,1,0:T(8,128)}), f32[32,8,128]{2,1,0:T(8,128)S(1)}, u32[]{:S(2)}, u32[]{:S(2)}) async-start(f32[32,8,128]{2,1,0:T(8,128)} %get-tuple-element.27), calls=%async_computation.2 | async-start | bytes 262144 | tf_op jit(solution)/shard_map/all_to_all | solution.py:347
  71.7 6.3 %ratio.6.refs_2_ = f32[8,128,2048]{2,1,0:T(8,128)} custom-call(f32[32,56,128]{2,1,0:T(8,128)S(1)} %get-tuple-element.35.atoms_ref, f32[32,16,8,128]{3,2,1,0:T(8,128)S(1)} %get-tuple-element.21.comps_ref), custom_call_target="tpu_custom_call" | custom-call | flops 134217728 | bytes 8388608 | tf_op jit(solution)/shard_map/ratio/pallas_call | solution.py:273
  78.0 2.8 %all-to-all-done.2 = f32[32,8,128]{2,1,0:T(8,128)S(1)} async-done(((f32[32,8,128]{2,1,0:T(8,128)}), f32[32,8,128]{2,1,0:T(8,128)S(1)}, u32[]{:S(2)}, u32[]{:S(2)}) %all-to-all-start.2) | async-done | bytes 131104 | tf_op jit(solution)/shard_map/all_to_all | solution.py:347
  80.8 0.1 spread.1
  80.9 0.0 copy-start
  80.9 1.0 copy-done
  81.9 7.1 %all-to-all-start.3 = ((f32[8,264,128]{2,1,0:T(8,128)}), f32[8,264,128]{2,1,0:T(8,128)}, u32[]{:S(2)}, u32[]{:S(2)}) async-start(f32[8,264,128]{2,1,0:T(8,128)} %copy-done), calls=%async_computation.3 | async-start | bytes 2162688 | tf_op jit(solution)/shard_map/all_to_all | solution.py:356
  89.0 0.0 copy-start.7
  89.0 0.0 copy-start.8
  89.0 6.3 %ratio.7.refs_3_ = f32[8,128,2048]{2,1,0:T(8,128)} custom-call(f32[32,56,128]{2,1,0:T(8,128)S(1)} %get-tuple-element.35.atoms_ref, f32[32,16,8,128]{3,2,1,0:T(8,128)S(1)} %get-tuple-element.21.comps_ref), custom_call_target="tpu_custom_call" | custom-call | flops 134217728 | bytes 8388608 | tf_op jit(solution)/shard_map/ratio/pallas_call | solution.py:273
  95.4 9.2 %all-to-all-done.3 = f32[8,264,128]{2,1,0:T(8,128)} async-done(((f32[8,264,128]{2,1,0:T(8,128)}), f32[8,264,128]{2,1,0:T(8,128)}, u32[]{:S(2)}, u32[]{:S(2)}) %all-to-all-start.3) | async-done | bytes 1081376 | tf_op jit(solution)/shard_map/all_to_all | solution.py:356
  104.6 0.0 copy-done.2
  104.6 0.0 copy-done.3
  104.6 0.0 copy-done.7
  104.6 0.0 copy-done.8
  104.6 18.6 %force.1 = f32[96,128]{1,0:T(8,128)} custom-call(s32[32]{0:T(128)S(1)} %copy-done.8, s32[16,32]{1,0:T(8,128)S(1)} %bitcast.24, s32[2048]{0:T(1024)S(1)} %copy-done.7, f32[96,128]{1,0:T(8,128)S(1)} %bitcast.18, f32[32,128]{1,0:T(8,128)S(1)} %bitcast.20, f32[32,16,8,128]{3,2,1,0:T(8,128)S(1)} %get-tuple-element.21.comps_ref, f32[2112,128]{1,0:T(8,128)} %bitcast.12.adjoint_ref, ...), custom_call_target="tpu_custom_call" | custom-call | tf_op jit(solution)/shard_map/force/pallas_call | solution.py:293
  123.2 1.4 %slice_bitcast_fusion = f32[8192]{0:T(1024)} fusion(f32[8,264,128]{2,1,0:T(8,128)} %all-to-all-done.3), kind=kLoop, calls=%fused_computation | loop fusion | bytes 65536 | tf_op jit(solution)/shard_map/reshape | solution.py:357
  (4 shorter events, 0.0 us)
Async XLA Ops:
  20.2 1.0 copy-start.1
  21.2 22.6 %all-to-all-start = ((f32[8,256,128]{2,1,0:T(8,128)}), f32[8,256,128]{2,1,0:T(8,128)}, u32[]{:S(2)}, u32[]{:S(2)}) async-start(f32[8,256,128]{2,1,0:T(8,128)} %bitcast.15), calls=%async_computation | async-start | bytes 2097152 | tf_op jit(solution)/shard_map/all_to_all | solution.py:327
  45.7 18.8 %all-to-all-start.1 = ((f32[32,8,128]{2,1,0:T(8,128)}), f32[32,8,128]{2,1,0:T(8,128)S(1)}, u32[]{:S(2)}, u32[]{:S(2)}) async-start(f32[32,8,128]{2,1,0:T(8,128)} %bitcast.7), calls=%async_computation.1 | async-start | bytes 262144 | tf_op jit(solution)/shard_map/all_to_all | solution.py:336
  55.3 9.2 %copy-start.4 = (f32[8192]{0:T(1024)S(1)}, f32[8192]{0:T(1024)}, u32[]{:S(2)}) copy-start(f32[8192]{0:T(1024)} %param.20) | copy-start | bytes 98308
  55.4 9.1 %copy-start.5 = (f32[8192]{0:T(1024)S(1)}, f32[8192]{0:T(1024)}, u32[]{:S(2)}) copy-start(f32[8192]{0:T(1024)} %param.21) | copy-start | bytes 98308
  65.2 15.6 %all-to-all-start.2 = ((f32[32,8,128]{2,1,0:T(8,128)}), f32[32,8,128]{2,1,0:T(8,128)S(1)}, u32[]{:S(2)}, u32[]{:S(2)}) async-start(f32[32,8,128]{2,1,0:T(8,128)} %get-tuple-element.27), calls=%async_computation.2 | async-start | bytes 262144 | tf_op jit(solution)/shard_map/all_to_all | solution.py:347
  80.9 1.0 copy-start
  81.9 22.7 %all-to-all-start.3 = ((f32[8,264,128]{2,1,0:T(8,128)}), f32[8,264,128]{2,1,0:T(8,128)}, u32[]{:S(2)}, u32[]{:S(2)}) async-start(f32[8,264,128]{2,1,0:T(8,128)} %copy-done), calls=%async_computation.3 | async-start | bytes 2162688 | tf_op jit(solution)/shard_map/all_to_all | solution.py:356
  89.0 15.6 %copy-start.2 = (f32[1,3,4096]{2,0,1:T(1,128)S(1)}, f32[1,3,4096]{2,0,1:T(1,128)}, u32[]{:S(2)}) copy-start(f32[1,3,4096]{2,0,1:T(1,128)} %param.11) | copy-start | bytes 147460
  89.0 15.6 %copy-start.3 = (f32[4096]{0:T(1024)S(1)}, f32[4096]{0:T(1024)}, u32[]{:S(2)}) copy-start(f32[4096]{0:T(1024)} %param.13) | copy-start | bytes 49156
  89.0 15.6 %copy-start.6 = (s32[32,16]{0,1:T(8,128)S(1)}, s32[32,16]{0,1:T(8,128)}, u32[]{:S(2)}) copy-start(s32[32,16]{0,1:T(8,128)} %param.15) | copy-start | bytes 6148
  89.0 15.6 %copy-start.7 = (s32[2048]{0:T(1024)S(1)}, s32[2048]{0:T(1024)}, u32[]{:S(2)}) copy-start(s32[2048]{0:T(1024)} %owner_ref.1) | copy-start | bytes 24580
  89.0 15.6 %copy-start.8 = (s32[32]{0:T(128)S(1)}, s32[32]{0:T(128)}, u32[]{:S(2)}) copy-start(s32[32]{0:T(128)} %live_ref.1) | copy-start | bytes 388

commit v4 on v3

--- a/solution.py
+++ b/solution.py
@@ -15,6 +15,9 @@
 COMP_BLOCKS = 2048
 REPLICAS = 8
 FEATS = 48
+ROOM = 96
+SHARE = 8
+OWNED = 256
 PART = 8
 
 ENERGY_UNIT = 2.494
@@ -58,8 +61,8 @@
 
 def overlap_kernel(
     live_any, list_any, owner_any, coords_any, var_any, weight_any, means_any, cvar_any, cweight_any,
-    model_ref, comps_ref, atoms_ref,
-    live_ref, list_ref, owner_ref, coords_ref, var_ref, weight_ref, means_ref, cvar_ref, cweight_ref, sems,
+    model_ref, over_ref, rows_ref, slots_ref, counts_ref, comps_ref, atoms_ref,
+    sums_ref, live_ref, list_ref, owner_ref, coords_ref, var_ref, weight_ref, means_ref, cvar_ref, cweight_ref, sems,
 ):
     pairs = (
         (live_any, live_ref), (list_any, list_ref), (owner_any, owner_ref), (coords_any, coords_ref),
@@ -72,7 +75,15 @@
     shape = (8, 128)
     row = lax.broadcasted_iota(jnp.int32, shape, 0)
     lane = lax.broadcasted_iota(jnp.int32, (1, 128), 1)
-    model_ref[...] = jnp.zeros_like(model_ref)
+    sums_ref[...] = jnp.zeros_like(sums_ref)
+    for r in range(REPLICAS + 1):
+        counts_ref[r] = 0
+
+    def unused(n, _):
+        slots_ref[n] = OWNED
+        return 0
+
+    lax.fori_loop(0, REPLICAS * ROOM, unused, 0, unroll=8)
     for copy in copies:
         copy.wait()
 
@@ -102,11 +113,22 @@
         for k, _, t in pair_terms(left, spread_var, comp_of):
             total = jnp.sum(jnp.sum(t * spread_weight, axis=0), axis=0, keepdims=True)
             place = owner_ref[list_ref[k, a]]
-            target = ((place & 56) << 5) + ((place >> 6) << 3) + (place & 7)
-            model_ref[pl.ds(target, 1), :] += NORM * total * comps_ref[a, k, 6:7, :]
+            rank = (place >> 3) & 7
+            owned = ((place >> 6) << 3) + (place & 7)
+            count = counts_ref[rank]
+            counts_ref[rank] = count + 1
+            fits = count < ROOM
+            counts_ref[REPLICAS] = jnp.where(fits, counts_ref[REPLICAS], 1)
+            slots_ref[jnp.where(fits, rank * ROOM + count, REPLICAS * ROOM)] = owned
+            dense = rank * OWNED + owned
+            rows_ref[k, a] = jnp.where(fits, rank * (ROOM + SHARE) + count, REPLICAS * (ROOM + SHARE) + dense)
+            target = jnp.where(fits, rank * ROOM + count, REPLICAS * ROOM + dense)
+            sums_ref[pl.ds(target, 1), :] += NORM * total * comps_ref[a, k, 6:7, :]
         return 0
 
     lax.fori_loop(0, BLK_DEV, block, 0)
+    model_ref[...] = sums_ref[: REPLICAS * ROOM]
+    over_ref[...] = sums_ref[REPLICAS * ROOM :]
 
 
 def ratio_kernel(atoms_ref, comps_ref, ratio_any, ratio_buf, sems):
@@ -138,8 +160,13 @@
     return pltpu.with_memory_space_constraint(array, pltpu.HBM)
 
 
-def rep_sum_kernel(parts_ref, out_ref):
-    out_ref[...] = jnp.sum(parts_ref[...], axis=0)
+def rep_sum_kernel(slots_ref, parts_ref, over_ref, out_ref, sum_ref, dense_ref):
+    sum_ref[...] = jnp.sum(parts_ref[...], axis=0)
+    dense_ref[:OWNED] = over_ref[...]
+    first = lax.axis_index("rep") * ROOM
+    for n in range(ROOM):
+        dense_ref[pl.ds(slots_ref[first + n], 1), :] += sum_ref[n : n + 1, :]
+    out_ref[...] = dense_ref[:OWNED]
 
 
 def adjoint_kernel(parts_ref, target_ref, sigma_ref, spread_ref, mean_ref):
@@ -153,15 +180,17 @@
     spread_ref[...] = jnp.broadcast_to(adjoint[None], spread_ref.shape)
 
 
-def spread_kernel(adjoint_ref, mean_ref, out_ref):
-    rows = adjoint_ref.shape[0]
+def spread_kernel(slots_ref, adjoint_ref, mean_ref, out_ref, rows_ref):
+    first = lax.axis_index("rep") * ROOM
+    for n in range(ROOM):
+        rows_ref[n : n + 1, :] = adjoint_ref[pl.ds(jnp.minimum(slots_ref[first + n], OWNED - 1), 1), :]
+    rows_ref[ROOM:] = mean_ref[...]
     for r in range(REPLICAS):
-        out_ref[r, :rows] = adjoint_ref[...]
-        out_ref[r, rows:] = mean_ref[...]
+        out_ref[r] = rows_ref[...]
 
 
 def force_kernel(
-    live_ref, list_ref, owner_ref, coords_ref, weight_ref, comps_ref, adjoint_ref, *refs,
+    live_ref, rows_ref, coords_ref, weight_ref, comps_ref, adjoint_ref, over_ref, *refs,
 ):
     parts = BLK_DEV // PART
     ratio_any, (force_ref, ratio_ref, ratio_sems) = refs[:parts], refs[parts:]
@@ -187,10 +216,12 @@
         slot = a % depth
         rights = []
         for k in range(LISTED):
-            place = owner_ref[list_ref[k, a]]
-            target = (place & 56) * 33 + ((place >> 6) << 3) + (place & 7)
+            target = rows_ref[k, a]
+            beyond = target - REPLICAS * (ROOM + SHARE)
+            near = adjoint_ref[pl.ds(jnp.minimum(target, REPLICAS * (ROOM + SHARE) - 1), 1), :]
+            far = over_ref[pl.ds(jnp.maximum(beyond, 0), 1), :]
             cx, cy, cz, cw = (comps_ref[a, k, d : d + 1, :] for d in (0, 1, 2, 6))
-            pull = (ENERGY_UNIT * NORM) * adjoint_ref[pl.ds(target, 1), :] * cw
+            pull = (ENERGY_UNIT * NORM) * jnp.where(beyond < 0, near, far) * cw
             hi, mid, low = split3(pull * choose(row & 3, (cx, cy, cz, 1.0), shape))
             rights.append(
                 jnp.concatenate([jnp.where(upper, hi, mid), jnp.where(upper, low, 0.0)], axis=0).astype(jnp.bfloat16)
@@ -242,13 +273,18 @@
     return pl.pallas_call(
         overlap_kernel,
         out_shape=(
+            jax.ShapeDtypeStruct((REPLICAS * ROOM, COMP_BLK), f32),
             jax.ShapeDtypeStruct((COMP_BLOCKS, COMP_BLK), f32),
+            jax.ShapeDtypeStruct((LISTED, BLK_DEV), jnp.int32),
+            jax.ShapeDtypeStruct((REPLICAS * ROOM + 128,), jnp.int32),
+            jax.ShapeDtypeStruct((128,), jnp.int32),
             jax.ShapeDtypeStruct((BLK_DEV, LISTED, 8, COMP_BLK), f32),
             jax.ShapeDtypeStruct((BLK_DEV, FEATS + 8, ATOM_BLK), f32),
         ),
         in_specs=[hbm] * 9,
-        out_specs=(vmem,) * 3,
+        out_specs=(vmem, vmem, SMEM_SPEC, SMEM_SPEC, SMEM_SPEC, vmem, vmem),
         scratch_shapes=[
+            pltpu.VMEM((REPLICAS * ROOM + COMP_BLOCKS, COMP_BLK), f32),
             pltpu.SMEM((BLK_DEV,), jnp.int32),
             pltpu.SMEM((LISTED, BLK_DEV), jnp.int32),
             pltpu.SMEM((COMP_BLOCKS,), jnp.int32),
@@ -293,7 +329,7 @@
     return pl.pallas_call(
         force_kernel,
         out_shape=jax.ShapeDtypeStruct((3 * BLK_DEV, ATOM_BLK), f32),
-        in_specs=[smem] * 3 + [vmem] * 4 + [hbm] * len(ratios),
+        in_specs=[smem] * 2 + [vmem] * 5 + [hbm] * len(ratios),
         out_specs=vmem,
         scratch_shapes=[
             pltpu.VMEM((4, ATOM_BLK, LISTED * COMP_BLK), f32),
@@ -319,18 +355,27 @@
     weights = atom_weight.reshape(BLK_DEV, ATOM_BLK)
     cvar = comp_var.reshape(COMP_BLOCKS, COMP_BLK)
     cweight = comp_weight.reshape(COMP_BLOCKS, COMP_BLK)
-    model, comps, atoms = call_overlap(
+    model, over, rows, slots, counts, comps, atoms = call_overlap(
         atoms_live, listed, owner_map, positions, variances, weights, comp_means, cvar, cweight
     )
+    crowded = counts[REPLICAS] > 0
     tie = lax.optimization_barrier
     ratios = [call_ratio(atoms, comps, 0)]
-    parts = lax.all_to_all(model.reshape(replicas, domains * share, COMP_BLK), "rep", 0, 0, tiled=True)
+    parts = lax.all_to_all(model.reshape(replicas, ROOM, COMP_BLK), "rep", 0, 0, tiled=True)
     parts, ratios[0] = tie((parts, ratios[0]))
+    over_sum = lax.cond(
+        crowded,
+        lambda v: jnp.sum(lax.all_to_all(v.reshape(replicas, OWNED, COMP_BLK), "rep", 0, 0, tiled=True), axis=0),
+        lambda v: jnp.zeros((OWNED, COMP_BLK), f32),
+        over,
+    )
     over_rep = pl.pallas_call(
         rep_sum_kernel,
-        out_shape=jax.ShapeDtypeStruct((domains * share, COMP_BLK), f32),
-        in_specs=[vmem], out_specs=vmem, compiler_params=small, name="rep_sum",
-    )(parts)
+        out_shape=jax.ShapeDtypeStruct((OWNED, COMP_BLK), f32),
+        in_specs=[SMEM_SPEC, vmem, vmem], out_specs=vmem,
+        scratch_shapes=[pltpu.VMEM((ROOM, COMP_BLK), f32), pltpu.VMEM((OWNED + 8, COMP_BLK), f32)],
+        compiler_params=small, name="rep_sum",
+    )(slots, parts, over_sum)
     over_rep, atoms = tie((over_rep, atoms))
     ratios.append(call_ratio(atoms, comps, 1))
     parts = lax.all_to_all(over_rep.reshape(domains, share, COMP_BLK), "dom", 0, 0, tiled=True)
@@ -346,18 +391,26 @@
     ratios.append(call_ratio(atoms, comps, 2))
     over_dom = lax.all_to_all(spread, "dom", 0, 0, tiled=True).reshape(domains * share, COMP_BLK)
     over_dom, ratios[2] = tie((over_dom, ratios[2]))
+    over_back = lax.cond(
+        crowded,
+        lambda v: lax.all_to_all(jnp.broadcast_to(v[None], (replicas, OWNED, COMP_BLK)), "rep", 0, 0, tiled=True),
+        lambda v: jnp.zeros((replicas, OWNED, COMP_BLK), f32),
+        over_dom,
+    ).reshape(-1, COMP_BLK)
     spread = pl.pallas_call(
         spread_kernel,
-        out_shape=jax.ShapeDtypeStruct((replicas, (domains + 1) * share, COMP_BLK), f32),
-        in_specs=[vmem] * 2, out_specs=vmem, compiler_params=small, name="spread",
-    )(over_dom, mean)
+        out_shape=jax.ShapeDtypeStruct((replicas, ROOM + share, COMP_BLK), f32),
+        in_specs=[SMEM_SPEC, vmem, vmem], out_specs=vmem,
+        scratch_shapes=[pltpu.VMEM((ROOM + share, COMP_BLK), f32)],
+        compiler_params=small, name="spread",
+    )(slots, over_dom, mean)
     spread, atoms = tie((spread, atoms))
     ratios.append(call_ratio(atoms, comps, 3))
     returned = lax.all_to_all(spread, "rep", 0, 0, tiled=True)
-    average = returned[:, domains * share :].reshape(-1)
+    average = returned[:, ROOM:].reshape(-1)
     returned = returned.reshape(-1, COMP_BLK)
 
-    forces = call_force(atoms_live, listed, owner_map, positions, weights, comps, returned, ratios)
+    forces = call_force(atoms_live, rows, positions, weights, comps, returned, over_back, ratios)
     return average, forces.reshape(coords.shape)
 
 

time: 125 us -> 115 us (0.920)
  waiting for transfers between devices: 23.7 us -> 9.44 us
  Pallas kernels: 66.2 us -> 69.3 us
    all_to_all x1, waiting for transfers between devices: 8.89 us -> 1.71 us  [shards(): lax.all_to_all(model.reshape(replicas, ROOM, COMP_BLK), 'rep', 0, 0, tile...]
    all_to_all x1, waiting for transfers between devices: 9.18 us -> 2.06 us  [shards(): returned = lax.all_to_all(spread, 'rep', 0, 0, tiled=True)]
    pallas_call x3, Pallas kernels: 21.6 us -> 24.2 us  [the longest x1 21.5 us: call_overlap(): pl.pallas_call(overlap_kernel, out_shape=(jax.ShapeDtypeStruct((REPLICAS...]
  transfers between devices with their start and end apart: 4 -> 4, of which waited for: 4 -> 4; matrix products, arithmetic and copies ran while one was open for 0% -> 0% of each run, Pallas kernels for 20% -> 22%
where the time goes in v4:
time: 115 us; the launch traced here: 114 us
  Pallas kernels  69.3 us (60%)
  starting transfers between devices  29.7 us (26%)
  waiting for transfers between devices  9.44 us (8%)
  local copies, waits for them, and re-layouts  4.49 us (4%)
  between operations  1.41 us (1%)
    pallas_call x4, Pallas kernels, call_ratio(): pl.pallas_call(ratio_kernel, grid=(1,), out_shape=pltpu.HBM((PART, ATOM_B...  25.5 us
    pallas_call x1, Pallas kernels, call_overlap(): pl.pallas_call(overlap_kernel, out_shape=(jax.ShapeDtypeStruct((REPLICAS...  21.5 us
    pallas_call x1, Pallas kernels, call_force(): pl.pallas_call(force_kernel, out_shape=jax.ShapeDtypeStruct((3 * BLK_DEV,...  18.9 us
    all_to_all x1, starting transfers between devices, shards(): lax.all_to_all(over_rep.reshape(domains, share, COMP_BLK), 'dom', 0, 0, t...  10.4 us
    all_to_all x1, starting transfers between devices, shards(): lax.all_to_all(model.reshape(replicas, ROOM, COMP_BLK), 'rep', 0, 0, tile...  6.59 us
    all_to_all x1, starting transfers between devices, shards(): lax.all_to_all(spread, 'dom', 0, 0, tiled=True)  6.44 us
    all_to_all x1, starting transfers between devices, shards(): returned = lax.all_to_all(spread, 'rep', 0, 0, tiled=True)  6.32 us
    all_to_all x1, waiting for transfers between devices, shards(): lax.all_to_all(spread, 'dom', 0, 0, tiled=True)  2.84 us
  transfers between devices with their start and end apart: 4, of which 4 were waited for; matrix products, arithmetic and copies ran while one was open for 0% of the time, Pallas kernels for 22%

profile of v4, /device:TPU:1, one launch (start us, length us, event | category | flops | bytes accessed | tf_op | source)
XLA Modules:
  0.0 114.3 jit_solution(3608784062259278595)
XLA Ops:
  0.6 21.5 %overlap.1 = (f32[768,128]{1,0:T(8,128)S(1)}, f32[2048,128]{1,0:T(8,128)}, s32[16,32]{1,0:T(8,128)S(1)}, s32[896]{0:T(1024)S(1)}, s32[128]{0:T(128)S(1)}, /*inde...) custom-call(s32[32]{0:T(128)} %live_ref.1, s32[16,32]{1,0:T(8,128)} %bitcast.34, s32[2048]{0:T(1024)} %owner_any.1, ...), custom_call_target="tpu_custom_call" | custom-call | tf_op jit(solution)/shard_map/overlap/pallas_call | solution.py:273
  22.2 0.0 copy-start.1
  22.2 0.8 copy-done.1
  22.9 0.6 slice.6
  24.2 0.0 copy-start.7
  24.2 0.6 copy-done.7
  24.9 6.6 %all-to-all-start.2 = ((f32[8,96,128]{2,1,0:T(8,128)}), f32[8,96,128]{2,1,0:T(8,128)S(1)}, u32[]{:S(2)}, u32[]{:S(2)}) async-start(f32[8,96,128]{2,1,0:T(8,128)} %bitcast.19), calls=%async_computation.2 | async-start | bytes 786432 | tf_op jit(solution)/shard_map/all_to_all | solution.py:364
  31.5 6.4 %ratio.4.refs_0_ = f32[8,128,2048]{2,1,0:T(8,128)} custom-call(f32[32,56,128]{2,1,0:T(8,128)S(1)} %get-tuple-element.52.atoms_ref, f32[32,16,8,128]{3,2,1,0:T(8,128)S(1)} %get-tuple-element.35.comps_ref), custom_call_target="tpu_custom_call" | custom-call | flops 134217728 | bytes 8388608 | tf_op jit(solution)/shard_map/ratio/pallas_call | solution.py:309
  37.8 0.0 copy-start.4
  37.8 0.0 copy-start.5
  37.8 1.7 %all-to-all-done.2.parts_ref = f32[8,96,128]{2,1,0:T(8,128)S(1)} async-done(((f32[8,96,128]{2,1,0:T(8,128)}), f32[8,96,128]{2,1,0:T(8,128)S(1)}, u32[]{:S(2)}, u32[]{:S(2)}) %all-to-all-start.2) | async-done | bytes 393248 | tf_op jit(solution)/shard_map/all_to_all | solution.py:364
  39.6 2.0 %rep_sum.1 = f32[256,128]{1,0:T(8,128)} custom-call(s32[896]{0:T(1024)S(1)} %get-tuple-element.32.slots_ref, f32[8,96,128]{2,1,0:T(8,128)S(1)} %all-to-all-done.2.parts_ref, f32[256,128]{1,0:T(8,128)} %copy-done.7), custom_call_target="tpu_custom_call" | custom-call | tf_op jit(solution)/shard_map/rep_sum/pallas_call | solution.py:372
  41.5 10.4 %all-to-all-start.3 = ((f32[32,8,128]{2,1,0:T(8,128)}), f32[32,8,128]{2,1,0:T(8,128)S(1)}, u32[]{:S(2)}, u32[]{:S(2)}) async-start(f32[32,8,128]{2,1,0:T(8,128)} %bitcast.10), calls=%async_computation.3 | async-start | bytes 262144 | tf_op jit(solution)/shard_map/all_to_all | solution.py:381
  51.9 6.3 %ratio.5.refs_1_ = f32[8,128,2048]{2,1,0:T(8,128)} custom-call(f32[32,56,128]{2,1,0:T(8,128)S(1)} %get-tuple-element.52.atoms_ref, f32[32,16,8,128]{3,2,1,0:T(8,128)S(1)} %get-tuple-element.35.comps_ref), custom_call_target="tpu_custom_call" | custom-call | flops 134217728 | bytes 8388608 | tf_op jit(solution)/shard_map/ratio/pallas_call | solution.py:309
  58.2 2.8 %all-to-all-done.3.parts_ref = f32[32,8,128]{2,1,0:T(8,128)S(1)} async-done(((f32[32,8,128]{2,1,0:T(8,128)}), f32[32,8,128]{2,1,0:T(8,128)S(1)}, u32[]{:S(2)}, u32[]{:S(2)}) %all-to-all-start.3) | async-done | bytes 131104 | tf_op jit(solution)/shard_map/all_to_all | solution.py:381
  61.1 0.0 copy-done.4
  61.1 0.0 copy-done.5
  61.1 0.7 adjoint.1
  61.8 6.4 %all-to-all-start.4 = ((f32[32,8,128]{2,1,0:T(8,128)}), f32[32,8,128]{2,1,0:T(8,128)S(1)}, u32[]{:S(2)}, u32[]{:S(2)}) async-start(f32[32,8,128]{2,1,0:T(8,128)} %get-tuple-element.43), calls=%async_computation.4 | async-start | bytes 262144 | tf_op jit(solution)/shard_map/all_to_all | solution.py:392
  68.2 6.4 %ratio.6.refs_2_ = f32[8,128,2048]{2,1,0:T(8,128)} custom-call(f32[32,56,128]{2,1,0:T(8,128)S(1)} %get-tuple-element.52.atoms_ref, f32[32,16,8,128]{3,2,1,0:T(8,128)S(1)} %get-tuple-element.35.comps_ref), custom_call_target="tpu_custom_call" | custom-call | flops 134217728 | bytes 8388608 | tf_op jit(solution)/shard_map/ratio/pallas_call | solution.py:309
  74.6 2.8 %all-to-all-done.4 = f32[32,8,128]{2,1,0:T(8,128)S(1)} async-done(((f32[32,8,128]{2,1,0:T(8,128)}), f32[32,8,128]{2,1,0:T(8,128)S(1)}, u32[]{:S(2)}, u32[]{:S(2)}) %all-to-all-start.4) | async-done | bytes 131104 | tf_op jit(solution)/shard_map/all_to_all | solution.py:392
  77.5 0.7 spread.1
  78.2 0.8 copy-done
  79.0 1.1 conditional.3
  79.0 1.0 reshape.41
  80.1 6.3 %all-to-all-start.5 = ((f32[8,104,128]{2,1,0:T(8,128)}), f32[8,104,128]{2,1,0:T(8,128)S(1)}, u32[]{:S(2)}, u32[]{:S(2)}) async-start(f32[8,104,128]{2,1,0:T(8,128)} %copy-done), calls=%async_computation.5 | async-start | bytes 851968 | tf_op jit(solution)/shard_map/all_to_all | solution.py:409
  86.4 6.4 %ratio.7.refs_3_ = f32[8,128,2048]{2,1,0:T(8,128)} custom-call(f32[32,56,128]{2,1,0:T(8,128)S(1)} %get-tuple-element.52.atoms_ref, f32[32,16,8,128]{3,2,1,0:T(8,128)S(1)} %get-tuple-element.35.comps_ref), custom_call_target="tpu_custom_call" | custom-call | flops 134217728 | bytes 8388608 | tf_op jit(solution)/shard_map/ratio/pallas_call | solution.py:309
  92.8 2.1 %all-to-all-done.5 = f32[8,104,128]{2,1,0:T(8,128)S(1)} async-done(((f32[8,104,128]{2,1,0:T(8,128)}), f32[8,104,128]{2,1,0:T(8,128)S(1)}, u32[]{:S(2)}, u32[]{:S(2)}) %all-to-all-start.5) | async-done | bytes 426016 | tf_op jit(solution)/shard_map/all_to_all | solution.py:409
  94.8 0.0 copy-done.2
  94.8 0.0 copy-done.6
  94.9 18.9 %force.1 = f32[96,128]{1,0:T(8,128)} custom-call(s32[32]{0:T(128)S(1)} %copy-done.6, s32[16,32]{1,0:T(8,128)S(1)} %get-tuple-element.48.rows_ref, f32[96,128]{1,0:T(8,128)S(1)} %bitcast.21, f32[32,128]{1,0:T(8,128)S(1)} %bitcast.23, f32[32,16,8,128]{3,2,1,0:T(8,128)S(1)} %get-tuple-element.35.comps_ref, f32[832,128]{1,0:T(8,128)S(1)} %bitcast.18, ...), custom_call_target="tpu_custom_call" | custom-call | tf_op jit(solution)/shard_map/force/pallas_call | solution.py:329
  113.7 0.6 slice_bitcast_fusion
  (7 shorter events, 0.0 us)
Async XLA Ops:
  22.2 0.8 copy-start.1
  24.2 0.7 copy-start.7
  24.9 14.7 %all-to-all-start.2 = ((f32[8,96,128]{2,1,0:T(8,128)}), f32[8,96,128]{2,1,0:T(8,128)S(1)}, u32[]{:S(2)}, u32[]{:S(2)}) async-start(f32[8,96,128]{2,1,0:T(8,128)} %bitcast.19), calls=%async_computation.2 | async-start | bytes 786432 | tf_op jit(solution)/shard_map/all_to_all | solution.py:364
  37.8 23.2 %copy-start.4 = (f32[8192]{0:T(1024)S(1)}, f32[8192]{0:T(1024)}, u32[]{:S(2)}) copy-start(f32[8192]{0:T(1024)} %param.24) | copy-start | bytes 98308
  37.8 23.2 %copy-start.5 = (f32[8192]{0:T(1024)S(1)}, f32[8192]{0:T(1024)}, u32[]{:S(2)}) copy-start(f32[8192]{0:T(1024)} %param.25) | copy-start | bytes 98308
  41.5 19.5 %all-to-all-start.3 = ((f32[32,8,128]{2,1,0:T(8,128)}), f32[32,8,128]{2,1,0:T(8,128)S(1)}, u32[]{:S(2)}, u32[]{:S(2)}) async-start(f32[32,8,128]{2,1,0:T(8,128)} %bitcast.10), calls=%async_computation.3 | async-start | bytes 262144 | tf_op jit(solution)/shard_map/all_to_all | solution.py:381
  61.8 15.7 %all-to-all-start.4 = ((f32[32,8,128]{2,1,0:T(8,128)}), f32[32,8,128]{2,1,0:T(8,128)S(1)}, u32[]{:S(2)}, u32[]{:S(2)}) async-start(f32[32,8,128]{2,1,0:T(8,128)} %get-tuple-element.43), calls=%async_computation.4 | async-start | bytes 262144 | tf_op jit(solution)/shard_map/all_to_all | solution.py:392
  78.2 0.8 copy-start
  79.0 15.8 %copy-start.2 = (f32[1,3,4096]{2,0,1:T(1,128)S(1)}, f32[1,3,4096]{2,0,1:T(1,128)}, u32[]{:S(2)}) copy-start(f32[1,3,4096]{2,0,1:T(1,128)} %param.15) | copy-start | bytes 147460
  79.0 15.8 %copy-start.3 = (f32[4096]{0:T(1024)S(1)}, f32[4096]{0:T(1024)}, u32[]{:S(2)}) copy-start(f32[4096]{0:T(1024)} %param.17) | copy-start | bytes 49156
  79.0 15.8 %copy-start.6 = (s32[32]{0:T(128)S(1)}, s32[32]{0:T(128)}, u32[]{:S(2)}) copy-start(s32[32]{0:T(128)} %live_ref.1) | copy-start | bytes 388
  80.1 14.8 %all-to-all-start.5 = ((f32[8,104,128]{2,1,0:T(8,128)}), f32[8,104,128]{2,1,0:T(8,128)S(1)}, u32[]{:S(2)}, u32[]{:S(2)}) async-start(f32[8,104,128]{2,1,0:T(8,128)} %copy-done), calls=%async_computation.5 | async-start | bytes 851968 | tf_op jit(solution)/shard_map/all_to_all | solution.py:409

commit v5 on v4

--- a/solution.py
+++ b/solution.py
@@ -142,12 +142,23 @@
         def _():
             store(a - 2).wait()
 
-        atoms = atoms_ref[a].T
-        left = atoms[:, :FEATS].astype(jnp.bfloat16)
-        spread_var = spread_lanes(atoms, FEATS)
         slot = a & 1
-        for k, q, t in pair_terms(left, spread_var, lambda k: comps_ref[a, k]):
-            ratio_buf[slot, :, k * 128 : (k + 1) * 128] = (t * q).reshape(128, 128)
+        row = lax.broadcasted_iota(jnp.int32, (8, 128), 0)
+        own = jnp.where(row == 5, 1.0, 0.0)
+        var = jnp.where(row == 4, jnp.broadcast_to(atoms_ref[a, FEATS : FEATS + 1, :], (8, 128)), 0.0)
+        hi, mid, low = split3(var)
+        sums = jnp.concatenate([hi + own, mid, low, own, jnp.zeros_like(own), own], axis=0)
+        right = jnp.concatenate([atoms_ref[a, :FEATS, :], sums], axis=1).astype(jnp.bfloat16)
+        for k in range(LISTED):
+            left = right_side(comps_ref[a, k]).T
+            both = jnp.dot(left, right, preferred_element_type=jnp.float32).reshape(16, 8, 256)
+            r = lax.rsqrt(both[:, :, 128:])
+            q = r * r
+            ratio = ((q * q) * (r * jnp.exp2(both[:, :, :128] * q))).reshape(128, 128)
+            hi = ratio.astype(jnp.bfloat16)
+            rows = slice(k * 128, (k + 1) * 128)
+            ratio_buf[slot, rows, :128] = hi
+            ratio_buf[slot, rows, 128:] = (ratio - hi.astype(jnp.float32)).astype(jnp.bfloat16)
         store(a).start()
         return 0
 
@@ -226,17 +237,12 @@
             rights.append(
                 jnp.concatenate([jnp.where(upper, hi, mid), jnp.where(upper, low, 0.0)], axis=0).astype(jnp.bfloat16)
             )
-        total = jnp.zeros((128, 16), jnp.float32)
-        dims = (((1,), (1,)), ((), ()))
+        total = jnp.zeros((16, 256), jnp.float32)
         for k in range(0, LISTED, 2):
-            right = jnp.concatenate(rights[k : k + 2], axis=1)
-            ratio = ratio_ref[slot, :, k * 128 : (k + 2) * 128]
-            hi = ratio.astype(jnp.bfloat16)
-            low = (ratio - hi.astype(jnp.float32)).astype(jnp.bfloat16)
-            total += lax.dot_general(hi, right, dims, preferred_element_type=jnp.float32)
-            total += lax.dot_general(low, right, dims, preferred_element_type=jnp.float32)
-        turned = total.T
-        got = turned[0:8] + turned[8:16]
+            pulls = jnp.concatenate(rights[k : k + 2], axis=1)
+            total += jnp.dot(pulls, ratio_ref[slot, k * 128 : (k + 2) * 128, :], preferred_element_type=jnp.float32)
+        got = total[:, :128] + total[:, 128:]
+        got = got[0:8] + got[8:16]
         got = got[0:4] + got[4:8]
         weight = jnp.where(lane < live_ref[a], weight_ref[pl.ds(a, 1), :], 0.0)
         for d in range(3):
@@ -309,11 +315,11 @@
     return pl.pallas_call(
         ratio_kernel,
         grid=(1,),
-        out_shape=pltpu.HBM((PART, ATOM_BLK, LISTED * COMP_BLK), f32),
+        out_shape=pltpu.HBM((PART, LISTED * COMP_BLK, 2 * ATOM_BLK), jnp.bfloat16),
         in_specs=specs,
         out_specs=HBM_SPEC,
         scratch_shapes=[
-            pltpu.VMEM((2, ATOM_BLK, LISTED * COMP_BLK), f32),
+            pltpu.VMEM((2, LISTED * COMP_BLK, 2 * ATOM_BLK), jnp.bfloat16),
             pltpu.SemaphoreType.DMA((2,)),
         ],
         compiler_params=pltpu.CompilerParams(vmem_limit_bytes=12 << 20),
@@ -332,7 +338,7 @@
         in_specs=[smem] * 2 + [vmem] * 5 + [hbm] * len(ratios),
         out_specs=vmem,
         scratch_shapes=[
-            pltpu.VMEM((4, ATOM_BLK, LISTED * COMP_BLK), f32),
+            pltpu.VMEM((4, LISTED * COMP_BLK, 2 * ATOM_BLK), jnp.bfloat16),
             pltpu.SemaphoreType.DMA((4,)),
         ],
         compiler_params=pltpu.CompilerParams(vmem_limit_bytes=16 << 20),

time: 115 us -> 113 us (0.983)
  waiting for transfers between devices: 9.44 us -> 4.23 us
  Pallas kernels: 69.3 us -> 71.7 us
  starting transfers between devices: 29.7 us -> 31.1 us
    pallas_call x4, Pallas kernels: 25.5 us -> 30.6 us  [call_ratio(): pl.pallas_call(ratio_kernel, grid=(1,), out_shape=pltpu.HBM((PART, LISTED...]
    pallas_call x1, Pallas kernels: 18.9 us -> 16.2 us  [call_force(): pl.pallas_call(force_kernel, out_shape=jax.ShapeDtypeStruct((3 * BLK_DEV,...]
    all_to_all x1, waiting for transfers between devices: 2.84 us -> 1.51 us  [shards(): lax.all_to_all(spread, 'dom', 0, 0, tiled=True)]
    all_to_all x1, waiting for transfers between devices: 2.83 us -> 1.51 us  [shards(): lax.all_to_all(over_rep.reshape(domains, share, COMP_BLK), 'dom', 0, 0, t...]
    all_to_all x1, starting transfers between devices: 6.44 us -> 7.74 us  [shards(): lax.all_to_all(spread, 'dom', 0, 0, tiled=True)]
    all_to_all x1, waiting for transfers between devices: 2.06 us -> 0.78 us  [shards(): returned = lax.all_to_all(spread, 'rep', 0, 0, tiled=True)]
    all_to_all x1, waiting for transfers between devices: 1.71 us -> 0.43 us  [shards(): lax.all_to_all(model.reshape(replicas, ROOM, COMP_BLK), 'rep', 0, 0, tile...]
  transfers between devices with their start and end apart: 4 -> 4, of which waited for: 4 -> 4; matrix products, arithmetic and copies ran while one was open for 0% -> 0% of each run, Pallas kernels for 22% -> 27%
where the time goes in v5:
time: 113 us
  Pallas kernels  71.7 us (63%)
  starting transfers between devices  31.1 us (28%)
  local copies, waits for them, and re-layouts  4.49 us (4%)
  waiting for transfers between devices  4.23 us (4%)
  between operations  1.41 us (1%)
    pallas_call x4, Pallas kernels, call_ratio(): pl.pallas_call(ratio_kernel, grid=(1,), out_shape=pltpu.HBM((PART, LISTED...  30.6 us
    pallas_call x1, Pallas kernels, call_overlap(): pl.pallas_call(overlap_kernel, out_shape=(jax.ShapeDtypeStruct((REPLICAS...  21.5 us
    pallas_call x1, Pallas kernels, call_force(): pl.pallas_call(force_kernel, out_shape=jax.ShapeDtypeStruct((3 * BLK_DEV,...  16.2 us
    all_to_all x1, starting transfers between devices, shards(): lax.all_to_all(over_rep.reshape(domains, share, COMP_BLK), 'dom', 0, 0, t...  10.4 us
    all_to_all x1, starting transfers between devices, shards(): lax.all_to_all(spread, 'dom', 0, 0, tiled=True)  7.74 us
    all_to_all x1, starting transfers between devices, shards(): lax.all_to_all(model.reshape(replicas, ROOM, COMP_BLK), 'rep', 0, 0, tile...  6.59 us
    all_to_all x1, starting transfers between devices, shards(): returned = lax.all_to_all(spread, 'rep', 0, 0, tiled=True)  6.32 us
  transfers between devices with their start and end apart: 4, of which 4 were waited for; matrix products, arithmetic and copies ran while one was open for 0% of the time, Pallas kernels for 27%

profile of v5, /device:TPU:1, one launch (start us, length us, event | category | flops | bytes accessed | tf_op | source)
XLA Modules:
  0.0 112.9 jit_solution(11331929506119967432)
XLA Ops:
  0.6 21.5 %overlap.1 = (f32[768,128]{1,0:T(8,128)S(1)}, f32[2048,128]{1,0:T(8,128)}, s32[16,32]{1,0:T(8,128)S(1)}, s32[896]{0:T(1024)S(1)}, s32[128]{0:T(128)S(1)}, /*inde...) custom-call(s32[32]{0:T(128)} %live_ref.1, s32[16,32]{1,0:T(8,128)} %bitcast.34, s32[2048]{0:T(1024)} %owner_any.1, ...), custom_call_target="tpu_custom_call" | custom-call | tf_op jit(solution)/shard_map/overlap/pallas_call | solution.py:279
  22.2 0.0 copy-start.1
  22.2 0.8 copy-done.1
  22.9 0.6 slice.6
  24.2 0.0 copy-start.7
  24.2 0.6 copy-done.7
  24.9 6.6 %all-to-all-start.2 = ((f32[8,96,128]{2,1,0:T(8,128)}), f32[8,96,128]{2,1,0:T(8,128)S(1)}, u32[]{:S(2)}, u32[]{:S(2)}) async-start(f32[8,96,128]{2,1,0:T(8,128)} %bitcast.19), calls=%async_computation.2 | async-start | bytes 786432 | tf_op jit(solution)/shard_map/all_to_all | solution.py:370
  31.5 7.6 %ratio.4.refs_0_ = bf16[8,2048,256]{2,1,0:T(8,128)(2,1)} custom-call(f32[32,56,128]{2,1,0:T(8,128)S(1)} %get-tuple-element.52.atoms_ref, f32[32,16,8,128]{3,2,1,0:T(8,128)S(1)} %get-tuple-element.35.comps_ref), custom_call_target="tpu_custom_call" | custom-call | flops 134217728 | bytes 8388608 | tf_op jit(solution)/shard_map/ratio/pallas_call | solution.py:315
  39.1 0.0 copy-start.4
  39.1 0.0 copy-start.5
  39.1 0.4 all-to-all-done.2.parts_ref
  39.6 2.0 %rep_sum.1 = f32[256,128]{1,0:T(8,128)} custom-call(s32[896]{0:T(1024)S(1)} %get-tuple-element.32.slots_ref, f32[8,96,128]{2,1,0:T(8,128)S(1)} %all-to-all-done.2.parts_ref, f32[256,128]{1,0:T(8,128)} %copy-done.7), custom_call_target="tpu_custom_call" | custom-call | tf_op jit(solution)/shard_map/rep_sum/pallas_call | solution.py:378
  41.5 10.4 %all-to-all-start.3 = ((f32[32,8,128]{2,1,0:T(8,128)}), f32[32,8,128]{2,1,0:T(8,128)S(1)}, u32[]{:S(2)}, u32[]{:S(2)}) async-start(f32[32,8,128]{2,1,0:T(8,128)} %bitcast.10), calls=%async_computation.3 | async-start | bytes 262144 | tf_op jit(solution)/shard_map/all_to_all | solution.py:387
  51.9 7.6 %ratio.5.refs_1_ = bf16[8,2048,256]{2,1,0:T(8,128)(2,1)} custom-call(f32[32,56,128]{2,1,0:T(8,128)S(1)} %get-tuple-element.52.atoms_ref, f32[32,16,8,128]{3,2,1,0:T(8,128)S(1)} %get-tuple-element.35.comps_ref), custom_call_target="tpu_custom_call" | custom-call | flops 134217728 | bytes 8388608 | tf_op jit(solution)/shard_map/ratio/pallas_call | solution.py:315
  59.6 1.5 %all-to-all-done.3.parts_ref = f32[32,8,128]{2,1,0:T(8,128)S(1)} async-done(((f32[32,8,128]{2,1,0:T(8,128)}), f32[32,8,128]{2,1,0:T(8,128)S(1)}, u32[]{:S(2)}, u32[]{:S(2)}) %all-to-all-start.3) | async-done | bytes 131104 | tf_op jit(solution)/shard_map/all_to_all | solution.py:387
  61.1 0.0 copy-done.4
  61.1 0.0 copy-done.5
  61.1 0.7 adjoint.1
  61.8 7.7 %all-to-all-start.4 = ((f32[32,8,128]{2,1,0:T(8,128)}), f32[32,8,128]{2,1,0:T(8,128)S(1)}, u32[]{:S(2)}, u32[]{:S(2)}) async-start(f32[32,8,128]{2,1,0:T(8,128)} %get-tuple-element.43), calls=%async_computation.4 | async-start | bytes 262144 | tf_op jit(solution)/shard_map/all_to_all | solution.py:398
  69.6 7.6 %ratio.6.refs_2_ = bf16[8,2048,256]{2,1,0:T(8,128)(2,1)} custom-call(f32[32,56,128]{2,1,0:T(8,128)S(1)} %get-tuple-element.52.atoms_ref, f32[32,16,8,128]{3,2,1,0:T(8,128)S(1)} %get-tuple-element.35.comps_ref), custom_call_target="tpu_custom_call" | custom-call | flops 134217728 | bytes 8388608 | tf_op jit(solution)/shard_map/ratio/pallas_call | solution.py:315
  77.2 1.5 %all-to-all-done.4 = f32[32,8,128]{2,1,0:T(8,128)S(1)} async-done(((f32[32,8,128]{2,1,0:T(8,128)}), f32[32,8,128]{2,1,0:T(8,128)S(1)}, u32[]{:S(2)}, u32[]{:S(2)}) %all-to-all-start.4) | async-done | bytes 131104 | tf_op jit(solution)/shard_map/all_to_all | solution.py:398
  78.7 0.7 spread.1
  79.5 0.8 copy-done
  80.3 1.1 conditional.3
  80.3 1.0 reshape.41
  81.3 6.3 %all-to-all-start.5 = ((f32[8,104,128]{2,1,0:T(8,128)}), f32[8,104,128]{2,1,0:T(8,128)S(1)}, u32[]{:S(2)}, u32[]{:S(2)}) async-start(f32[8,104,128]{2,1,0:T(8,128)} %copy-done), calls=%async_computation.5 | async-start | bytes 851968 | tf_op jit(solution)/shard_map/all_to_all | solution.py:415
  87.7 7.6 %ratio.7.refs_3_ = bf16[8,2048,256]{2,1,0:T(8,128)(2,1)} custom-call(f32[32,56,128]{2,1,0:T(8,128)S(1)} %get-tuple-element.52.atoms_ref, f32[32,16,8,128]{3,2,1,0:T(8,128)S(1)} %get-tuple-element.35.comps_ref), custom_call_target="tpu_custom_call" | custom-call | flops 134217728 | bytes 8388608 | tf_op jit(solution)/shard_map/ratio/pallas_call | solution.py:315
  95.3 0.8 all-to-all-done.5
  96.1 0.0 copy-done.2
  96.1 0.0 copy-done.3
  96.1 16.2 %force.1 = f32[96,128]{1,0:T(8,128)} custom-call(s32[32]{0:T(128)S(1)} %copy-done.6, s32[16,32]{1,0:T(8,128)S(1)} %get-tuple-element.48.rows_ref, f32[96,128]{1,0:T(8,128)S(1)} %bitcast.21, f32[32,128]{1,0:T(8,128)S(1)} %bitcast.23, f32[32,16,8,128]{3,2,1,0:T(8,128)S(1)} %get-tuple-element.35.comps_ref, f32[832,128]{1,0:T(8,128)S(1)} %bitcast.18, ...), custom_call_target="tpu_custom_call" | custom-call | tf_op jit(solution)/shard_map/force/pallas_call | solution.py:335
  112.3 0.6 slice_bitcast_fusion
  (7 shorter events, 0.0 us)
Async XLA Ops:
  22.2 0.8 copy-start.1
  24.2 0.7 copy-start.7
  24.9 14.7 %all-to-all-start.2 = ((f32[8,96,128]{2,1,0:T(8,128)}), f32[8,96,128]{2,1,0:T(8,128)S(1)}, u32[]{:S(2)}, u32[]{:S(2)}) async-start(f32[8,96,128]{2,1,0:T(8,128)} %bitcast.19), calls=%async_computation.2 | async-start | bytes 786432 | tf_op jit(solution)/shard_map/all_to_all | solution.py:370
  39.1 22.0 %copy-start.4 = (f32[8192]{0:T(1024)S(1)}, f32[8192]{0:T(1024)}, u32[]{:S(2)}) copy-start(f32[8192]{0:T(1024)} %param.24) | copy-start | bytes 98308
  39.1 22.0 %copy-start.5 = (f32[8192]{0:T(1024)S(1)}, f32[8192]{0:T(1024)}, u32[]{:S(2)}) copy-start(f32[8192]{0:T(1024)} %param.25) | copy-start | bytes 98308
  41.5 19.6 %all-to-all-start.3 = ((f32[32,8,128]{2,1,0:T(8,128)}), f32[32,8,128]{2,1,0:T(8,128)S(1)}, u32[]{:S(2)}, u32[]{:S(2)}) async-start(f32[32,8,128]{2,1,0:T(8,128)} %bitcast.10), calls=%async_computation.3 | async-start | bytes 262144 | tf_op jit(solution)/shard_map/all_to_all | solution.py:387
  61.8 16.9 %all-to-all-start.4 = ((f32[32,8,128]{2,1,0:T(8,128)}), f32[32,8,128]{2,1,0:T(8,128)S(1)}, u32[]{:S(2)}, u32[]{:S(2)}) async-start(f32[32,8,128]{2,1,0:T(8,128)} %get-tuple-element.43), calls=%async_computation.4 | async-start | bytes 262144 | tf_op jit(solution)/shard_map/all_to_all | solution.py:398
  79.5 0.8 copy-start
  80.3 15.8 %copy-start.2 = (f32[1,3,4096]{2,0,1:T(1,128)S(1)}, f32[1,3,4096]{2,0,1:T(1,128)}, u32[]{:S(2)}) copy-start(f32[1,3,4096]{2,0,1:T(1,128)} %param.15) | copy-start | bytes 147460
  80.3 15.8 %copy-start.3 = (f32[4096]{0:T(1024)S(1)}, f32[4096]{0:T(1024)}, u32[]{:S(2)}) copy-start(f32[4096]{0:T(1024)} %param.17) | copy-start | bytes 49156
  80.3 15.8 %copy-start.6 = (s32[32]{0:T(128)S(1)}, s32[32]{0:T(128)}, u32[]{:S(2)}) copy-start(s32[32]{0:T(128)} %live_ref.1) | copy-start | bytes 388
  81.3 14.7 %all-to-all-start.5 = ((f32[8,104,128]{2,1,0:T(8,128)}), f32[8,104,128]{2,1,0:T(8,128)S(1)}, u32[]{:S(2)}, u32[]{:S(2)}) async-start(f32[8,104,128]{2,1,0:T(8,128)} %copy-done), calls=%async_computation.5 | async-start | bytes 851968 | tf_op jit(solution)/shard_map/all_to_all | solution.py:415

commit v6 on v5

--- a/solution.py
+++ b/solution.py
@@ -19,6 +19,7 @@
 SHARE = 8
 OWNED = 256
 PART = 8
+DEPTH = 8
 
 ENERGY_UNIT = 2.494
 EXP_SCALE = -0.5 / math.log(2.0)
@@ -61,8 +62,8 @@
 
 def overlap_kernel(
     live_any, list_any, owner_any, coords_any, var_any, weight_any, means_any, cvar_any, cweight_any,
-    model_ref, over_ref, rows_ref, slots_ref, counts_ref, comps_ref, atoms_ref,
-    sums_ref, live_ref, list_ref, owner_ref, coords_ref, var_ref, weight_ref, means_ref, cvar_ref, cweight_ref, sems,
+    model_ref, over_ref, rows_ref, slots_ref, flag_ref, comps_ref, atoms_ref,
+    counts_ref, sums_ref, live_ref, list_ref, owner_ref, coords_ref, var_ref, weight_ref, means_ref, cvar_ref, cweight_ref, sems,
 ):
     pairs = (
         (live_any, live_ref), (list_any, list_ref), (owner_any, owner_ref), (coords_any, coords_ref),
@@ -127,11 +128,18 @@
         return 0
 
     lax.fori_loop(0, BLK_DEV, block, 0)
-    model_ref[...] = sums_ref[: REPLICAS * ROOM]
-    over_ref[...] = sums_ref[REPLICAS * ROOM :]
-
-
-def ratio_kernel(atoms_ref, comps_ref, ratio_any, ratio_buf, sems):
+    flag_ref[0] = counts_ref[REPLICAS]
+    copies = [
+        pltpu.make_async_copy(sums_ref.at[pl.ds(0, REPLICAS * ROOM)], model_ref, sems.at[0]),
+        pltpu.make_async_copy(sums_ref.at[pl.ds(REPLICAS * ROOM, COMP_BLOCKS)], over_ref, sems.at[1]),
+    ]
+    for copy in copies:
+        copy.start()
+    for copy in copies:
+        copy.wait()
+
+
+def ratio_kernel(first, atoms_ref, comps_ref, ratio_any, ratio_buf, sems):
     blocks = ratio_any.shape[0]
 
     def store(a):
@@ -145,12 +153,12 @@
         slot = a & 1
         row = lax.broadcasted_iota(jnp.int32, (8, 128), 0)
         own = jnp.where(row == 5, 1.0, 0.0)
-        var = jnp.where(row == 4, jnp.broadcast_to(atoms_ref[a, FEATS : FEATS + 1, :], (8, 128)), 0.0)
+        var = jnp.where(row == 4, jnp.broadcast_to(atoms_ref[first + a, FEATS : FEATS + 1, :], (8, 128)), 0.0)
         hi, mid, low = split3(var)
         sums = jnp.concatenate([hi + own, mid, low, own, jnp.zeros_like(own), own], axis=0)
-        right = jnp.concatenate([atoms_ref[a, :FEATS, :], sums], axis=1).astype(jnp.bfloat16)
+        right = jnp.concatenate([atoms_ref[first + a, :FEATS, :], sums], axis=1).astype(jnp.bfloat16)
         for k in range(LISTED):
-            left = right_side(comps_ref[a, k]).T
+            left = right_side(comps_ref[first + a, k]).T
             both = jnp.dot(left, right, preferred_element_type=jnp.float32).reshape(16, 8, 256)
             r = lax.rsqrt(both[:, :, 128:])
             q = r * r
@@ -191,13 +199,16 @@
     spread_ref[...] = jnp.broadcast_to(adjoint[None], spread_ref.shape)
 
 
-def spread_kernel(slots_ref, adjoint_ref, mean_ref, out_ref, rows_ref):
+def spread_kernel(slots_ref, adjoint_ref, mean_ref, out_ref, rows_ref, sems):
     first = lax.axis_index("rep") * ROOM
     for n in range(ROOM):
         rows_ref[n : n + 1, :] = adjoint_ref[pl.ds(jnp.minimum(slots_ref[first + n], OWNED - 1), 1), :]
     rows_ref[ROOM:] = mean_ref[...]
-    for r in range(REPLICAS):
-        out_ref[r] = rows_ref[...]
+    copies = [pltpu.make_async_copy(rows_ref, out_ref.at[r], sems.at[r]) for r in range(REPLICAS)]
+    for copy in copies:
+        copy.start()
+    for copy in copies:
+        copy.wait()
 
 
 def force_kernel(
@@ -279,17 +290,18 @@
     return pl.pallas_call(
         overlap_kernel,
         out_shape=(
-            jax.ShapeDtypeStruct((REPLICAS * ROOM, COMP_BLK), f32),
-            jax.ShapeDtypeStruct((COMP_BLOCKS, COMP_BLK), f32),
+            pltpu.HBM((REPLICAS * ROOM, COMP_BLK), f32),
+            pltpu.HBM((COMP_BLOCKS, COMP_BLK), f32),
             jax.ShapeDtypeStruct((LISTED, BLK_DEV), jnp.int32),
             jax.ShapeDtypeStruct((REPLICAS * ROOM + 128,), jnp.int32),
-            jax.ShapeDtypeStruct((128,), jnp.int32),
+            jax.ShapeDtypeStruct((1,), jnp.int32),
             jax.ShapeDtypeStruct((BLK_DEV, LISTED, 8, COMP_BLK), f32),
             jax.ShapeDtypeStruct((BLK_DEV, FEATS + 8, ATOM_BLK), f32),
         ),
         in_specs=[hbm] * 9,
-        out_specs=(vmem, vmem, SMEM_SPEC, SMEM_SPEC, SMEM_SPEC, vmem, vmem),
+        out_specs=(hbm, hbm, SMEM_SPEC, SMEM_SPEC, SMEM_SPEC, vmem, vmem),
         scratch_shapes=[
+            pltpu.SMEM((REPLICAS + 1,), jnp.int32),
             pltpu.VMEM((REPLICAS * ROOM + COMP_BLOCKS, COMP_BLK), f32),
             pltpu.SMEM((BLK_DEV,), jnp.int32),
             pltpu.SMEM((LISTED, BLK_DEV), jnp.int32),
@@ -309,14 +321,10 @@
 
 def call_ratio(atoms, comps, part):
     f32 = jnp.float32
-    specs = [
-        pl.BlockSpec((PART,) + a.shape[1:], lambda i, n=a.ndim: (part,) + (0,) * (n - 1)) for a in (atoms, comps)
-    ]
     return pl.pallas_call(
-        ratio_kernel,
-        grid=(1,),
+        functools.partial(ratio_kernel, part * PART),
         out_shape=pltpu.HBM((PART, LISTED * COMP_BLK, 2 * ATOM_BLK), jnp.bfloat16),
-        in_specs=specs,
+        in_specs=[VMEM_SPEC] * 2,
         out_specs=HBM_SPEC,
         scratch_shapes=[
             pltpu.VMEM((2, LISTED * COMP_BLK, 2 * ATOM_BLK), jnp.bfloat16),
@@ -338,10 +346,10 @@
         in_specs=[smem] * 2 + [vmem] * 5 + [hbm] * len(ratios),
         out_specs=vmem,
         scratch_shapes=[
-            pltpu.VMEM((4, LISTED * COMP_BLK, 2 * ATOM_BLK), jnp.bfloat16),
-            pltpu.SemaphoreType.DMA((4,)),
+            pltpu.VMEM((DEPTH, LISTED * COMP_BLK, 2 * ATOM_BLK), jnp.bfloat16),
+            pltpu.SemaphoreType.DMA((DEPTH,)),
         ],
-        compiler_params=pltpu.CompilerParams(vmem_limit_bytes=16 << 20),
+        compiler_params=pltpu.CompilerParams(vmem_limit_bytes=24 << 20),
         name="force",
     )(*arrays, *(in_hbm(ratio) for ratio in ratios))
 
@@ -361,10 +369,10 @@
     weights = atom_weight.reshape(BLK_DEV, ATOM_BLK)
     cvar = comp_var.reshape(COMP_BLOCKS, COMP_BLK)
     cweight = comp_weight.reshape(COMP_BLOCKS, COMP_BLK)
-    model, over, rows, slots, counts, comps, atoms = call_overlap(
+    model, over, rows, slots, flag, comps, atoms = call_overlap(
         atoms_live, listed, owner_map, positions, variances, weights, comp_means, cvar, cweight
     )
-    crowded = counts[REPLICAS] > 0
+    crowded = flag[0] > 0
     tie = lax.optimization_barrier
     ratios = [call_ratio(atoms, comps, 0)]
     parts = lax.all_to_all(model.reshape(replicas, ROOM, COMP_BLK), "rep", 0, 0, tiled=True)
@@ -405,9 +413,9 @@
     ).reshape(-1, COMP_BLK)
     spread = pl.pallas_call(
         spread_kernel,
-        out_shape=jax.ShapeDtypeStruct((replicas, ROOM + share, COMP_BLK), f32),
-        in_specs=[SMEM_SPEC, vmem, vmem], out_specs=vmem,
-        scratch_shapes=[pltpu.VMEM((ROOM + share, COMP_BLK), f32)],
+        out_shape=pltpu.HBM((replicas, ROOM + share, COMP_BLK), f32),
+        in_specs=[SMEM_SPEC, vmem, vmem], out_specs=HBM_SPEC,
+        scratch_shapes=[pltpu.VMEM((ROOM + share, COMP_BLK), f32), pltpu.SemaphoreType.DMA((replicas,))],
         compiler_params=small, name="spread",
     )(slots, over_dom, mean)
     spread, atoms = tie((spread, atoms))

time: 113 us -> 110 us (0.973)
  local copies, waits for them, and re-layouts: 4.49 us -> 2.37 us
  Pallas kernels: 71.7 us -> 70.1 us
    pallas_call x1, Pallas kernels: 16.2 us -> 13 us  [call_force(): pl.pallas_call(force_kernel, out_shape=jax.ShapeDtypeStruct((3 * BLK_DEV,...]
    pallas_call x6, Pallas kernels: 52.8 us -> 54.5 us  [the longest x4 30.5 us: call_ratio(): pl.pallas_call(functools.partial(ratio_kernel, part * PART), out_shape=pl...]
    unnamed x16 -> x12, local copies, waits for them, and re-layouts: 2.23 us -> 0.68 us
  transfers between devices with their start and end apart: 4 -> 4, of which waited for: 4 -> 4; matrix products, arithmetic and copies ran while one was open for 0% -> 0% of each run, Pallas kernels for 27% -> 28%
where the time goes in v6:
time: 110 us; the launch traced here: 109 us
  Pallas kernels  70.1 us (64%)
  starting transfers between devices  31 us (28%)
  waiting for transfers between devices  4.33 us (4%)
  local copies, waits for them, and re-layouts  2.37 us (2%)
  between operations  1.42 us (1%)
    pallas_call x4, Pallas kernels, call_ratio(): pl.pallas_call(functools.partial(ratio_kernel, part * PART), out_shape=pl...  30.5 us
    pallas_call x1, Pallas kernels, call_overlap(): pl.pallas_call(overlap_kernel, out_shape=(pltpu.HBM((REPLICAS * ROOM, COM...  22.4 us
    pallas_call x1, Pallas kernels, call_force(): pl.pallas_call(force_kernel, out_shape=jax.ShapeDtypeStruct((3 * BLK_DEV,...  13 us
    all_to_all x1, starting transfers between devices, shards(): lax.all_to_all(over_rep.reshape(domains, share, COMP_BLK), 'dom', 0, 0, t...  10.4 us
    all_to_all x1, starting transfers between devices, shards(): lax.all_to_all(spread, 'dom', 0, 0, tiled=True)  7.76 us
    all_to_all x1, starting transfers between devices, shards(): lax.all_to_all(model.reshape(replicas, ROOM, COMP_BLK), 'rep', 0, 0, tile...  6.59 us
    all_to_all x1, starting transfers between devices, shards(): returned = lax.all_to_all(spread, 'rep', 0, 0, tiled=True)  6.3 us
  transfers between devices with their start and end apart: 4, of which 4 were waited for; matrix products, arithmetic and copies ran while one was open for 0% of the time, Pallas kernels for 28%

profile of v6, /device:TPU:1, one launch (start us, length us, event | category | flops | bytes accessed | tf_op | source)
XLA Modules:
  0.0 109.3 jit_solution(12502594385847500775)
XLA Ops:
  0.6 22.4 %overlap.1 = (f32[768,128]{1,0:T(8,128)}, f32[2048,128]{1,0:T(8,128)}, s32[16,32]{1,0:T(8,128)S(1)}, s32[896]{0:T(1024)S(1)}, s32[1]{0:T(128)}, /*index=5*/f32[3...) custom-call(s32[32]{0:T(128)} %live_ref.1, s32[16,32]{1,0:T(8,128)} %bitcast.34, s32[2048]{0:T(1024)} %owner_any.1, ...), custom_call_target="tpu_custom_call" | custom-call | tf_op jit(solution)/shard_map/overlap/pallas_call | solution.py:290
  23.7 0.0 copy-start.5
  23.7 0.6 copy-done.5
  24.4 6.6 %all-to-all-start.2 = ((f32[8,96,128]{2,1,0:T(8,128)}), f32[8,96,128]{2,1,0:T(8,128)S(1)}, u32[]{:S(2)}, u32[]{:S(2)}) async-start(f32[8,96,128]{2,1,0:T(8,128)} %bitcast.31), calls=%async_computation.2 | async-start | bytes 786432 | tf_op jit(solution)/shard_map/all_to_all | solution.py:378
  30.9 7.6 %ratio.4.refs_0_ = bf16[8,2048,256]{2,1,0:T(8,128)(2,1)} custom-call(f32[32,56,128]{2,1,0:T(8,128)S(1)} %get-tuple-element.52.atoms_ref, f32[32,16,8,128]{3,2,1,0:T(8,128)S(1)} %get-tuple-element.35.comps_ref), custom_call_target="tpu_custom_call" | custom-call | flops 134217728 | bytes 8388608 | tf_op jit(solution)/shard_map/ratio/pallas_call | solution.py:324
  38.5 0.0 copy-start.2
  38.6 0.0 copy-start.3
  38.6 0.5 all-to-all-done.2.parts_ref
  39.0 2.0 %rep_sum.1 = f32[256,128]{1,0:T(8,128)} custom-call(s32[896]{0:T(1024)S(1)} %get-tuple-element.32.slots_ref, f32[8,96,128]{2,1,0:T(8,128)S(1)} %all-to-all-done.2.parts_ref, f32[256,128]{1,0:T(8,128)} %copy-done.5), custom_call_target="tpu_custom_call" | custom-call | tf_op jit(solution)/shard_map/rep_sum/pallas_call | solution.py:386
  41.0 10.4 %all-to-all-start.3 = ((f32[32,8,128]{2,1,0:T(8,128)}), f32[32,8,128]{2,1,0:T(8,128)S(1)}, u32[]{:S(2)}, u32[]{:S(2)}) async-start(f32[32,8,128]{2,1,0:T(8,128)} %bitcast.10), calls=%async_computation.3 | async-start | bytes 262144 | tf_op jit(solution)/shard_map/all_to_all | solution.py:395
  51.4 7.6 %ratio.5.refs_1_ = bf16[8,2048,256]{2,1,0:T(8,128)(2,1)} custom-call(f32[32,56,128]{2,1,0:T(8,128)S(1)} %get-tuple-element.52.atoms_ref, f32[32,16,8,128]{3,2,1,0:T(8,128)S(1)} %get-tuple-element.35.comps_ref), custom_call_target="tpu_custom_call" | custom-call | flops 134217728 | bytes 8388608 | tf_op jit(solution)/shard_map/ratio/pallas_call | solution.py:324
  59.1 1.5 %all-to-all-done.3.parts_ref = f32[32,8,128]{2,1,0:T(8,128)S(1)} async-done(((f32[32,8,128]{2,1,0:T(8,128)}), f32[32,8,128]{2,1,0:T(8,128)S(1)}, u32[]{:S(2)}, u32[]{:S(2)}) %all-to-all-start.3) | async-done | bytes 131104 | tf_op jit(solution)/shard_map/all_to_all | solution.py:395
  60.6 0.0 copy-done.2
  60.6 0.0 copy-done.3
  60.6 0.7 adjoint.1
  61.3 7.8 %all-to-all-start.4 = ((f32[32,8,128]{2,1,0:T(8,128)}), f32[32,8,128]{2,1,0:T(8,128)S(1)}, u32[]{:S(2)}, u32[]{:S(2)}) async-start(f32[32,8,128]{2,1,0:T(8,128)} %get-tuple-element.43), calls=%async_computation.4 | async-start | bytes 262144 | tf_op jit(solution)/shard_map/all_to_all | solution.py:406
  69.1 7.6 %ratio.6.refs_2_ = bf16[8,2048,256]{2,1,0:T(8,128)(2,1)} custom-call(f32[32,56,128]{2,1,0:T(8,128)S(1)} %get-tuple-element.52.atoms_ref, f32[32,16,8,128]{3,2,1,0:T(8,128)S(1)} %get-tuple-element.35.comps_ref), custom_call_target="tpu_custom_call" | custom-call | flops 134217728 | bytes 8388608 | tf_op jit(solution)/shard_map/ratio/pallas_call | solution.py:324
  76.7 1.6 %all-to-all-done.4 = f32[32,8,128]{2,1,0:T(8,128)S(1)} async-done(((f32[32,8,128]{2,1,0:T(8,128)}), f32[32,8,128]{2,1,0:T(8,128)S(1)}, u32[]{:S(2)}, u32[]{:S(2)}) %all-to-all-start.4) | async-done | bytes 131104 | tf_op jit(solution)/shard_map/all_to_all | solution.py:406
  78.2 1.6 %spread.1 = f32[8,104,128]{2,1,0:T(8,128)} custom-call(s32[896]{0:T(1024)S(1)} %get-tuple-element.32.slots_ref, f32[256,128]{1,0:T(8,128)S(1)} %bitcast.26, f32[8,128]{1,0:T(8,128)S(1)} %get-tuple-element.46.mean_ref), custom_call_target="tpu_custom_call" | custom-call | tf_op jit(solution)/shard_map/spread/pallas_call | solution.py:414
  79.8 0.0 copy-start
  79.8 0.0 copy-start.1
  79.9 0.0 copy-start.4
  79.9 1.1 conditional.3
  79.9 1.1 reshape.41
  80.9 6.3 %all-to-all-start.5 = ((f32[8,104,128]{2,1,0:T(8,128)}), f32[8,104,128]{2,1,0:T(8,128)S(1)}, u32[]{:S(2)}, u32[]{:S(2)}) async-start(f32[8,104,128]{2,1,0:T(8,128)} %spread.1), calls=%async_computation.5 | async-start | bytes 851968 | tf_op jit(solution)/shard_map/all_to_all | solution.py:423
  87.3 7.6 %ratio.7.refs_3_ = bf16[8,2048,256]{2,1,0:T(8,128)(2,1)} custom-call(f32[32,56,128]{2,1,0:T(8,128)S(1)} %get-tuple-element.52.atoms_ref, f32[32,16,8,128]{3,2,1,0:T(8,128)S(1)} %get-tuple-element.35.comps_ref), custom_call_target="tpu_custom_call" | custom-call | flops 134217728 | bytes 8388608 | tf_op jit(solution)/shard_map/ratio/pallas_call | solution.py:324
  94.9 0.8 all-to-all-done.5
  95.7 0.0 copy-done
  95.7 0.0 copy-done.1
  95.7 0.0 copy-done.4
  95.7 13.0 %force.1 = f32[96,128]{1,0:T(8,128)} custom-call(s32[32]{0:T(128)S(1)} %copy-done.4, s32[16,32]{1,0:T(8,128)S(1)} %get-tuple-element.48.rows_ref, f32[96,128]{1,0:T(8,128)S(1)} %bitcast.20, f32[32,128]{1,0:T(8,128)S(1)} %bitcast.22, f32[32,16,8,128]{3,2,1,0:T(8,128)S(1)} %get-tuple-element.35.comps_ref, f32[832,128]{1,0:T(8,128)S(1)} %bitcast.18, ...), custom_call_target="tpu_custom_call" | custom-call | tf_op jit(solution)/shard_map/force/pallas_call | solution.py:343
  108.7 0.6 slice_bitcast_fusion
  (2 shorter events, 0.0 us)
Async XLA Ops:
  23.7 0.7 copy-start.5
  24.4 14.7 %all-to-all-start.2 = ((f32[8,96,128]{2,1,0:T(8,128)}), f32[8,96,128]{2,1,0:T(8,128)S(1)}, u32[]{:S(2)}, u32[]{:S(2)}) async-start(f32[8,96,128]{2,1,0:T(8,128)} %bitcast.31), calls=%async_computation.2 | async-start | bytes 786432 | tf_op jit(solution)/shard_map/all_to_all | solution.py:378
  38.5 22.1 %copy-start.2 = (f32[8192]{0:T(1024)S(1)}, f32[8192]{0:T(1024)}, u32[]{:S(2)}) copy-start(f32[8192]{0:T(1024)} %param.24) | copy-start | bytes 98308
  38.6 22.0 %copy-start.3 = (f32[8192]{0:T(1024)S(1)}, f32[8192]{0:T(1024)}, u32[]{:S(2)}) copy-start(f32[8192]{0:T(1024)} %param.25) | copy-start | bytes 98308
  41.0 19.6 %all-to-all-start.3 = ((f32[32,8,128]{2,1,0:T(8,128)}), f32[32,8,128]{2,1,0:T(8,128)S(1)}, u32[]{:S(2)}, u32[]{:S(2)}) async-start(f32[32,8,128]{2,1,0:T(8,128)} %bitcast.10), calls=%async_computation.3 | async-start | bytes 262144 | tf_op jit(solution)/shard_map/all_to_all | solution.py:395
  61.3 16.9 %all-to-all-start.4 = ((f32[32,8,128]{2,1,0:T(8,128)}), f32[32,8,128]{2,1,0:T(8,128)S(1)}, u32[]{:S(2)}, u32[]{:S(2)}) async-start(f32[32,8,128]{2,1,0:T(8,128)} %get-tuple-element.43), calls=%async_computation.4 | async-start | bytes 262144 | tf_op jit(solution)/shard_map/all_to_all | solution.py:406
  79.8 15.9 %copy-start = (f32[1,3,4096]{2,0,1:T(1,128)S(1)}, f32[1,3,4096]{2,0,1:T(1,128)}, u32[]{:S(2)}) copy-start(f32[1,3,4096]{2,0,1:T(1,128)} %param.15) | copy-start | bytes 147460
  79.8 15.9 %copy-start.1 = (f32[4096]{0:T(1024)S(1)}, f32[4096]{0:T(1024)}, u32[]{:S(2)}) copy-start(f32[4096]{0:T(1024)} %param.17) | copy-start | bytes 49156
  79.9 15.8 %copy-start.4 = (s32[32]{0:T(128)S(1)}, s32[32]{0:T(128)}, u32[]{:S(2)}) copy-start(s32[32]{0:T(128)} %live_ref.1) | copy-start | bytes 388
  80.9 14.8 %all-to-all-start.5 = ((f32[8,104,128]{2,1,0:T(8,128)}), f32[8,104,128]{2,1,0:T(8,128)S(1)}, u32[]{:S(2)}, u32[]{:S(2)}) async-start(f32[8,104,128]{2,1,0:T(8,128)} %spread.1), calls=%async_computation.5 | async-start | bytes 851968 | tf_op jit(solution)/shard_map/all_to_all | solution.py:423

commit v7 on v6

--- a/solution.py
+++ b/solution.py
@@ -20,6 +20,7 @@
 OWNED = 256
 PART = 8
 DEPTH = 8
+ROW_STEPS = (64, 80, 96, 112, 128)
 
 ENERGY_UNIT = 2.494
 EXP_SCALE = -0.5 / math.log(2.0)
@@ -46,14 +47,15 @@
 
 
 def spread_lanes(atoms, column):
-    return jnp.broadcast_to(atoms[:, column : column + 1], (128, 128)).reshape(16, 8, 128)
+    rows = atoms.shape[0]
+    return jnp.broadcast_to(atoms[:, column : column + 1], (rows, 128)).reshape(rows // 8, 8, 128)
 
 
 def pair_terms(left, spread_var, comp_of):
     for k in range(0, LISTED, 2):
         comps = [comp_of(k), comp_of(k + 1)]
         right = jnp.concatenate([right_side(comp) for comp in comps], axis=1)
-        scaled = jnp.dot(left, right, preferred_element_type=jnp.float32).reshape(16, 8, 256)
+        scaled = jnp.dot(left, right, preferred_element_type=jnp.float32).reshape(-1, 8, 256)
         for n in range(2):
             r = lax.rsqrt(spread_var + comps[n][5:6].reshape(1, 1, 128))
             q = r * r
@@ -77,8 +79,8 @@
     row = lax.broadcasted_iota(jnp.int32, shape, 0)
     lane = lax.broadcasted_iota(jnp.int32, (1, 128), 1)
     sums_ref[...] = jnp.zeros_like(sums_ref)
-    for r in range(REPLICAS + 1):
-        counts_ref[r] = 0
+    for r in range(REPLICAS):
+        counts_ref[r] = r * ROOM
 
     def unused(n, _):
         slots_ref[n] = OWNED
@@ -88,7 +90,7 @@
     for copy in copies:
         copy.wait()
 
-    def block(a, _):
+    def rows_of_block(a, rows):
         x, y, z = (coords_ref[pl.ds(d * BLK_DEV + a, 1), :] for d in range(3))
         norm2 = EXP_SCALE * (x * x + y * y + z * z)
         t = -2.0 * EXP_SCALE
@@ -97,7 +99,7 @@
         extra = choose(row, (var_ref[pl.ds(a, 1), :], weight), shape)
         feats = jnp.concatenate([hi, mid, low, hi, mid, hi, extra], axis=0)
         atoms_ref[a] = feats
-        atoms = feats.T
+        atoms = feats.T[:rows]
         left = atoms[:, :FEATS].astype(jnp.bfloat16)
         spread_var = spread_lanes(atoms, FEATS)
         spread_weight = spread_lanes(atoms, FEATS + 1)
@@ -116,19 +118,24 @@
             place = owner_ref[list_ref[k, a]]
             rank = (place >> 3) & 7
             owned = ((place >> 6) << 3) + (place & 7)
-            count = counts_ref[rank]
-            counts_ref[rank] = count + 1
-            fits = count < ROOM
-            counts_ref[REPLICAS] = jnp.where(fits, counts_ref[REPLICAS], 1)
-            slots_ref[jnp.where(fits, rank * ROOM + count, REPLICAS * ROOM)] = owned
-            dense = rank * OWNED + owned
-            rows_ref[k, a] = jnp.where(fits, rank * (ROOM + SHARE) + count, REPLICAS * (ROOM + SHARE) + dense)
-            target = jnp.where(fits, rank * ROOM + count, REPLICAS * ROOM + dense)
+            place = counts_ref[rank]
+            counts_ref[rank] = place + 1
+            fits = place < rank * ROOM + ROOM
+            target = jnp.where(fits, place, rank * OWNED + owned + REPLICAS * ROOM)
+            slots_ref[target] = owned
+            rows_ref[k, a] = target + jnp.where(fits, rank * SHARE, REPLICAS * SHARE)
             sums_ref[pl.ds(target, 1), :] += NORM * total * comps_ref[a, k, 6:7, :]
+
+    def block(a, _):
+        step = jnp.clip((live_ref[a] - ROW_STEPS[0] + 15) // 16, 0, len(ROW_STEPS) - 1)
+        lax.switch(step, [functools.partial(rows_of_block, a, rows) for rows in ROW_STEPS])
         return 0
 
     lax.fori_loop(0, BLK_DEV, block, 0)
-    flag_ref[0] = counts_ref[REPLICAS]
+    crowded = jnp.int32(0)
+    for r in range(REPLICAS):
+        crowded = jnp.where(counts_ref[r] > (r + 1) * ROOM, 1, crowded)
+    flag_ref[0] = crowded
     copies = [
         pltpu.make_async_copy(sums_ref.at[pl.ds(0, REPLICAS * ROOM)], model_ref, sems.at[0]),
         pltpu.make_async_copy(sums_ref.at[pl.ds(REPLICAS * ROOM, COMP_BLOCKS)], over_ref, sems.at[1]),
@@ -293,7 +300,7 @@
             pltpu.HBM((REPLICAS * ROOM, COMP_BLK), f32),
             pltpu.HBM((COMP_BLOCKS, COMP_BLK), f32),
             jax.ShapeDtypeStruct((LISTED, BLK_DEV), jnp.int32),
-            jax.ShapeDtypeStruct((REPLICAS * ROOM + 128,), jnp.int32),
+            jax.ShapeDtypeStruct((REPLICAS * ROOM + COMP_BLOCKS,), jnp.int32),
             jax.ShapeDtypeStruct((1,), jnp.int32),
             jax.ShapeDtypeStruct((BLK_DEV, LISTED, 8, COMP_BLK), f32),
             jax.ShapeDtypeStruct((BLK_DEV, FEATS + 8, ATOM_BLK), f32),
@@ -301,7 +308,7 @@
         in_specs=[hbm] * 9,
         out_specs=(hbm, hbm, SMEM_SPEC, SMEM_SPEC, SMEM_SPEC, vmem, vmem),
         scratch_shapes=[
-            pltpu.SMEM((REPLICAS + 1,), jnp.int32),
+            pltpu.SMEM((REPLICAS,), jnp.int32),
             pltpu.VMEM((REPLICAS * ROOM + COMP_BLOCKS, COMP_BLK), f32),
             pltpu.SMEM((BLK_DEV,), jnp.int32),
             pltpu.SMEM((LISTED, BLK_DEV), jnp.int32),

time: 110 us -> 109 us (level)
  no operation moved by 1% of the time
where the time goes in v7:
time: 109 us; the launch traced here: 108 us
  Pallas kernels  69.4 us (64%)
  starting transfers between devices  30.7 us (28%)
  waiting for transfers between devices  4.4 us (4%)
  local copies, waits for them, and re-layouts  2.37 us (2%)
  between operations  1.42 us (1%)
    pallas_call x4, Pallas kernels, call_ratio(): pl.pallas_call(functools.partial(ratio_kernel, part * PART), out_shape=pl...  30.5 us
    pallas_call x1, Pallas kernels, call_overlap(): pl.pallas_call(overlap_kernel, out_shape=(pltpu.HBM((REPLICAS * ROOM, COM...  21.5 us
    pallas_call x1, Pallas kernels, call_force(): pl.pallas_call(force_kernel, out_shape=jax.ShapeDtypeStruct((3 * BLK_DEV,...  13 us
    all_to_all x1, starting transfers between devices, shards(): lax.all_to_all(over_rep.reshape(domains, share, COMP_BLK), 'dom', 0, 0, t...  10.1 us
    all_to_all x1, starting transfers between devices, shards(): lax.all_to_all(spread, 'dom', 0, 0, tiled=True)  7.75 us
    all_to_all x1, starting transfers between devices, shards(): lax.all_to_all(model.reshape(replicas, ROOM, COMP_BLK), 'rep', 0, 0, tile...  6.59 us
    all_to_all x1, starting transfers between devices, shards(): returned = lax.all_to_all(spread, 'rep', 0, 0, tiled=True)  6.27 us
  transfers between devices with their start and end apart: 4, of which 4 were waited for; matrix products, arithmetic and copies ran while one was open for 0% of the time, Pallas kernels for 28%

profile of v7, /device:TPU:1, one launch (start us, length us, event | category | flops | bytes accessed | tf_op | source)
XLA Modules:
  0.0 108.4 jit_solution(4913308246589161906)
XLA Ops:
  0.6 21.5 %overlap.1 = (f32[768,128]{1,0:T(8,128)}, f32[2048,128]{1,0:T(8,128)}, s32[16,32]{1,0:T(8,128)S(1)}, s32[2816]{0:T(1024)S(1)}, s32[1]{0:T(128)}, /*index=5*/f32[...) custom-call(s32[32]{0:T(128)} %live_ref.1, s32[16,32]{1,0:T(8,128)} %bitcast.34, s32[2048]{0:T(1024)} %owner_any.1, ...), custom_call_target="tpu_custom_call" | custom-call | tf_op jit(solution)/shard_map/overlap/pallas_call | solution.py:297
  22.8 0.0 copy-start.5
  22.9 0.6 copy-done.5
  23.5 6.6 %all-to-all-start.2 = ((f32[8,96,128]{2,1,0:T(8,128)}), f32[8,96,128]{2,1,0:T(8,128)S(1)}, u32[]{:S(2)}, u32[]{:S(2)}) async-start(f32[8,96,128]{2,1,0:T(8,128)} %bitcast.31), calls=%async_computation.2 | async-start | bytes 786432 | tf_op jit(solution)/shard_map/all_to_all | solution.py:385
  30.1 7.6 %ratio.4.refs_0_ = bf16[8,2048,256]{2,1,0:T(8,128)(2,1)} custom-call(f32[32,56,128]{2,1,0:T(8,128)S(1)} %get-tuple-element.52.atoms_ref, f32[32,16,8,128]{3,2,1,0:T(8,128)S(1)} %get-tuple-element.35.comps_ref), custom_call_target="tpu_custom_call" | custom-call | flops 134217728 | bytes 8388608 | tf_op jit(solution)/shard_map/ratio/pallas_call | solution.py:331
  37.7 0.0 copy-start.2
  37.7 0.0 copy-start.3
  37.7 0.5 all-to-all-done.2.parts_ref
  38.2 2.0 %rep_sum.1 = f32[256,128]{1,0:T(8,128)} custom-call(s32[2816]{0:T(1024)S(1)} %get-tuple-element.32.slots_ref, f32[8,96,128]{2,1,0:T(8,128)S(1)} %all-to-all-done.2.parts_ref, f32[256,128]{1,0:T(8,128)} %copy-done.5), custom_call_target="tpu_custom_call" | custom-call | tf_op jit(solution)/shard_map/rep_sum/pallas_call | solution.py:393
  40.2 10.1 %all-to-all-start.3 = ((f32[32,8,128]{2,1,0:T(8,128)}), f32[32,8,128]{2,1,0:T(8,128)S(1)}, u32[]{:S(2)}, u32[]{:S(2)}) async-start(f32[32,8,128]{2,1,0:T(8,128)} %bitcast.10), calls=%async_computation.3 | async-start | bytes 262144 | tf_op jit(solution)/shard_map/all_to_all | solution.py:402
  50.3 7.7 %ratio.5.refs_1_ = bf16[8,2048,256]{2,1,0:T(8,128)(2,1)} custom-call(f32[32,56,128]{2,1,0:T(8,128)S(1)} %get-tuple-element.52.atoms_ref, f32[32,16,8,128]{3,2,1,0:T(8,128)S(1)} %get-tuple-element.35.comps_ref), custom_call_target="tpu_custom_call" | custom-call | flops 134217728 | bytes 8388608 | tf_op jit(solution)/shard_map/ratio/pallas_call | solution.py:331
  58.0 1.5 %all-to-all-done.3.parts_ref = f32[32,8,128]{2,1,0:T(8,128)S(1)} async-done(((f32[32,8,128]{2,1,0:T(8,128)}), f32[32,8,128]{2,1,0:T(8,128)S(1)}, u32[]{:S(2)}, u32[]{:S(2)}) %all-to-all-start.3) | async-done | bytes 131104 | tf_op jit(solution)/shard_map/all_to_all | solution.py:402
  59.5 0.0 copy-done.2
  59.5 0.0 copy-done.3
  59.5 0.7 adjoint.1
  60.2 7.7 %all-to-all-start.4 = ((f32[32,8,128]{2,1,0:T(8,128)}), f32[32,8,128]{2,1,0:T(8,128)S(1)}, u32[]{:S(2)}, u32[]{:S(2)}) async-start(f32[32,8,128]{2,1,0:T(8,128)} %get-tuple-element.43), calls=%async_computation.4 | async-start | bytes 262144 | tf_op jit(solution)/shard_map/all_to_all | solution.py:413
  67.9 7.6 %ratio.6.refs_2_ = bf16[8,2048,256]{2,1,0:T(8,128)(2,1)} custom-call(f32[32,56,128]{2,1,0:T(8,128)S(1)} %get-tuple-element.52.atoms_ref, f32[32,16,8,128]{3,2,1,0:T(8,128)S(1)} %get-tuple-element.35.comps_ref), custom_call_target="tpu_custom_call" | custom-call | flops 134217728 | bytes 8388608 | tf_op jit(solution)/shard_map/ratio/pallas_call | solution.py:331
  75.6 1.6 %all-to-all-done.4 = f32[32,8,128]{2,1,0:T(8,128)S(1)} async-done(((f32[32,8,128]{2,1,0:T(8,128)}), f32[32,8,128]{2,1,0:T(8,128)S(1)}, u32[]{:S(2)}, u32[]{:S(2)}) %all-to-all-start.4) | async-done | bytes 131104 | tf_op jit(solution)/shard_map/all_to_all | solution.py:413
  77.2 1.7 %spread.1 = f32[8,104,128]{2,1,0:T(8,128)} custom-call(s32[2816]{0:T(1024)S(1)} %get-tuple-element.32.slots_ref, f32[256,128]{1,0:T(8,128)S(1)} %bitcast.26, f32[8,128]{1,0:T(8,128)S(1)} %get-tuple-element.46.mean_ref), custom_call_target="tpu_custom_call" | custom-call | tf_op jit(solution)/shard_map/spread/pallas_call | solution.py:421
  78.9 0.0 copy-start
  78.9 0.0 copy-start.1
  79.0 0.0 copy-start.4
  79.0 1.1 conditional.3
  79.0 1.1 reshape.41
  80.0 6.3 %all-to-all-start.5 = ((f32[8,104,128]{2,1,0:T(8,128)}), f32[8,104,128]{2,1,0:T(8,128)S(1)}, u32[]{:S(2)}, u32[]{:S(2)}) async-start(f32[8,104,128]{2,1,0:T(8,128)} %spread.1), calls=%async_computation.5 | async-start | bytes 851968 | tf_op jit(solution)/shard_map/all_to_all | solution.py:430
  86.3 7.6 %ratio.7.refs_3_ = bf16[8,2048,256]{2,1,0:T(8,128)(2,1)} custom-call(f32[32,56,128]{2,1,0:T(8,128)S(1)} %get-tuple-element.52.atoms_ref, f32[32,16,8,128]{3,2,1,0:T(8,128)S(1)} %get-tuple-element.35.comps_ref), custom_call_target="tpu_custom_call" | custom-call | flops 134217728 | bytes 8388608 | tf_op jit(solution)/shard_map/ratio/pallas_call | solution.py:331
  94.0 0.8 all-to-all-done.5
  94.8 0.0 copy-done
  94.8 0.0 copy-done.1
  94.8 0.0 copy-done.4
  94.8 13.0 %force.1 = f32[96,128]{1,0:T(8,128)} custom-call(s32[32]{0:T(128)S(1)} %copy-done.4, s32[16,32]{1,0:T(8,128)S(1)} %get-tuple-element.48.rows_ref, f32[96,128]{1,0:T(8,128)S(1)} %bitcast.20, f32[32,128]{1,0:T(8,128)S(1)} %bitcast.22, f32[32,16,8,128]{3,2,1,0:T(8,128)S(1)} %get-tuple-element.35.comps_ref, f32[832,128]{1,0:T(8,128)S(1)} %bitcast.18, ...), custom_call_target="tpu_custom_call" | custom-call | tf_op jit(solution)/shard_map/force/pallas_call | solution.py:350
  107.8 0.6 slice_bitcast_fusion
  (2 shorter events, 0.0 us)
Async XLA Ops:
  22.8 0.7 copy-start.5
  23.5 14.7 %all-to-all-start.2 = ((f32[8,96,128]{2,1,0:T(8,128)}), f32[8,96,128]{2,1,0:T(8,128)S(1)}, u32[]{:S(2)}, u32[]{:S(2)}) async-start(f32[8,96,128]{2,1,0:T(8,128)} %bitcast.31), calls=%async_computation.2 | async-start | bytes 786432 | tf_op jit(solution)/shard_map/all_to_all | solution.py:385
  37.7 21.8 %copy-start.2 = (f32[8192]{0:T(1024)S(1)}, f32[8192]{0:T(1024)}, u32[]{:S(2)}) copy-start(f32[8192]{0:T(1024)} %param.24) | copy-start | bytes 98308
  37.7 21.8 %copy-start.3 = (f32[8192]{0:T(1024)S(1)}, f32[8192]{0:T(1024)}, u32[]{:S(2)}) copy-start(f32[8192]{0:T(1024)} %param.25) | copy-start | bytes 98308
  40.2 19.3 %all-to-all-start.3 = ((f32[32,8,128]{2,1,0:T(8,128)}), f32[32,8,128]{2,1,0:T(8,128)S(1)}, u32[]{:S(2)}, u32[]{:S(2)}) async-start(f32[32,8,128]{2,1,0:T(8,128)} %bitcast.10), calls=%async_computation.3 | async-start | bytes 262144 | tf_op jit(solution)/shard_map/all_to_all | solution.py:402
  60.2 17.0 %all-to-all-start.4 = ((f32[32,8,128]{2,1,0:T(8,128)}), f32[32,8,128]{2,1,0:T(8,128)S(1)}, u32[]{:S(2)}, u32[]{:S(2)}) async-start(f32[32,8,128]{2,1,0:T(8,128)} %get-tuple-element.43), calls=%async_computation.4 | async-start | bytes 262144 | tf_op jit(solution)/shard_map/all_to_all | solution.py:413
  78.9 15.8 %copy-start = (f32[1,3,4096]{2,0,1:T(1,128)S(1)}, f32[1,3,4096]{2,0,1:T(1,128)}, u32[]{:S(2)}) copy-start(f32[1,3,4096]{2,0,1:T(1,128)} %param.15) | copy-start | bytes 147460
  78.9 15.8 %copy-start.1 = (f32[4096]{0:T(1024)S(1)}, f32[4096]{0:T(1024)}, u32[]{:S(2)}) copy-start(f32[4096]{0:T(1024)} %param.17) | copy-start | bytes 49156
  79.0 15.8 %copy-start.4 = (s32[32]{0:T(128)S(1)}, s32[32]{0:T(128)}, u32[]{:S(2)}) copy-start(s32[32]{0:T(128)} %live_ref.1) | copy-start | bytes 388
  80.0 14.7 %all-to-all-start.5 = ((f32[8,104,128]{2,1,0:T(8,128)}), f32[8,104,128]{2,1,0:T(8,128)S(1)}, u32[]{:S(2)}, u32[]{:S(2)}) async-start(f32[8,104,128]{2,1,0:T(8,128)} %spread.1), calls=%async_computation.5 | async-start | bytes 851968 | tf_op jit(solution)/shard_map/all_to_all | solution.py:430

commit v8 on v7

--- a/solution.py
+++ b/solution.py
@@ -414,10 +414,13 @@
     over_dom, ratios[2] = tie((over_dom, ratios[2]))
     over_back = lax.cond(
         crowded,
-        lambda v: lax.all_to_all(jnp.broadcast_to(v[None], (replicas, OWNED, COMP_BLK)), "rep", 0, 0, tiled=True),
-        lambda v: jnp.zeros((replicas, OWNED, COMP_BLK), f32),
+        lambda v, unread: lax.all_to_all(
+            jnp.broadcast_to(v[None], (replicas, OWNED, COMP_BLK)), "rep", 0, 0, tiled=True
+        ).reshape(unread.shape),
+        lambda v, unread: unread,
         over_dom,
-    ).reshape(-1, COMP_BLK)
+        over,
+    )
     spread = pl.pallas_call(
         spread_kernel,
         out_shape=pltpu.HBM((replicas, ROOM + share, COMP_BLK), f32),

time: 109 us -> 108 us (level)
  no operation moved by 1% of the time
where the time goes in v8:
time: 108 us; the launch traced here: 107 us
  Pallas kernels  69.2 us (64%)
  starting transfers between devices  30.8 us (29%)
  waiting for transfers between devices  4.27 us (4%)
  between operations  1.42 us (1%)
  local copies, waits for them, and re-layouts  1.31 us (1%)
    pallas_call x4, Pallas kernels, call_ratio(): pl.pallas_call(functools.partial(ratio_kernel, part * PART), out_shape=pl...  30.5 us
    pallas_call x1, Pallas kernels, call_overlap(): pl.pallas_call(overlap_kernel, out_shape=(pltpu.HBM((REPLICAS * ROOM, COM...  21.3 us
    pallas_call x1, Pallas kernels, call_force(): pl.pallas_call(force_kernel, out_shape=jax.ShapeDtypeStruct((3 * BLK_DEV,...  13 us
    all_to_all x1, starting transfers between devices, shards(): lax.all_to_all(over_rep.reshape(domains, share, COMP_BLK), 'dom', 0, 0, t...  10.1 us
    all_to_all x1, starting transfers between devices, shards(): lax.all_to_all(spread, 'dom', 0, 0, tiled=True)  7.75 us
    all_to_all x1, starting transfers between devices, shards(): lax.all_to_all(model.reshape(replicas, ROOM, COMP_BLK), 'rep', 0, 0, tile...  6.58 us
    all_to_all x1, starting transfers between devices, shards(): returned = lax.all_to_all(spread, 'rep', 0, 0, tiled=True)  6.36 us
  transfers between devices with their start and end apart: 4, of which 4 were waited for; matrix products, arithmetic and copies ran while one was open for 0% of the time, Pallas kernels for 28%

profile of v8, /device:TPU:1, one launch (start us, length us, event | category | flops | bytes accessed | tf_op | source)
XLA Modules:
  0.0 107.0 jit_solution(11371013408162679807)
XLA Ops:
  0.6 21.3 %overlap.1 = (f32[768,128]{1,0:T(8,128)}, f32[2048,128]{1,0:T(8,128)}, s32[16,32]{1,0:T(8,128)S(1)}, s32[2816]{0:T(1024)S(1)}, s32[1]{0:T(128)}, /*index=5*/f32[...) custom-call(s32[32]{0:T(128)} %live_ref.1, s32[16,32]{1,0:T(8,128)} %bitcast.34, s32[2048]{0:T(1024)} %owner_any.1, ...), custom_call_target="tpu_custom_call" | custom-call | tf_op jit(solution)/shard_map/overlap/pallas_call | solution.py:297
  22.6 0.0 copy-start.5
  22.6 0.6 copy-done.5
  23.3 6.6 %all-to-all-start.2 = ((f32[8,96,128]{2,1,0:T(8,128)}), f32[8,96,128]{2,1,0:T(8,128)S(1)}, u32[]{:S(2)}, u32[]{:S(2)}) async-start(f32[8,96,128]{2,1,0:T(8,128)} %bitcast.31), calls=%async_computation.2 | async-start | bytes 786432 | tf_op jit(solution)/shard_map/all_to_all | solution.py:385
  29.8 7.6 %ratio.4.refs_0_ = bf16[8,2048,256]{2,1,0:T(8,128)(2,1)} custom-call(f32[32,56,128]{2,1,0:T(8,128)S(1)} %get-tuple-element.52.atoms_ref, f32[32,16,8,128]{3,2,1,0:T(8,128)S(1)} %get-tuple-element.35.comps_ref), custom_call_target="tpu_custom_call" | custom-call | flops 134217728 | bytes 8388608 | tf_op jit(solution)/shard_map/ratio/pallas_call | solution.py:331
  37.4 0.0 copy-start.2
  37.5 0.0 copy-start.3
  37.5 0.5 all-to-all-done.2.parts_ref
  37.9 2.0 %rep_sum.1 = f32[256,128]{1,0:T(8,128)} custom-call(s32[2816]{0:T(1024)S(1)} %get-tuple-element.32.slots_ref, f32[8,96,128]{2,1,0:T(8,128)S(1)} %all-to-all-done.2.parts_ref, f32[256,128]{1,0:T(8,128)} %copy-done.5), custom_call_target="tpu_custom_call" | custom-call | tf_op jit(solution)/shard_map/rep_sum/pallas_call | solution.py:393
  39.9 10.1 %all-to-all-start.3 = ((f32[32,8,128]{2,1,0:T(8,128)}), f32[32,8,128]{2,1,0:T(8,128)S(1)}, u32[]{:S(2)}, u32[]{:S(2)}) async-start(f32[32,8,128]{2,1,0:T(8,128)} %bitcast.10), calls=%async_computation.3 | async-start | bytes 262144 | tf_op jit(solution)/shard_map/all_to_all | solution.py:402
  50.1 7.7 %ratio.5.refs_1_ = bf16[8,2048,256]{2,1,0:T(8,128)(2,1)} custom-call(f32[32,56,128]{2,1,0:T(8,128)S(1)} %get-tuple-element.52.atoms_ref, f32[32,16,8,128]{3,2,1,0:T(8,128)S(1)} %get-tuple-element.35.comps_ref), custom_call_target="tpu_custom_call" | custom-call | flops 134217728 | bytes 8388608 | tf_op jit(solution)/shard_map/ratio/pallas_call | solution.py:331
  57.7 1.5 %all-to-all-done.3.parts_ref = f32[32,8,128]{2,1,0:T(8,128)S(1)} async-done(((f32[32,8,128]{2,1,0:T(8,128)}), f32[32,8,128]{2,1,0:T(8,128)S(1)}, u32[]{:S(2)}, u32[]{:S(2)}) %all-to-all-start.3) | async-done | bytes 131104 | tf_op jit(solution)/shard_map/all_to_all | solution.py:402
  59.2 0.0 copy-done.2
  59.2 0.0 copy-done.3
  59.2 0.7 adjoint.1
  60.0 7.8 %all-to-all-start.4 = ((f32[32,8,128]{2,1,0:T(8,128)}), f32[32,8,128]{2,1,0:T(8,128)S(1)}, u32[]{:S(2)}, u32[]{:S(2)}) async-start(f32[32,8,128]{2,1,0:T(8,128)} %get-tuple-element.43), calls=%async_computation.4 | async-start | bytes 262144 | tf_op jit(solution)/shard_map/all_to_all | solution.py:413
  67.7 7.6 %ratio.6.refs_2_ = bf16[8,2048,256]{2,1,0:T(8,128)(2,1)} custom-call(f32[32,56,128]{2,1,0:T(8,128)S(1)} %get-tuple-element.52.atoms_ref, f32[32,16,8,128]{3,2,1,0:T(8,128)S(1)} %get-tuple-element.35.comps_ref), custom_call_target="tpu_custom_call" | custom-call | flops 134217728 | bytes 8388608 | tf_op jit(solution)/shard_map/ratio/pallas_call | solution.py:331
  75.3 0.0 copy-start
  75.3 0.0 copy-start.1
  75.3 0.0 copy-start.4
  75.4 1.5 %all-to-all-done.4 = f32[32,8,128]{2,1,0:T(8,128)S(1)} async-done(((f32[32,8,128]{2,1,0:T(8,128)}), f32[32,8,128]{2,1,0:T(8,128)S(1)}, u32[]{:S(2)}, u32[]{:S(2)}) %all-to-all-start.4) | async-done | bytes 131104 | tf_op jit(solution)/shard_map/all_to_all | solution.py:413
  76.9 1.7 %spread.1 = f32[8,104,128]{2,1,0:T(8,128)} custom-call(s32[2816]{0:T(1024)S(1)} %get-tuple-element.32.slots_ref, f32[256,128]{1,0:T(8,128)S(1)} %bitcast.28, f32[8,128]{1,0:T(8,128)S(1)} %get-tuple-element.46.mean_ref), custom_call_target="tpu_custom_call" | custom-call | tf_op jit(solution)/shard_map/spread/pallas_call | solution.py:424
  78.6 6.4 %all-to-all-start.5 = ((f32[8,104,128]{2,1,0:T(8,128)}), f32[8,104,128]{2,1,0:T(8,128)S(1)}, u32[]{:S(2)}, u32[]{:S(2)}) async-start(f32[8,104,128]{2,1,0:T(8,128)} %spread.1), calls=%async_computation.5 | async-start | bytes 851968 | tf_op jit(solution)/shard_map/all_to_all | solution.py:433
  85.0 7.6 %ratio.7.refs_3_ = bf16[8,2048,256]{2,1,0:T(8,128)(2,1)} custom-call(f32[32,56,128]{2,1,0:T(8,128)S(1)} %get-tuple-element.52.atoms_ref, f32[32,16,8,128]{3,2,1,0:T(8,128)S(1)} %get-tuple-element.35.comps_ref), custom_call_target="tpu_custom_call" | custom-call | flops 134217728 | bytes 8388608 | tf_op jit(solution)/shard_map/ratio/pallas_call | solution.py:331
  92.6 0.8 all-to-all-done.5
  93.4 0.0 copy-done
  93.4 0.0 copy-done.1
  93.4 0.0 copy-done.4
  93.4 13.0 %force.1 = f32[96,128]{1,0:T(8,128)} custom-call(s32[32]{0:T(128)S(1)} %copy-done.4, s32[16,32]{1,0:T(8,128)S(1)} %get-tuple-element.48.rows_ref, f32[96,128]{1,0:T(8,128)S(1)} %bitcast.20, f32[32,128]{1,0:T(8,128)S(1)} %bitcast.22, f32[32,16,8,128]{3,2,1,0:T(8,128)S(1)} %get-tuple-element.35.comps_ref, f32[832,128]{1,0:T(8,128)S(1)} %bitcast.18, ...), custom_call_target="tpu_custom_call" | custom-call | tf_op jit(solution)/shard_map/force/pallas_call | solution.py:350
  106.4 0.6 slice_bitcast_fusion
  (3 shorter events, 0.0 us)
Async XLA Ops:
  22.6 0.7 copy-start.5
  23.3 14.7 %all-to-all-start.2 = ((f32[8,96,128]{2,1,0:T(8,128)}), f32[8,96,128]{2,1,0:T(8,128)S(1)}, u32[]{:S(2)}, u32[]{:S(2)}) async-start(f32[8,96,128]{2,1,0:T(8,128)} %bitcast.31), calls=%async_computation.2 | async-start | bytes 786432 | tf_op jit(solution)/shard_map/all_to_all | solution.py:385
  37.4 21.8 %copy-start.2 = (f32[8192]{0:T(1024)S(1)}, f32[8192]{0:T(1024)}, u32[]{:S(2)}) copy-start(f32[8192]{0:T(1024)} %param.24) | copy-start | bytes 98308
  37.5 21.8 %copy-start.3 = (f32[8192]{0:T(1024)S(1)}, f32[8192]{0:T(1024)}, u32[]{:S(2)}) copy-start(f32[8192]{0:T(1024)} %param.25) | copy-start | bytes 98308
  39.9 19.3 %all-to-all-start.3 = ((f32[32,8,128]{2,1,0:T(8,128)}), f32[32,8,128]{2,1,0:T(8,128)S(1)}, u32[]{:S(2)}, u32[]{:S(2)}) async-start(f32[32,8,128]{2,1,0:T(8,128)} %bitcast.10), calls=%async_computation.3 | async-start | bytes 262144 | tf_op jit(solution)/shard_map/all_to_all | solution.py:402
  60.0 16.9 %all-to-all-start.4 = ((f32[32,8,128]{2,1,0:T(8,128)}), f32[32,8,128]{2,1,0:T(8,128)S(1)}, u32[]{:S(2)}, u32[]{:S(2)}) async-start(f32[32,8,128]{2,1,0:T(8,128)} %get-tuple-element.43), calls=%async_computation.4 | async-start | bytes 262144 | tf_op jit(solution)/shard_map/all_to_all | solution.py:413
  75.3 18.1 %copy-start = (f32[1,3,4096]{2,0,1:T(1,128)S(1)}, f32[1,3,4096]{2,0,1:T(1,128)}, u32[]{:S(2)}) copy-start(f32[1,3,4096]{2,0,1:T(1,128)} %param.15) | copy-start | bytes 147460
  75.3 18.1 %copy-start.1 = (f32[4096]{0:T(1024)S(1)}, f32[4096]{0:T(1024)}, u32[]{:S(2)}) copy-start(f32[4096]{0:T(1024)} %param.17) | copy-start | bytes 49156
  75.3 18.1 %copy-start.4 = (s32[32]{0:T(128)S(1)}, s32[32]{0:T(128)}, u32[]{:S(2)}) copy-start(s32[32]{0:T(128)} %live_ref.1) | copy-start | bytes 388
  78.6 14.8 %all-to-all-start.5 = ((f32[8,104,128]{2,1,0:T(8,128)}), f32[8,104,128]{2,1,0:T(8,128)S(1)}, u32[]{:S(2)}, u32[]{:S(2)}) async-start(f32[8,104,128]{2,1,0:T(8,128)} %spread.1), calls=%async_computation.5 | async-start | bytes 851968 | tf_op jit(solution)/shard_map/all_to_all | solution.py:433

commit v9 on v8

--- a/solution.py
+++ b/solution.py
@@ -186,9 +186,17 @@
     return pltpu.with_memory_space_constraint(array, pltpu.HBM)
 
 
-def rep_sum_kernel(slots_ref, parts_ref, over_ref, out_ref, sum_ref, dense_ref):
+def rep_sum_kernel(flag_ref, slots_ref, parts_ref, over_any, out_ref, sum_ref, dense_ref, over_ref, sem):
     sum_ref[...] = jnp.sum(parts_ref[...], axis=0)
-    dense_ref[:OWNED] = over_ref[...]
+    dense_ref[...] = jnp.zeros_like(dense_ref)
+
+    @pl.when(flag_ref[0] > 0)
+    def _():
+        copy = pltpu.make_async_copy(over_any, over_ref, sem)
+        copy.start()
+        copy.wait()
+        dense_ref[:OWNED] = jnp.sum(over_ref[...].reshape(REPLICAS, OWNED, COMP_BLK), axis=0)
+
     first = lax.axis_index("rep") * ROOM
     for n in range(ROOM):
         dense_ref[pl.ds(slots_ref[first + n], 1), :] += sum_ref[n : n + 1, :]
@@ -222,8 +230,11 @@
     live_ref, rows_ref, coords_ref, weight_ref, comps_ref, adjoint_ref, over_ref, *refs,
 ):
     parts = BLK_DEV // PART
-    ratio_any, (force_ref, ratio_ref, ratio_sems) = refs[:parts], refs[parts:]
+    ratio_any, (force_ref, average_ref, ratio_ref, ratio_sems) = refs[:parts], refs[parts:]
     depth = ratio_ref.shape[0]
+    for r in range(REPLICAS):
+        first = r * (ROOM + SHARE) + ROOM
+        average_ref[r * SHARE : (r + 1) * SHARE] = adjoint_ref[first : first + SHARE]
     shape = (8, 128)
     row = lax.broadcasted_iota(jnp.int32, shape, 0)
     upper = row < 4
@@ -349,9 +360,12 @@
     *arrays, ratios = arrays
     return pl.pallas_call(
         force_kernel,
-        out_shape=jax.ShapeDtypeStruct((3 * BLK_DEV, ATOM_BLK), f32),
+        out_shape=(
+            jax.ShapeDtypeStruct((3 * BLK_DEV, ATOM_BLK), f32),
+            jax.ShapeDtypeStruct((REPLICAS * SHARE, COMP_BLK), f32),
+        ),
         in_specs=[smem] * 2 + [vmem] * 5 + [hbm] * len(ratios),
-        out_specs=vmem,
+        out_specs=(vmem, vmem),
         scratch_shapes=[
             pltpu.VMEM((DEPTH, LISTED * COMP_BLK, 2 * ATOM_BLK), jnp.bfloat16),
             pltpu.SemaphoreType.DMA((DEPTH,)),
@@ -386,17 +400,22 @@
     parts, ratios[0] = tie((parts, ratios[0]))
     over_sum = lax.cond(
         crowded,
-        lambda v: jnp.sum(lax.all_to_all(v.reshape(replicas, OWNED, COMP_BLK), "rep", 0, 0, tiled=True), axis=0),
-        lambda v: jnp.zeros((OWNED, COMP_BLK), f32),
+        lambda v: lax.all_to_all(v.reshape(replicas, OWNED, COMP_BLK), "rep", 0, 0, tiled=True).reshape(v.shape),
+        lambda v: v,
         over,
     )
     over_rep = pl.pallas_call(
         rep_sum_kernel,
         out_shape=jax.ShapeDtypeStruct((OWNED, COMP_BLK), f32),
-        in_specs=[SMEM_SPEC, vmem, vmem], out_specs=vmem,
-        scratch_shapes=[pltpu.VMEM((ROOM, COMP_BLK), f32), pltpu.VMEM((OWNED + 8, COMP_BLK), f32)],
+        in_specs=[SMEM_SPEC, SMEM_SPEC, vmem, HBM_SPEC], out_specs=vmem,
+        scratch_shapes=[
+            pltpu.VMEM((ROOM, COMP_BLK), f32),
+            pltpu.VMEM((OWNED + 8, COMP_BLK), f32),
+            pltpu.VMEM((COMP_BLOCKS, COMP_BLK), f32),
+            pltpu.SemaphoreType.DMA,
+        ],
         compiler_params=small, name="rep_sum",
-    )(slots, parts, over_sum)
+    )(flag, slots, parts, in_hbm(over_sum))
     over_rep, atoms = tie((over_rep, atoms))
     ratios.append(call_ratio(atoms, comps, 1))
     parts = lax.all_to_all(over_rep.reshape(domains, share, COMP_BLK), "dom", 0, 0, tiled=True)
@@ -431,11 +450,10 @@
     spread, atoms = tie((spread, atoms))
     ratios.append(call_ratio(atoms, comps, 3))
     returned = lax.all_to_all(spread, "rep", 0, 0, tiled=True)
-    average = returned[:, ROOM:].reshape(-1)
     returned = returned.reshape(-1, COMP_BLK)
 
-    forces = call_force(atoms_live, rows, positions, weights, comps, returned, over_back, ratios)
-    return average, forces.reshape(coords.shape)
+    forces, average = call_force(atoms_live, rows, positions, weights, comps, returned, over_back, ratios)
+    return average.reshape(-1), forces.reshape(coords.shape)
 
 
 def solution(mesh):

time: 108 us -> 110 us (1.019)
    cond x0 -> x1, local copies, waits for them, and re-layouts: none -> 2.34 us
where the time goes in v9:
time: 110 us; the launch traced here: 109 us
  Pallas kernels  70.3 us (64%)
  starting transfers between devices  30.5 us (28%)
  waiting for transfers between devices  4.19 us (4%)
  local copies, waits for them, and re-layouts  2.38 us (2%)
  between operations  1.4 us (1%)
    pallas_call x4, Pallas kernels, call_ratio(): pl.pallas_call(functools.partial(ratio_kernel, part * PART), out_shape=pl...  30.5 us
    pallas_call x1, Pallas kernels, call_overlap(): pl.pallas_call(overlap_kernel, out_shape=(pltpu.HBM((REPLICAS * ROOM, COM...  21.7 us
    pallas_call x1, Pallas kernels, call_force(): pl.pallas_call(force_kernel, out_shape=(jax.ShapeDtypeStruct((3 * BLK_DEV...  13 us
    all_to_all x1, starting transfers between devices, shards(): lax.all_to_all(over_rep.reshape(domains, share, COMP_BLK), 'dom', 0, 0, t...  9.75 us
    all_to_all x1, starting transfers between devices, shards(): lax.all_to_all(spread, 'dom', 0, 0, tiled=True)  7.74 us
    all_to_all x1, starting transfers between devices, shards(): lax.all_to_all(model.reshape(replicas, ROOM, COMP_BLK), 'rep', 0, 0, tile...  6.59 us
    all_to_all x1, starting transfers between devices, shards(): returned = lax.all_to_all(spread, 'rep', 0, 0, tiled=True)  6.41 us
    pallas_call x1, Pallas kernels, shards(): pl.pallas_call(rep_sum_kernel, out_shape=jax.ShapeDtypeStruct((OWNED, COM...  2.58 us
  transfers between devices with their start and end apart: 4, of which 4 were waited for; matrix products, arithmetic and copies ran while one was open for 0% of the time, Pallas kernels for 28%

profile of v9, /device:TPU:1, one launch (start us, length us, event | category | flops | bytes accessed | tf_op | source)
XLA Modules:
  0.0 108.7 jit_solution(7501043462056862581)
XLA Ops:
  0.6 21.7 %overlap.1 = (f32[768,128]{1,0:T(8,128)}, f32[2048,128]{1,0:T(8,128)}, s32[16,32]{1,0:T(8,128)S(1)}, s32[2816]{0:T(1024)S(1)}, s32[1]{0:T(128)}, /*index=5*/f32[...) custom-call(s32[32]{0:T(128)} %live_ref.1, s32[16,32]{1,0:T(8,128)} %bitcast.34, s32[2048]{0:T(1024)} %owner_any.1, ...), custom_call_target="tpu_custom_call" | custom-call | tf_op jit(solution)/shard_map/overlap/pallas_call | solution.py:308
  23.0 2.4 %conditional.2 = (f32[2048,128]{1,0:T(8,128)}) conditional(s32[]{:T(128)} %bitcast.10, f32[2048,128]{1,0:T(8,128)} %get-tuple-element.42, f32[2048,128]{1,0:T(8,128)} %get-tuple-element.42), branch_computations={%region_0.0_spmd, %region_1.0_spmd} | conditional | bytes 2097160 | solution.py:401
  23.0 2.3 %copy.15 = f32[2048,128]{1,0:T(8,128)} copy(f32[2048,128]{1,0:T(8,128)} %param) | data formatting | bytes 2097152 | tf_op jit(solution)/shard_map/cond
  25.4 6.6 %all-to-all-start.2 = ((f32[8,96,128]{2,1,0:T(8,128)}), f32[8,96,128]{2,1,0:T(8,128)S(1)}, u32[]{:S(2)}, u32[]{:S(2)}) async-start(f32[8,96,128]{2,1,0:T(8,128)} %bitcast.32), calls=%async_computation.2 | async-start | bytes 786432 | tf_op jit(solution)/shard_map/all_to_all | solution.py:399
  31.9 7.6 %ratio.4.refs_0_ = bf16[8,2048,256]{2,1,0:T(8,128)(2,1)} custom-call(f32[32,56,128]{2,1,0:T(8,128)S(1)} %get-tuple-element.55.atoms_ref, f32[32,16,8,128]{3,2,1,0:T(8,128)S(1)} %get-tuple-element.36.comps_ref), custom_call_target="tpu_custom_call" | custom-call | flops 134217728 | bytes 8388608 | tf_op jit(solution)/shard_map/ratio/pallas_call | solution.py:342
  39.6 0.0 copy-start.2
  39.6 0.0 copy-start.3
  39.6 0.4 all-to-all-done.2.parts_ref
  40.0 2.6 %rep_sum.1 = f32[256,128]{1,0:T(8,128)} custom-call(s32[1]{0:T(128)} %get-tuple-element.38.flag_ref, s32[2816]{0:T(1024)S(1)} %get-tuple-element.37.slots_ref, f32[8,96,128]{2,1,0:T(8,128)S(1)} %all-to-all-done.2.parts_ref, f32[2048,128]{1,0:T(8,128)} %get-tuple-element.62.over_any), custom_call_target="tpu_custom_call" | custom-call | tf_op jit(solution)/shard_map/rep_sum/pallas_call | solution.py:407
  42.6 9.8 %all-to-all-start.3 = ((f32[32,8,128]{2,1,0:T(8,128)}), f32[32,8,128]{2,1,0:T(8,128)S(1)}, u32[]{:S(2)}, u32[]{:S(2)}) async-start(f32[32,8,128]{2,1,0:T(8,128)} %bitcast.11), calls=%async_computation.3 | async-start | bytes 262144 | tf_op jit(solution)/shard_map/all_to_all | solution.py:421
  52.4 7.6 %ratio.5.refs_1_ = bf16[8,2048,256]{2,1,0:T(8,128)(2,1)} custom-call(f32[32,56,128]{2,1,0:T(8,128)S(1)} %get-tuple-element.55.atoms_ref, f32[32,16,8,128]{3,2,1,0:T(8,128)S(1)} %get-tuple-element.36.comps_ref), custom_call_target="tpu_custom_call" | custom-call | flops 134217728 | bytes 8388608 | tf_op jit(solution)/shard_map/ratio/pallas_call | solution.py:342
  60.0 1.5 %all-to-all-done.3.parts_ref = f32[32,8,128]{2,1,0:T(8,128)S(1)} async-done(((f32[32,8,128]{2,1,0:T(8,128)}), f32[32,8,128]{2,1,0:T(8,128)S(1)}, u32[]{:S(2)}, u32[]{:S(2)}) %all-to-all-start.3) | async-done | bytes 131104 | tf_op jit(solution)/shard_map/all_to_all | solution.py:421
  61.5 0.0 copy-done.2
  61.5 0.0 copy-done.3
  61.5 0.7 adjoint.1
  62.3 7.7 %all-to-all-start.4 = ((f32[32,8,128]{2,1,0:T(8,128)}), f32[32,8,128]{2,1,0:T(8,128)S(1)}, u32[]{:S(2)}, u32[]{:S(2)}) async-start(f32[32,8,128]{2,1,0:T(8,128)} %get-tuple-element.47), calls=%async_computation.4 | async-start | bytes 262144 | tf_op jit(solution)/shard_map/all_to_all | solution.py:432
  70.0 7.6 %ratio.6.refs_2_ = bf16[8,2048,256]{2,1,0:T(8,128)(2,1)} custom-call(f32[32,56,128]{2,1,0:T(8,128)S(1)} %get-tuple-element.55.atoms_ref, f32[32,16,8,128]{3,2,1,0:T(8,128)S(1)} %get-tuple-element.36.comps_ref), custom_call_target="tpu_custom_call" | custom-call | flops 134217728 | bytes 8388608 | tf_op jit(solution)/shard_map/ratio/pallas_call | solution.py:342
  77.7 0.0 copy-start
  77.7 0.0 copy-start.1
  77.7 0.0 copy-start.4
  77.7 1.5 %all-to-all-done.4 = f32[32,8,128]{2,1,0:T(8,128)S(1)} async-done(((f32[32,8,128]{2,1,0:T(8,128)}), f32[32,8,128]{2,1,0:T(8,128)S(1)}, u32[]{:S(2)}, u32[]{:S(2)}) %all-to-all-start.4) | async-done | bytes 131104 | tf_op jit(solution)/shard_map/all_to_all | solution.py:432
  79.2 1.7 %spread.1 = f32[8,104,128]{2,1,0:T(8,128)} custom-call(s32[2816]{0:T(1024)S(1)} %get-tuple-element.37.slots_ref, f32[256,128]{1,0:T(8,128)S(1)} %bitcast.29, f32[8,128]{1,0:T(8,128)S(1)} %get-tuple-element.50.mean_ref), custom_call_target="tpu_custom_call" | custom-call | tf_op jit(solution)/shard_map/spread/pallas_call | solution.py:443
  80.9 6.4 %all-to-all-start.5 = ((f32[8,104,128]{2,1,0:T(8,128)}), f32[8,104,128]{2,1,0:T(8,128)S(1)}, u32[]{:S(2)}, u32[]{:S(2)}) async-start(f32[8,104,128]{2,1,0:T(8,128)} %spread.1), calls=%async_computation.5 | async-start | bytes 851968 | tf_op jit(solution)/shard_map/all_to_all | solution.py:452
  87.3 7.6 %ratio.7.refs_3_ = bf16[8,2048,256]{2,1,0:T(8,128)(2,1)} custom-call(f32[32,56,128]{2,1,0:T(8,128)S(1)} %get-tuple-element.55.atoms_ref, f32[32,16,8,128]{3,2,1,0:T(8,128)S(1)} %get-tuple-element.36.comps_ref), custom_call_target="tpu_custom_call" | custom-call | flops 134217728 | bytes 8388608 | tf_op jit(solution)/shard_map/ratio/pallas_call | solution.py:342
  95.0 0.8 all-to-all-done.5
  95.7 0.0 copy-done
  95.7 0.0 copy-done.1
  95.7 0.0 copy-done.4
  95.7 13.0 %force.1 = (f32[96,128]{1,0:T(8,128)}, f32[64,128]{1,0:T(8,128)}) custom-call(s32[32]{0:T(128)S(1)} %copy-done.4, s32[16,32]{1,0:T(8,128)S(1)} %get-tuple-element.35.rows_ref, f32[96,128]{1,0:T(8,128)S(1)} %bitcast.20, f32[32,128]{1,0:T(8,128)S(1)} %bitcast.22, f32[32,16,8,128]{3,2,1,0:T(8,128)S(1)} %get-tuple-element.36.comps_ref, f32[832,128]{1,0:T(8,128)S(1)} %bitcast.18, ...), custom_call_target="tpu_custom_call" | custom-call | tf_op jit(solution)/shard_map/force/pallas_call | solution.py:361
  (1 shorter events, 0.0 us)
Async XLA Ops:
  25.4 14.7 %all-to-all-start.2 = ((f32[8,96,128]{2,1,0:T(8,128)}), f32[8,96,128]{2,1,0:T(8,128)S(1)}, u32[]{:S(2)}, u32[]{:S(2)}) async-start(f32[8,96,128]{2,1,0:T(8,128)} %bitcast.32), calls=%async_computation.2 | async-start | bytes 786432 | tf_op jit(solution)/shard_map/all_to_all | solution.py:399
  39.6 22.0 %copy-start.2 = (f32[8192]{0:T(1024)S(1)}, f32[8192]{0:T(1024)}, u32[]{:S(2)}) copy-start(f32[8192]{0:T(1024)} %param.24) | copy-start | bytes 98308
  39.6 22.0 %copy-start.3 = (f32[8192]{0:T(1024)S(1)}, f32[8192]{0:T(1024)}, u32[]{:S(2)}) copy-start(f32[8192]{0:T(1024)} %param.25) | copy-start | bytes 98308
  42.6 18.9 %all-to-all-start.3 = ((f32[32,8,128]{2,1,0:T(8,128)}), f32[32,8,128]{2,1,0:T(8,128)S(1)}, u32[]{:S(2)}, u32[]{:S(2)}) async-start(f32[32,8,128]{2,1,0:T(8,128)} %bitcast.11), calls=%async_computation.3 | async-start | bytes 262144 | tf_op jit(solution)/shard_map/all_to_all | solution.py:421
  62.3 16.9 %all-to-all-start.4 = ((f32[32,8,128]{2,1,0:T(8,128)}), f32[32,8,128]{2,1,0:T(8,128)S(1)}, u32[]{:S(2)}, u32[]{:S(2)}) async-start(f32[32,8,128]{2,1,0:T(8,128)} %get-tuple-element.47), calls=%async_computation.4 | async-start | bytes 262144 | tf_op jit(solution)/shard_map/all_to_all | solution.py:432
  77.7 18.1 %copy-start = (f32[1,3,4096]{2,0,1:T(1,128)S(1)}, f32[1,3,4096]{2,0,1:T(1,128)}, u32[]{:S(2)}) copy-start(f32[1,3,4096]{2,0,1:T(1,128)} %param.15) | copy-start | bytes 147460
  77.7 18.1 %copy-start.1 = (f32[4096]{0:T(1024)S(1)}, f32[4096]{0:T(1024)}, u32[]{:S(2)}) copy-start(f32[4096]{0:T(1024)} %param.17) | copy-start | bytes 49156
  77.7 18.1 %copy-start.4 = (s32[32]{0:T(128)S(1)}, s32[32]{0:T(128)}, u32[]{:S(2)}) copy-start(s32[32]{0:T(128)} %live_ref.1) | copy-start | bytes 388
  80.9 14.8 %all-to-all-start.5 = ((f32[8,104,128]{2,1,0:T(8,128)}), f32[8,104,128]{2,1,0:T(8,128)S(1)}, u32[]{:S(2)}, u32[]{:S(2)}) async-start(f32[8,104,128]{2,1,0:T(8,128)} %spread.1), calls=%async_computation.5 | async-start | bytes 851968 | tf_op jit(solution)/shard_map/all_to_all | solution.py:452

commit v10 on v8

--- a/solution.py
+++ b/solution.py
@@ -222,8 +222,11 @@
     live_ref, rows_ref, coords_ref, weight_ref, comps_ref, adjoint_ref, over_ref, *refs,
 ):
     parts = BLK_DEV // PART
-    ratio_any, (force_ref, ratio_ref, ratio_sems) = refs[:parts], refs[parts:]
+    ratio_any, (force_ref, average_ref, ratio_ref, ratio_sems) = refs[:parts], refs[parts:]
     depth = ratio_ref.shape[0]
+    for r in range(REPLICAS):
+        first = r * (ROOM + SHARE) + ROOM
+        average_ref[r * SHARE : (r + 1) * SHARE] = adjoint_ref[first : first + SHARE]
     shape = (8, 128)
     row = lax.broadcasted_iota(jnp.int32, shape, 0)
     upper = row < 4
@@ -349,9 +352,12 @@
     *arrays, ratios = arrays
     return pl.pallas_call(
         force_kernel,
-        out_shape=jax.ShapeDtypeStruct((3 * BLK_DEV, ATOM_BLK), f32),
+        out_shape=(
+            jax.ShapeDtypeStruct((3 * BLK_DEV, ATOM_BLK), f32),
+            jax.ShapeDtypeStruct((REPLICAS * SHARE, COMP_BLK), f32),
+        ),
         in_specs=[smem] * 2 + [vmem] * 5 + [hbm] * len(ratios),
-        out_specs=vmem,
+        out_specs=(vmem, vmem),
         scratch_shapes=[
             pltpu.VMEM((DEPTH, LISTED * COMP_BLK, 2 * ATOM_BLK), jnp.bfloat16),
             pltpu.SemaphoreType.DMA((DEPTH,)),
@@ -431,11 +437,10 @@
     spread, atoms = tie((spread, atoms))
     ratios.append(call_ratio(atoms, comps, 3))
     returned = lax.all_to_all(spread, "rep", 0, 0, tiled=True)
-    average = returned[:, ROOM:].reshape(-1)
     returned = returned.reshape(-1, COMP_BLK)
 
-    forces = call_force(atoms_live, rows, positions, weights, comps, returned, over_back, ratios)
-    return average, forces.reshape(coords.shape)
+    forces, average = call_force(atoms_live, rows, positions, weights, comps, returned, over_back, ratios)
+    return average.reshape(-1), forces.reshape(coords.shape)
 
 
 def solution(mesh):

time: 108 us -> 107 us (level)
  transfers between devices with their start and end apart: 4 -> 4, of which waited for: 4 -> 4; matrix products, arithmetic and copies ran while one was open for 0% -> 0% of each run, Pallas kernels for 28% -> 29%
where the time goes in v10:
time: 107 us
  Pallas kernels  69.8 us (65%)
  starting transfers between devices  30.9 us (29%)
  waiting for transfers between devices  4.25 us (4%)
  between operations  1.41 us (1%)
    pallas_call x4, Pallas kernels, call_ratio(): pl.pallas_call(functools.partial(ratio_kernel, part * PART), out_shape=pl...  30.5 us
    pallas_call x1, Pallas kernels, call_overlap(): pl.pallas_call(overlap_kernel, out_shape=(pltpu.HBM((REPLICAS * ROOM, COM...  21.8 us
    pallas_call x1, Pallas kernels, call_force(): pl.pallas_call(force_kernel, out_shape=(jax.ShapeDtypeStruct((3 * BLK_DEV...  13 us
    all_to_all x1, starting transfers between devices, shards(): lax.all_to_all(over_rep.reshape(domains, share, COMP_BLK), 'dom', 0, 0, t...  10.2 us
    all_to_all x1, starting transfers between devices, shards(): lax.all_to_all(spread, 'dom', 0, 0, tiled=True)  7.75 us
    all_to_all x1, starting transfers between devices, shards(): lax.all_to_all(model.reshape(replicas, ROOM, COMP_BLK), 'rep', 0, 0, tile...  6.59 us
    all_to_all x1, starting transfers between devices, shards(): returned = lax.all_to_all(spread, 'rep', 0, 0, tiled=True)  6.28 us
  transfers between devices with their start and end apart: 4, of which 4 were waited for; matrix products, arithmetic and copies ran while one was open for 0% of the time, Pallas kernels for 29%

profile of v10, /device:TPU:1, one launch (start us, length us, event | category | flops | bytes accessed | tf_op | source)
XLA Modules:
  0.0 107.0 jit_solution(7262327877076778732)
XLA Ops:
  0.6 21.8 %overlap.1 = (f32[768,128]{1,0:T(8,128)}, f32[2048,128]{1,0:T(8,128)}, s32[16,32]{1,0:T(8,128)S(1)}, s32[2816]{0:T(1024)S(1)}, s32[1]{0:T(128)}, /*index=5*/f32[...) custom-call(s32[32]{0:T(128)} %live_ref.1, s32[16,32]{1,0:T(8,128)} %bitcast.32, s32[2048]{0:T(1024)} %owner_any.1, ...), custom_call_target="tpu_custom_call" | custom-call | tf_op jit(solution)/shard_map/overlap/pallas_call | solution.py:300
  23.1 0.0 copy-start.5
  23.2 0.6 copy-done.5
  23.8 6.6 %all-to-all-start.2 = ((f32[8,96,128]{2,1,0:T(8,128)}), f32[8,96,128]{2,1,0:T(8,128)S(1)}, u32[]{:S(2)}, u32[]{:S(2)}) async-start(f32[8,96,128]{2,1,0:T(8,128)} %bitcast.30), calls=%async_computation.2 | async-start | bytes 786432 | tf_op jit(solution)/shard_map/all_to_all | solution.py:391
  30.4 7.6 %ratio.4.refs_0_ = bf16[8,2048,256]{2,1,0:T(8,128)(2,1)} custom-call(f32[32,56,128]{2,1,0:T(8,128)S(1)} %get-tuple-element.54.atoms_ref, f32[32,16,8,128]{3,2,1,0:T(8,128)S(1)} %get-tuple-element.35.comps_ref), custom_call_target="tpu_custom_call" | custom-call | flops 134217728 | bytes 8388608 | tf_op jit(solution)/shard_map/ratio/pallas_call | solution.py:334
  38.0 0.0 copy-start.2
  38.0 0.0 copy-start.3
  38.0 0.4 all-to-all-done.2.parts_ref
  38.5 2.0 %rep_sum.1 = f32[256,128]{1,0:T(8,128)} custom-call(s32[2816]{0:T(1024)S(1)} %get-tuple-element.36.slots_ref, f32[8,96,128]{2,1,0:T(8,128)S(1)} %all-to-all-done.2.parts_ref, f32[256,128]{1,0:T(8,128)} %copy-done.5), custom_call_target="tpu_custom_call" | custom-call | tf_op jit(solution)/shard_map/rep_sum/pallas_call | solution.py:399
  40.5 10.2 %all-to-all-start.3 = ((f32[32,8,128]{2,1,0:T(8,128)}), f32[32,8,128]{2,1,0:T(8,128)S(1)}, u32[]{:S(2)}, u32[]{:S(2)}) async-start(f32[32,8,128]{2,1,0:T(8,128)} %bitcast.10), calls=%async_computation.3 | async-start | bytes 262144 | tf_op jit(solution)/shard_map/all_to_all | solution.py:408
  50.7 7.6 %ratio.5.refs_1_ = bf16[8,2048,256]{2,1,0:T(8,128)(2,1)} custom-call(f32[32,56,128]{2,1,0:T(8,128)S(1)} %get-tuple-element.54.atoms_ref, f32[32,16,8,128]{3,2,1,0:T(8,128)S(1)} %get-tuple-element.35.comps_ref), custom_call_target="tpu_custom_call" | custom-call | flops 134217728 | bytes 8388608 | tf_op jit(solution)/shard_map/ratio/pallas_call | solution.py:334
  58.4 1.5 %all-to-all-done.3.parts_ref = f32[32,8,128]{2,1,0:T(8,128)S(1)} async-done(((f32[32,8,128]{2,1,0:T(8,128)}), f32[32,8,128]{2,1,0:T(8,128)S(1)}, u32[]{:S(2)}, u32[]{:S(2)}) %all-to-all-start.3) | async-done | bytes 131104 | tf_op jit(solution)/shard_map/all_to_all | solution.py:408
  59.9 0.0 copy-done.2
  59.9 0.0 copy-done.3
  59.9 0.7 adjoint.1
  60.6 7.7 %all-to-all-start.4 = ((f32[32,8,128]{2,1,0:T(8,128)}), f32[32,8,128]{2,1,0:T(8,128)S(1)}, u32[]{:S(2)}, u32[]{:S(2)}) async-start(f32[32,8,128]{2,1,0:T(8,128)} %get-tuple-element.46), calls=%async_computation.4 | async-start | bytes 262144 | tf_op jit(solution)/shard_map/all_to_all | solution.py:419
  68.3 7.6 %ratio.6.refs_2_ = bf16[8,2048,256]{2,1,0:T(8,128)(2,1)} custom-call(f32[32,56,128]{2,1,0:T(8,128)S(1)} %get-tuple-element.54.atoms_ref, f32[32,16,8,128]{3,2,1,0:T(8,128)S(1)} %get-tuple-element.35.comps_ref), custom_call_target="tpu_custom_call" | custom-call | flops 134217728 | bytes 8388608 | tf_op jit(solution)/shard_map/ratio/pallas_call | solution.py:334
  76.0 0.0 copy-start
  76.0 0.0 copy-start.1
  76.0 0.0 copy-start.4
  76.0 1.5 %all-to-all-done.4 = f32[32,8,128]{2,1,0:T(8,128)S(1)} async-done(((f32[32,8,128]{2,1,0:T(8,128)}), f32[32,8,128]{2,1,0:T(8,128)S(1)}, u32[]{:S(2)}, u32[]{:S(2)}) %all-to-all-start.4) | async-done | bytes 131104 | tf_op jit(solution)/shard_map/all_to_all | solution.py:419
  77.5 1.7 %spread.1 = f32[8,104,128]{2,1,0:T(8,128)} custom-call(s32[2816]{0:T(1024)S(1)} %get-tuple-element.36.slots_ref, f32[256,128]{1,0:T(8,128)S(1)} %bitcast.27, f32[8,128]{1,0:T(8,128)S(1)} %get-tuple-element.49.mean_ref), custom_call_target="tpu_custom_call" | custom-call | tf_op jit(solution)/shard_map/spread/pallas_call | solution.py:430
  79.3 6.3 %all-to-all-start.5 = ((f32[8,104,128]{2,1,0:T(8,128)}), f32[8,104,128]{2,1,0:T(8,128)S(1)}, u32[]{:S(2)}, u32[]{:S(2)}) async-start(f32[8,104,128]{2,1,0:T(8,128)} %spread.1), calls=%async_computation.5 | async-start | bytes 851968 | tf_op jit(solution)/shard_map/all_to_all | solution.py:439
  85.5 7.6 %ratio.7.refs_3_ = bf16[8,2048,256]{2,1,0:T(8,128)(2,1)} custom-call(f32[32,56,128]{2,1,0:T(8,128)S(1)} %get-tuple-element.54.atoms_ref, f32[32,16,8,128]{3,2,1,0:T(8,128)S(1)} %get-tuple-element.35.comps_ref), custom_call_target="tpu_custom_call" | custom-call | flops 134217728 | bytes 8388608 | tf_op jit(solution)/shard_map/ratio/pallas_call | solution.py:334
  93.2 0.8 all-to-all-done.5
  94.0 0.0 copy-done
  94.0 0.0 copy-done.1
  94.0 0.0 copy-done.4
  94.0 13.0 %force.1 = (f32[96,128]{1,0:T(8,128)}, f32[64,128]{1,0:T(8,128)}) custom-call(s32[32]{0:T(128)S(1)} %copy-done.4, s32[16,32]{1,0:T(8,128)S(1)} %get-tuple-element.34.rows_ref, f32[96,128]{1,0:T(8,128)S(1)} %bitcast.19, f32[32,128]{1,0:T(8,128)S(1)} %bitcast.21, f32[32,16,8,128]{3,2,1,0:T(8,128)S(1)} %get-tuple-element.35.comps_ref, f32[832,128]{1,0:T(8,128)S(1)} %bitcast.17, ...), custom_call_target="tpu_custom_call" | custom-call | tf_op jit(solution)/shard_map/force/pallas_call | solution.py:353
  (3 shorter events, 0.0 us)
Async XLA Ops:
  23.1 0.6 copy-start.5
  23.8 14.7 %all-to-all-start.2 = ((f32[8,96,128]{2,1,0:T(8,128)}), f32[8,96,128]{2,1,0:T(8,128)S(1)}, u32[]{:S(2)}, u32[]{:S(2)}) async-start(f32[8,96,128]{2,1,0:T(8,128)} %bitcast.30), calls=%async_computation.2 | async-start | bytes 786432 | tf_op jit(solution)/shard_map/all_to_all | solution.py:391
  38.0 21.9 %copy-start.2 = (f32[8192]{0:T(1024)S(1)}, f32[8192]{0:T(1024)}, u32[]{:S(2)}) copy-start(f32[8192]{0:T(1024)} %param.24) | copy-start | bytes 98308
  38.0 21.9 %copy-start.3 = (f32[8192]{0:T(1024)S(1)}, f32[8192]{0:T(1024)}, u32[]{:S(2)}) copy-start(f32[8192]{0:T(1024)} %param.25) | copy-start | bytes 98308
  40.5 19.4 %all-to-all-start.3 = ((f32[32,8,128]{2,1,0:T(8,128)}), f32[32,8,128]{2,1,0:T(8,128)S(1)}, u32[]{:S(2)}, u32[]{:S(2)}) async-start(f32[32,8,128]{2,1,0:T(8,128)} %bitcast.10), calls=%async_computation.3 | async-start | bytes 262144 | tf_op jit(solution)/shard_map/all_to_all | solution.py:408
  60.6 16.9 %all-to-all-start.4 = ((f32[32,8,128]{2,1,0:T(8,128)}), f32[32,8,128]{2,1,0:T(8,128)S(1)}, u32[]{:S(2)}, u32[]{:S(2)}) async-start(f32[32,8,128]{2,1,0:T(8,128)} %get-tuple-element.46), calls=%async_computation.4 | async-start | bytes 262144 | tf_op jit(solution)/shard_map/all_to_all | solution.py:419
  76.0 18.0 %copy-start = (f32[1,3,4096]{2,0,1:T(1,128)S(1)}, f32[1,3,4096]{2,0,1:T(1,128)}, u32[]{:S(2)}) copy-start(f32[1,3,4096]{2,0,1:T(1,128)} %param.15) | copy-start | bytes 147460
  76.0 18.0 %copy-start.1 = (f32[4096]{0:T(1024)S(1)}, f32[4096]{0:T(1024)}, u32[]{:S(2)}) copy-start(f32[4096]{0:T(1024)} %param.17) | copy-start | bytes 49156
  76.0 18.0 %copy-start.4 = (s32[32]{0:T(128)S(1)}, s32[32]{0:T(128)}, u32[]{:S(2)}) copy-start(s32[32]{0:T(128)} %live_ref.1) | copy-start | bytes 388
  79.3 14.7 %all-to-all-start.5 = ((f32[8,104,128]{2,1,0:T(8,128)}), f32[8,104,128]{2,1,0:T(8,128)S(1)}, u32[]{:S(2)}, u32[]{:S(2)}) async-start(f32[8,104,128]{2,1,0:T(8,128)} %spread.1), calls=%async_computation.5 | async-start | bytes 851968 | tf_op jit(solution)/shard_map/all_to_all | solution.py:439
